TPU v7x, 32 devices: a whole 2x2x4 slice. The times are simulated.
32 devices in a mesh: ctx: 16 (over z, y, x), fsdp: 2 (over core).
Axes of the slice: x: 2, y: 2, z: 4, core: 2. Of those that a mesh axis runs over, the one named last changes fastest.
Arguments:
- tokens_in: bfloat16 [6, 1024, 896], P('fsdp', 'ctx'), may hold values from -6 to 6
- cotangent: bfloat16 [6, 1024, 896], P('fsdp', 'ctx'), may hold values from -6 to 6
- block_order: int32 [32], replicated, may hold values from 0 to 31, as said below
- weight_query: float32 [896, 896], P(('ctx', 'fsdp')), may hold values from -0.25 to 0.25
- weight_key: float32 [896, 128], P(('ctx', 'fsdp')), may hold values from -0.25 to 0.25
- weight_value: float32 [896, 128], P(('ctx', 'fsdp')), may hold values from -0.1875 to 0.1875
- weight_out: float32 [896, 896], P(('ctx', 'fsdp')), may hold values from -1 to 1
- weight_gate: float32 [896, 4864], P(('ctx', 'fsdp')), may hold values from -0.1875 to 0.1875
- weight_up: float32 [896, 4864], P(('ctx', 'fsdp')), may hold values from -0.1875 to 0.1875
- weight_down: float32 [4864, 896], P(('ctx', 'fsdp')), may hold values from -0.078125 to 0.078125
- moment_query: float32 [896, 896], P(('ctx', 'fsdp')), may hold values from -24 to 24
- moment_key: float32 [896, 128], P(('ctx', 'fsdp')), may hold values from -1280 to 1280
- moment_value: float32 [896, 128], P(('ctx', 'fsdp')), may hold values from -1280 to 1280
- moment_out: float32 [896, 896], P(('ctx', 'fsdp')), may hold values from -112 to 112
- moment_gate: float32 [896, 4864], P(('ctx', 'fsdp')), may hold values from -96 to 96
- moment_up: float32 [896, 4864], P(('ctx', 'fsdp')), may hold values from -96 to 96
- moment_down: float32 [4864, 896], P(('ctx', 'fsdp')), may hold values from -224 to 224
- small_params: float32 [2944], P(('ctx', 'fsdp')), may hold values from -1.6 to 1.6, as said below
Outputs:
- activations: bfloat16 [6, 1024, 896], P('fsdp', 'ctx')
- input_grad: float32 [6, 1024, 896], P('fsdp', 'ctx')
- grad_query: float32 [896, 896], P(('ctx', 'fsdp'))
- grad_key: float32 [896, 128], P(('ctx', 'fsdp'))
- grad_value: float32 [896, 128], P(('ctx', 'fsdp'))
- grad_out: float32 [896, 896], P(('ctx', 'fsdp'))
- grad_gate: float32 [896, 4864], P(('ctx', 'fsdp'))
- grad_up: float32 [896, 4864], P(('ctx', 'fsdp'))
- grad_down: float32 [4864, 896], P(('ctx', 'fsdp'))
- new_query: float32 [896, 896], P(('ctx', 'fsdp'))
- new_key: float32 [896, 128], P(('ctx', 'fsdp'))
- new_value: float32 [896, 128], P(('ctx', 'fsdp'))
- new_out: float32 [896, 896], P(('ctx', 'fsdp'))
- new_gate: float32 [896, 4864], P(('ctx', 'fsdp'))
- new_up: float32 [896, 4864], P(('ctx', 'fsdp'))
- new_down: float32 [4864, 896], P(('ctx', 'fsdp'))
- new_mom_query: float32 [896, 896], P(('ctx', 'fsdp'))
- new_mom_key: float32 [896, 128], P(('ctx', 'fsdp'))
- new_mom_value: float32 [896, 128], P(('ctx', 'fsdp'))
- new_mom_out: float32 [896, 896], P(('ctx', 'fsdp'))
- new_mom_gate: float32 [896, 4864], P(('ctx', 'fsdp'))
- new_mom_up: float32 [896, 4864], P(('ctx', 'fsdp'))
- new_mom_down: float32 [4864, 896], P(('ctx', 'fsdp'))
- grad_small: float32 [2944], P(('ctx', 'fsdp'))
- new_small: float32 [2944], P(('ctx', 'fsdp'))
Inputs may be any that keep to these rules, and one draw needn't show every extreme that they name: `block_order`: stored blocks 2 c and 2 c + 1 hold position blocks j and 31 - j for some j; every number appears once. `small_params`: the first 1792 entries are gains between 0.6 and 1.4.
All inputs are finite; a program needn't handle non-finite values.
Results may differ from a plain program's by a relative error of at most 0.017.
The roundings to bfloat16 on the way count: a program that leaves them out, or rounds other values in their place, can miss the bound.
Values may be sent and summed in bfloat16 or wider, within the bound.
No kernel may reach another device: no remote copies, remote signals or barrier semaphores. Data moves between devices by JAX's collectives and lax.ppermute only.
A program may use at most 256 MiB of HBM per device.

v0:
```python
import math

import jax
import jax.numpy as jnp
from jax import lax
from jax.sharding import PartitionSpec as P

HEAD_DIM = 64
NS_STEPS = 5


theta_base = 1000000.0
norm_eps = 1e-06
ns_coeffs = (3.4445, -4.775, 2.0315)
momentum_decay = 0.95
muon_rate = 1.5
plain_rate = 2.0


def shortened(shard):

    def short(part):
        return part.astype(jnp.bfloat16) if part.dtype == jnp.float32 else part

    return jax.tree.map(short, shard)


def rope_tables(positions):
    frequency = theta_base ** (-jnp.arange(0, HEAD_DIM, 2, dtype=jnp.float32) / HEAD_DIM)
    angles = positions.astype(jnp.float32)[:, None] * frequency[None, :]
    angles = jnp.concatenate([angles, angles], axis=-1)
    return (jnp.cos(angles), jnp.sin(angles))


def rotate(values, cosine_table, sine_table):
    half_width = values.shape[-1] // 2
    turned = jnp.concatenate([-values[..., half_width:], values[..., :half_width]], axis=-1)
    return values * cosine_table + turned * sine_table


def unrotate(gradient, cosine_table, sine_table):
    half_width = gradient.shape[-1] // 2
    shifted = gradient * sine_table
    turned_back = jnp.concatenate([shifted[..., half_width:], -shifted[..., :half_width]], axis=-1)
    return gradient * cosine_table + turned_back


def norm_forward(values):
    rescale = lax.rsqrt(jnp.mean(values * values, axis=-1, keepdims=True) + norm_eps)
    return (values * rescale, rescale)


def norm_backward(grad_normed, plain_norm, rescale, gain_values):
    inner_term = grad_normed * gain_values
    grad_in = rescale * (
        inner_term - plain_norm * jnp.mean(inner_term * plain_norm, axis=-1, keepdims=True)
    )
    return (grad_in, jnp.sum(grad_normed * plain_norm, axis=0))


def product(left_side, right_side):
    return jnp.dot(left_side, right_side, preferred_element_type=jnp.float32)


def contract_rows(left_side, right_side):
    return lax.dot_general(
        left_side, right_side, (((0,), (0,)), ((), ())), preferred_element_type=jnp.float32
    )


def contract_cols(left_side, right_side):
    return lax.dot_general(
        left_side, right_side, (((1,), (1,)), ((), ())), preferred_element_type=jnp.float32
    )


def exact_product(left_side, right_side):
    return jnp.dot(left_side, right_side, precision=lax.Precision.HIGHEST)


def exact_gram(matrix):
    return lax.dot_general(
        matrix, matrix, (((1,), (1,)), ((), ())), precision=lax.Precision.HIGHEST
    )


def padded_form(matrix, height, breadth):
    if matrix.shape[0] > matrix.shape[1]:
        matrix = matrix.T
    return jnp.pad(matrix, ((0, height - matrix.shape[0]), (0, breadth - matrix.shape[1])))


def on_device(
    tokens_in,
    cotangent,
    block_order,
    weight_query,
    weight_key,
    weight_value,
    weight_out,
    weight_gate,
    weight_up,
    weight_down,
    moment_query,
    moment_key,
    moment_value,
    moment_out,
    moment_gate,
    moment_up,
    moment_down,
    small_params,
):
    masters = (
        weight_query,
        weight_key,
        weight_value,
        weight_out,
        weight_gate,
        weight_up,
        weight_down,
    )
    moments = (
        moment_query,
        moment_key,
        moment_value,
        moment_out,
        moment_gate,
        moment_up,
        moment_down,
    )
    seq_count, seq_rows, model_width = tokens_in.shape
    ctx_count = lax.axis_size("ctx")
    seq_length = seq_rows * ctx_count
    block_rows = seq_rows // 2
    all_tokens = seq_count * lax.axis_size("fsdp") * seq_length
    row_count = seq_count * seq_rows
    kv_width = weight_key.shape[1]
    head_count = model_width // HEAD_DIM
    kv_count = kv_width // HEAD_DIM
    group_size = head_count // kv_count
    score_scale = HEAD_DIM ** (-0.5)
    query_low = weight_query.astype(jnp.bfloat16)
    key_low = weight_key.astype(jnp.bfloat16)
    value_low = weight_value.astype(jnp.bfloat16)
    out_low = weight_out.astype(jnp.bfloat16)
    gate_low = weight_gate.astype(jnp.bfloat16)
    up_low = weight_up.astype(jnp.bfloat16)
    down_low = weight_down.astype(jnp.bfloat16)
    small_low = small_params.astype(jnp.bfloat16)
    query_mat, key_mat, value_mat, out_mat, gate_mat, up_mat, down_mat, small_whole = (
        lax.all_gather(query_low, ("ctx", "fsdp"), axis=0, tiled=True),
        lax.all_gather(key_low, ("ctx", "fsdp"), axis=0, tiled=True),
        lax.all_gather(value_low, ("ctx", "fsdp"), axis=0, tiled=True),
        lax.all_gather(out_low, ("ctx", "fsdp"), axis=0, tiled=True),
        lax.all_gather(gate_low, ("ctx", "fsdp"), axis=0, tiled=True),
        lax.all_gather(up_low, ("ctx", "fsdp"), axis=0, tiled=True),
        lax.all_gather(down_low, ("ctx", "fsdp"), axis=0, tiled=True),
        lax.all_gather(small_low, ("ctx", "fsdp"), axis=0, tiled=True),
    )
    small_vals = small_whole.astype(jnp.float32)
    gain_one = small_vals[:model_width]
    gain_two = small_vals[model_width : 2 * model_width]
    bias_query = small_vals[2 * model_width : 3 * model_width]
    bias_key = small_vals[3 * model_width : 3 * model_width + kv_width]
    bias_value = small_vals[3 * model_width + kv_width :]
    stored = jnp.arange(block_rows, dtype=jnp.int32)
    key_pos = (block_order[:, None] * block_rows + stored[None, :]).reshape(seq_length)
    ctx_index = lax.axis_index("ctx")
    own_blocks = lax.dynamic_slice_in_dim(block_order, 2 * ctx_index, 2)
    query_pos = (own_blocks[:, None] * block_rows + stored[None, :]).reshape(seq_rows)
    cos_table, sin_table = rope_tables(query_pos)
    cos_rows = cos_table[None, :, None, :]
    sin_rows = sin_table[None, :, None, :]
    inputs = tokens_in.astype(jnp.float32).reshape(row_count, model_width)
    plain_one, rescale_one = norm_forward(inputs)
    normed_one = (plain_one * gain_one).astype(jnp.bfloat16)
    query_lin = product(normed_one, query_mat) + bias_query
    key_lin = product(normed_one, key_mat) + bias_key
    value_lin = product(normed_one, value_mat) + bias_value
    query_rot = rotate(
        query_lin.reshape(seq_count, seq_rows, head_count, HEAD_DIM), cos_rows, sin_rows
    ).astype(jnp.bfloat16)
    query_rot = query_rot.reshape(seq_count, seq_rows, kv_count, group_size, HEAD_DIM)
    key_rot = rotate(
        key_lin.reshape(seq_count, seq_rows, kv_count, HEAD_DIM), cos_rows, sin_rows
    ).astype(jnp.bfloat16)
    key_rot = key_rot.reshape(seq_count, seq_rows, kv_width)
    value_rows = value_lin.astype(jnp.bfloat16).reshape(seq_count, seq_rows, kv_width)
    keys_all, values_all = (
        lax.all_gather(key_rot, "ctx", axis=1, tiled=True),
        lax.all_gather(value_rows, "ctx", axis=1, tiled=True),
    )
    key_block = math.gcd(seq_length, 512)
    block_count = seq_length // key_block
    stat_shape = (seq_count, seq_rows, kv_count, group_size, 1)
    out_shape = (seq_count, seq_rows, kv_count, group_size, HEAD_DIM)

    def key_slice(number):
        begin = number * key_block
        keys_blk = lax.dynamic_slice_in_dim(keys_all, begin, key_block, 1).reshape(
            seq_count, key_block, kv_count, HEAD_DIM
        )
        values_blk = lax.dynamic_slice_in_dim(values_all, begin, key_block, 1).reshape(
            seq_count, key_block, kv_count, HEAD_DIM
        )
        pos_blk = lax.dynamic_slice_in_dim(key_pos, begin, key_block, 0)
        allowed = (pos_blk[None, :] <= query_pos[:, None])[None, :, None, None, :]
        return (keys_blk, values_blk, allowed)

    def block_scores(keys_blk):
        return (
            jnp.einsum("bqhgd,bkhd->bqhgk", query_rot, keys_blk, preferred_element_type=jnp.float32)
            * score_scale
        )

    def first_pass(number, loop_state):
        running, totals = loop_state
        keys_blk, values_blk, allowed = key_slice(number)
        masked = jnp.where(allowed, block_scores(keys_blk), -1e30)
        highest = jnp.maximum(running, jnp.max(masked, axis=-1, keepdims=True))
        weights = jnp.where(allowed, jnp.exp(masked - highest), 0.0)
        totals = totals * jnp.exp(running - highest) + jnp.sum(weights, axis=-1, keepdims=True)
        return (highest, totals)

    row_max, row_total = lax.fori_loop(
        0,
        block_count,
        first_pass,
        (jnp.full(stat_shape, -1e30, jnp.float32), jnp.zeros(stat_shape, jnp.float32)),
    )

    def block_probs(keys_blk, allowed):
        return jnp.where(allowed, jnp.exp(block_scores(keys_blk) - row_max), 0.0) / row_total

    def second_pass(number, loop_state):
        mixed, exact_sum = loop_state
        keys_blk, values_blk, allowed = key_slice(number)
        probabilities = block_probs(keys_blk, allowed)
        mixed = mixed + jnp.einsum(
            "bqhgk,bkhd->bqhgd",
            probabilities.astype(jnp.bfloat16),
            values_blk,
            preferred_element_type=jnp.float32,
        )
        exact_sum = exact_sum + jnp.einsum(
            "bqhgk,bkhd->bqhgd",
            probabilities,
            values_blk.astype(jnp.float32),
            precision=lax.Precision.HIGHEST,
        )
        return (mixed, exact_sum)

    mixed, exact_sum = lax.fori_loop(
        0,
        block_count,
        second_pass,
        (jnp.zeros(out_shape, jnp.float32), jnp.zeros(out_shape, jnp.float32)),
    )
    attn_low = mixed.astype(jnp.bfloat16).reshape(row_count, model_width)
    residual = inputs + product(attn_low, out_mat)
    plain_two, rescale_two = norm_forward(residual)
    normed_two = (plain_two * gain_two).astype(jnp.bfloat16)
    gate_lin = product(normed_two, gate_mat)
    up_lin = product(normed_two, up_mat)
    sigmoid_gate = lax.logistic(gate_lin)
    silu_gate = gate_lin * sigmoid_gate
    hidden = (silu_gate * up_lin).astype(jnp.bfloat16)
    result = residual + product(hidden, down_mat)
    activations = result.astype(jnp.bfloat16).reshape(seq_count, seq_rows, model_width)
    grad_low = cotangent.reshape(row_count, model_width)
    grad_result = grad_low.astype(jnp.float32)
    grad_hidden = contract_cols(grad_low, down_mat)
    grad_gate_lin = (
        grad_hidden * up_lin * sigmoid_gate * (1.0 + gate_lin * (1.0 - sigmoid_gate))
    ).astype(jnp.bfloat16)
    grad_up_lin = (grad_hidden * silu_gate).astype(jnp.bfloat16)
    part_down = contract_rows(hidden, grad_low)
    part_gate = contract_rows(normed_two, grad_gate_lin)
    part_up = contract_rows(normed_two, grad_up_lin)
    grad_normed_two = contract_cols(grad_gate_lin, gate_mat) + contract_cols(grad_up_lin, up_mat)
    grad_norm_two, grad_gain_two = norm_backward(grad_normed_two, plain_two, rescale_two, gain_two)
    grad_residual = grad_result + grad_norm_two
    grad_attn = grad_residual.astype(jnp.bfloat16)
    part_out = contract_rows(attn_low, grad_attn)
    grad_mixed = contract_cols(grad_attn, out_mat).astype(jnp.bfloat16).reshape(out_shape)
    delta_rows = jnp.sum(grad_mixed.astype(jnp.float32) * exact_sum, axis=-1, keepdims=True)

    def back_pass(number, loop_state):
        grad_query_acc, grad_keys_acc, grad_values_acc = loop_state
        keys_blk, values_blk, allowed = key_slice(number)
        probabilities = block_probs(keys_blk, allowed)
        grad_probs = jnp.einsum(
            "bqhgd,bkhd->bqhgk", grad_mixed, values_blk, preferred_element_type=jnp.float32
        )
        grad_scores = (probabilities * (grad_probs - delta_rows)).astype(jnp.bfloat16)
        grad_query_acc = grad_query_acc + jnp.einsum(
            "bqhgk,bkhd->bqhgd", grad_scores, keys_blk, preferred_element_type=jnp.float32
        )
        key_part = (
            jnp.einsum(
                "bqhgk,bqhgd->bkhd", grad_scores, query_rot, preferred_element_type=jnp.float32
            )
            * score_scale
        )
        value_part = jnp.einsum(
            "bqhgk,bqhgd->bkhd",
            probabilities.astype(jnp.bfloat16),
            grad_mixed,
            preferred_element_type=jnp.float32,
        )
        begin = number * key_block
        grad_keys_acc = lax.dynamic_update_slice_in_dim(
            grad_keys_acc, key_part.reshape(seq_count, key_block, kv_width), begin, 1
        )
        grad_values_acc = lax.dynamic_update_slice_in_dim(
            grad_values_acc, value_part.reshape(seq_count, key_block, kv_width), begin, 1
        )
        return (grad_query_acc, grad_keys_acc, grad_values_acc)

    zero_keys = jnp.zeros((seq_count, seq_length, kv_width), jnp.float32)
    grad_query_rot, grad_keys_all, grad_values_all = lax.fori_loop(
        0, block_count, back_pass, (jnp.zeros(out_shape, jnp.float32), zero_keys, zero_keys)
    )
    own_keys, own_values = (
        lax.psum_scatter(grad_keys_all, "ctx", scatter_dimension=1, tiled=True),
        lax.psum_scatter(grad_values_all, "ctx", scatter_dimension=1, tiled=True),
    )
    grad_query_lin = unrotate(
        (grad_query_rot * score_scale).reshape(seq_count, seq_rows, head_count, HEAD_DIM),
        cos_rows,
        sin_rows,
    )
    grad_query_lin = grad_query_lin.astype(jnp.bfloat16).reshape(row_count, model_width)
    grad_key_lin = unrotate(
        own_keys.reshape(seq_count, seq_rows, kv_count, HEAD_DIM), cos_rows, sin_rows
    )
    grad_key_lin = grad_key_lin.astype(jnp.bfloat16).reshape(row_count, kv_width)
    grad_value_lin = own_values.astype(jnp.bfloat16).reshape(row_count, kv_width)
    part_query = contract_rows(normed_one, grad_query_lin)
    part_key = contract_rows(normed_one, grad_key_lin)
    part_value = contract_rows(normed_one, grad_value_lin)
    grad_normed_one = (
        contract_cols(grad_query_lin, query_mat)
        + contract_cols(grad_key_lin, key_mat)
        + contract_cols(grad_value_lin, value_mat)
    )
    grad_norm_one, grad_gain_one = norm_backward(grad_normed_one, plain_one, rescale_one, gain_one)
    input_grad = (grad_residual + grad_norm_one).reshape(seq_count, seq_rows, model_width)
    part_small = jnp.concatenate(
        [
            grad_gain_one,
            grad_gain_two,
            jnp.sum(grad_query_lin.astype(jnp.float32), axis=0),
            jnp.sum(grad_key_lin.astype(jnp.float32), axis=0),
            jnp.sum(grad_value_lin.astype(jnp.float32), axis=0),
        ]
    )
    sum_query, sum_key, sum_value, sum_out, sum_gate, sum_up, sum_down, sum_small = (
        lax.psum_scatter(part_query, ("ctx", "fsdp"), scatter_dimension=0, tiled=True),
        lax.psum_scatter(part_key, ("ctx", "fsdp"), scatter_dimension=0, tiled=True),
        lax.psum_scatter(part_value, ("ctx", "fsdp"), scatter_dimension=0, tiled=True),
        lax.psum_scatter(part_out, ("ctx", "fsdp"), scatter_dimension=0, tiled=True),
        lax.psum_scatter(part_gate, ("ctx", "fsdp"), scatter_dimension=0, tiled=True),
        lax.psum_scatter(part_up, ("ctx", "fsdp"), scatter_dimension=0, tiled=True),
        lax.psum_scatter(part_down, ("ctx", "fsdp"), scatter_dimension=0, tiled=True),
        lax.psum_scatter(part_small, ("ctx", "fsdp"), scatter_dimension=0, tiled=True),
    )
    summed = (sum_query, sum_key, sum_value, sum_out, sum_gate, sum_up, sum_down)
    new_moments = tuple(
        (momentum_decay * moment + reduced for moment, reduced in zip(moments, summed))
    )
    outgoing = tuple(
        (
            reduced + momentum_decay * fresh_moment
            for reduced, fresh_moment in zip(summed, new_moments)
        )
    )
    device_count = lax.axis_size(("ctx", "fsdp"))
    fsdp_count = lax.axis_size("fsdp")
    fsdp_index = lax.axis_index("fsdp")
    ctx_spacing = ctx_count // 8
    owns_one = jnp.logical_and(ctx_index % ctx_spacing == 0, ctx_index // ctx_spacing < 7)
    number_here = jnp.where(owns_one, ctx_index // ctx_spacing, 7)
    whole_updates = (
        lax.all_gather(outgoing[0], ("ctx", "fsdp"), axis=0, tiled=True),
        lax.all_gather(outgoing[1], ("ctx", "fsdp"), axis=0, tiled=True),
        lax.all_gather(outgoing[2], ("ctx", "fsdp"), axis=0, tiled=True),
        lax.all_gather(outgoing[3], ("ctx", "fsdp"), axis=0, tiled=True),
        lax.all_gather(outgoing[4], ("ctx", "fsdp"), axis=0, tiled=True),
        lax.all_gather(outgoing[5], ("ctx", "fsdp"), axis=0, tiled=True),
        lax.all_gather(outgoing[6], ("ctx", "fsdp"), axis=0, tiled=True),
    )
    pad_breadth = max(model_width, weight_gate.shape[1])

    def make_branch(number):

        def branch():
            return padded_form(whole_updates[number], model_width, pad_breadth)

        return branch

    def empty_branch():
        return jnp.zeros((model_width, pad_breadth), jnp.float32)

    canonical = lax.switch(
        number_here, [make_branch(number) for number in range(7)] + [empty_branch]
    )
    half_breadth = pad_breadth // fsdp_count
    current = lax.dynamic_slice_in_dim(canonical, fsdp_index * half_breadth, half_breadth, 1)
    total_squares = lax.psum(jnp.sum(current * current), "fsdp")
    current = current / (jnp.sqrt(total_squares) + 1e-07)
    alpha_term, beta_term, gamma_term = ns_coeffs
    for sweep_number in range(NS_STEPS):
        gram_matrix = lax.psum(exact_gram(current), "fsdp")
        square = exact_product(gram_matrix, gram_matrix)
        polynomial = beta_term * gram_matrix + gamma_term * square
        current = alpha_term * current + exact_product(polynomial, current)
    joined = lax.all_gather(shortened(current), "fsdp", axis=1, tiled=True).astype(current.dtype)
    leader = fsdp_index == 0
    orthogonal = []
    for number in range(7):
        rows_all = masters[number].shape[0] * device_count
        columns = masters[number].shape[1]
        if rows_all > columns:
            piece = joined[:columns, :rows_all].T
        else:
            piece = joined[:rows_all, :columns]
        keep_here = jnp.logical_and(number_here == number, leader)
        orthogonal.append(jnp.where(keep_here, piece, 0.0))
    shards = list(
        (
            lax.psum_scatter(orthogonal[0], ("ctx", "fsdp"), scatter_dimension=0, tiled=True),
            lax.psum_scatter(orthogonal[1], ("ctx", "fsdp"), scatter_dimension=0, tiled=True),
            lax.psum_scatter(orthogonal[2], ("ctx", "fsdp"), scatter_dimension=0, tiled=True),
            lax.psum_scatter(orthogonal[3], ("ctx", "fsdp"), scatter_dimension=0, tiled=True),
            lax.psum_scatter(orthogonal[4], ("ctx", "fsdp"), scatter_dimension=0, tiled=True),
            lax.psum_scatter(orthogonal[5], ("ctx", "fsdp"), scatter_dimension=0, tiled=True),
            lax.psum_scatter(orthogonal[6], ("ctx", "fsdp"), scatter_dimension=0, tiled=True),
        )
    )
    new_masters = []
    for number in range(7):
        rows_all = masters[number].shape[0] * device_count
        columns = masters[number].shape[1]
        factor = math.sqrt(max(1.0, columns / rows_all))
        new_masters.append(masters[number] - muon_rate * (shards[number] * factor))
    new_small = small_params - plain_rate / math.sqrt(all_tokens) * sum_small
    return (
        activations,
        input_grad,
        sum_query,
        sum_key,
        sum_value,
        sum_out,
        sum_gate,
        sum_up,
        sum_down,
        new_masters[0],
        new_masters[1],
        new_masters[2],
        new_masters[3],
        new_masters[4],
        new_masters[5],
        new_masters[6],
        new_moments[0],
        new_moments[1],
        new_moments[2],
        new_moments[3],
        new_moments[4],
        new_moments[5],
        new_moments[6],
        sum_small,
        new_small,
    )


def solution(mesh):
    placed = (
        P("fsdp", "ctx", None),
        P("fsdp", "ctx", None),
        P(),
        P(("ctx", "fsdp"), None),
        P(("ctx", "fsdp"), None),
        P(("ctx", "fsdp"), None),
        P(("ctx", "fsdp"), None),
        P(("ctx", "fsdp"), None),
        P(("ctx", "fsdp"), None),
        P(("ctx", "fsdp"), None),
        P(("ctx", "fsdp"), None),
        P(("ctx", "fsdp"), None),
        P(("ctx", "fsdp"), None),
        P(("ctx", "fsdp"), None),
        P(("ctx", "fsdp"), None),
        P(("ctx", "fsdp"), None),
        P(("ctx", "fsdp"), None),
        P(("ctx", "fsdp")),
    )
    return jax.shard_map(
        on_device,
        mesh=mesh,
        in_specs=placed,
        out_specs=(
            P("fsdp", "ctx", None),
            P("fsdp", "ctx", None),
            P(("ctx", "fsdp"), None),
            P(("ctx", "fsdp"), None),
            P(("ctx", "fsdp"), None),
            P(("ctx", "fsdp"), None),
            P(("ctx", "fsdp"), None),
            P(("ctx", "fsdp"), None),
            P(("ctx", "fsdp"), None),
            P(("ctx", "fsdp"), None),
            P(("ctx", "fsdp"), None),
            P(("ctx", "fsdp"), None),
            P(("ctx", "fsdp"), None),
            P(("ctx", "fsdp"), None),
            P(("ctx", "fsdp"), None),
            P(("ctx", "fsdp"), None),
            P(("ctx", "fsdp"), None),
            P(("ctx", "fsdp"), None),
            P(("ctx", "fsdp"), None),
            P(("ctx", "fsdp"), None),
            P(("ctx", "fsdp"), None),
            P(("ctx", "fsdp"), None),
            P(("ctx", "fsdp"), None),
            P(("ctx", "fsdp")),
            P(("ctx", "fsdp")),
        ),
        check_vma=False,
    )
```

profile of v0, /device:TPU:25, one launch (start us, length us, event | category | flops | bytes accessed | tf_op | source)
XLA Modules:
  0.0 3387.5 jit_solution(4750096806720764936)
XLA Ops:
  19.9 35.0 %all-gather = bf16[32,28,128]{2,1,0:T(8,128)(2,1)S(1)} all-gather(bf16[1,28,128]{2,1,0:T(8,128)(2,1)S(1)} %convert_bitcast_fusion.5), channel_id=1, replica_groups=mesh['ctx'=16,'fsdp'=2] {'ctx','fsdp'}, dimensions={0}, use_global_device_ids=true | all-gather | bytes 236544 | tf_op jit(solution)/shard_map/all_gather | solution.py:153
  55.6 38.1 %all-gather.1 = bf16[32,28,128]{2,1,0:T(8,128)(2,1)S(1)} all-gather(bf16[1,28,128]{2,1,0:T(8,128)(2,1)S(1)} %convert_bitcast_fusion.4), channel_id=1, replica_groups=mesh['ctx'=16,'fsdp'=2] {'ctx','fsdp'}, dimensions={0}, use_global_device_ids=true | all-gather | bytes 236544 | tf_op jit(solution)/shard_map/all_gather | solution.py:152
  94.6 42.1 %all-reduce.4 = bf16[2944]{0:T(1024)(128)(2,1)S(1)} all-reduce(bf16[2944]{0:T(1024)(128)(2,1)S(1)} %dynamic-update-slice), channel_id=1, replica_groups=mesh['ctx'=16,'fsdp'=2] {'ctx','fsdp'}, use_global_device_ids=true, to_apply=%add.4 | all-reduce | flops 2944 | bytes 11776
  146.6 38.0 %all_gather.79 = bf16[3,1024,128]{2,1,0:T(8,128)(2,1)} all-gather(bf16[3,64,128]{2,1,0:T(8,128)(2,1)S(1)} %add_convert_fusion.6), channel_id=1, replica_groups=mesh['ctx'=16,'fsdp'=2] {'ctx'}, dimensions={1}, use_global_device_ids=true | all-gather | bytes 835584 | tf_op jit(solution)/shard_map/all_gather | solution.py:190
  187.2 44.5 %all_gather.77 = bf16[3,1024,128]{2,1,0:T(8,128)(2,1)} all-gather(bf16[3,64,128]{2,1,0:T(8,128)(2,1)S(1)} %bitcast.350), channel_id=1, replica_groups=mesh['ctx'=16,'fsdp'=2] {'ctx'}, dimensions={1}, use_global_device_ids=true | all-gather | bytes 835584 | tf_op jit(solution)/shard_map/all_gather | solution.py:191
  264.8 10.9 while.50
  275.7 19.6 while.51
  301.8 13.2 reshape.476
  315.1 24.6 reshape.478
  339.6 7.6 fusion.105
  351.3 42.6 %all-gather.24.cloned.1.call-done = bf16[4864,896]{1,0:T(8,128)(2,1)} async-done(((bf16[152,896]{1,0:T(8,128)(2,1)}), bf16[4864,896]{1,0:T(8,128)(2,1)}) %all-gather.24.cloned.1.call-update) | async-done | bytes 8716304 | tf_op jit(solution)/shard_map/all_gather | solution.py:157
  393.9 11.3 multiply_convert_fusion
  424.3 41.4 %while.52 = (s32[]{:T(128)}, f32[3,64,2,7,64]{1,4,3,2,0:T(8,128)}, f32[3,1024,128]{2,1,0:T(8,128)}, f32[3,1024,128]{2,1,0:T(8,128)}, bf16[3,1024,128]{1,2,0:T(8,...) while((s32[]{:T(128)}, f32[3,64,2,7,64]{1,4,3,2,0:T(8,128)}, ...), condition=%wide.region_11.12_spmd.clone, body=%wide.region_10.11_spmd.clone.sunk | while | flops 892387392 | bytes 46898088 | solution.py:321
  467.2 7.6 fusion.113
  486.7 8.5 fusion.112
  495.2 8.5 fusion.111
  503.7 25.3 reduce-scatter.30.cloned.1.call-done
  535.6 71.5 %reduce-scatter.32.cloned.1.call-done = f32[3,64,128]{2,1,0:T(8,128)} async-done(((f32[3,1024,128]{2,1,0:T(8,128)}), f32[3,64,128]{2,1,0:T(8,128)}) %reduce-scatter.32.cloned.1.call-update) | async-done | bytes 98320 | tf_op jit(solution)/shard_map/reduce_scatter | solution.py:326
  611.6 713.6 %fusion.98 = (f32[32,896]{1,0:T(8,128)S(1)}, f32[32,128]{1,0:T(8,128)S(1)}, f32[32,128]{1,0:T(8,128)S(1)}, f32[32,896]{1,0:T(8,128)S(1)}, f32[32,4864]{1,0:T(8,128)}, /*index=5*/f32[32,4864]{1,0:T(8,128)}) fusion(f32[896,896]{1,0:T(8,128)S(1)} %fusion.109, f32[896,128]{1,0:T(8,128)} %fusion.110, f32[896,128]{1,0:T(8,128)} %convolution_bitcast_fusion.3, ...), kind=kCustom, calls=%all-reduce-scatter.11 | all-reduce-scatter fusion | flops 12058625 | bytes 43712512
  1369.9 42.1 %collective-permute-done.19 = f32[28,4864]{1,0:T(8,128)S(1)} collective-permute-done((f32[28,4864]{1,0:T(8,128)S(1)}, f32[28,4864]{1,0:T(8,128)S(1)}, u32[]{:S(2)}, u32[]{:S(2)}) %collective-permute-start.19) | collective-permute-done | bytes 544800
  1412.8 18.9 concatenate.65
  1436.3 19.9 collective-permute-start.21
  1460.3 31.1 collective-permute-done.23
  1492.2 18.9 concatenate.66
  1518.0 16.8 collective-permute-start.9
  1551.7 44.6 %all-gather.8 = f32[32,28,128]{2,1,0:T(8,128)} all-gather(f32[1,28,128]{2,1,0:T(8,128)S(1)} %get-tuple-element.1051), channel_id=1, replica_groups=mesh['ctx'=16,'fsdp'=2] {'ctx','fsdp'}, dimensions={0}, use_global_device_ids=true | all-gather | bytes 473088 | tf_op jit(solution)/shard_map/all_gather | solution.py:387
  1597.5 45.4 %all-gather.7 = f32[32,28,128]{2,1,0:T(8,128)} all-gather(f32[1,28,128]{2,1,0:T(8,128)S(1)} %get-tuple-element.1054), channel_id=1, replica_groups=mesh['ctx'=16,'fsdp'=2] {'ctx','fsdp'}, dimensions={0}, use_global_device_ids=true | all-gather | bytes 473088 | tf_op jit(solution)/shard_map/all_gather | solution.py:386
  1642.9 30.2 all-gather.42.cloned.1.call-done
  1673.1 131.3 %all-gather.44.cloned.1.call-done = f32[32,28,4864]{2,1,0:T(8,128)} async-done(((f32[1,28,4864]{2,1,0:T(8,128)}), f32[32,28,4864]{2,1,0:T(8,128)}) %all-gather.44.cloned.1.call-update) | async-done | bytes 17432592 | tf_op jit(solution)/shard_map/all_gather | solution.py:390
  1804.4 119.6 %all-gather.26.cloned.1.call-done = f32[4864,896]{1,0:T(8,128)} async-done(((f32[152,896]{1,0:T(8,128)}), f32[4864,896]{1,0:T(8,128)}) %all-gather.26.cloned.1.call-update) | async-done | bytes 17432592 | tf_op jit(solution)/shard_map/all_gather | solution.py:391
  1924.0 19.1 conditional.1
  1924.0 18.9 copy.228
  1953.2 33.9 %fusion.54 = f32[896,896]{1,0:T(8,128)} fusion(f32[896,4864]{1,0:T(8,128)} %get-tuple-element.942, s32[]{:T(128)S(6)} %select_n.143, f32[]{:T(128)S(6)} %add.438), kind=kOutput, calls=%fused_computation.75 | convolution fusion | flops 23431561216 | bytes 11927560 | tf_op jit(solution)/shard_map/dot_general | solution.py:82
  1987.6 23.1 all-reduce.40.cloned.1.call-done
  2010.8 14.5 fusion.114
  2025.2 35.0 %multiply_add_fusion.3 = f32[896,2432]{1,0:T(8,128)S(1)} fusion(f32[896,896]{1,0:T(8,128)S(1)} %fusion.114, f32[896,896]{1,0:T(8,128)S(1)} %copy-done.11, f32[]{:T(128)S(6)} %add.438, f32[896,4864]{1,0:T(8,128)} %get-tuple-element.942, s32[]{:T(128)S(6)} %select_n.143), kind=kOutput, calls=%fused_computation.52 | convolution fusion | flops 23440506880 | bytes 32573440 | tf_op jit(solution)/shard_map/dot_general | solution.py:78
  2063.7 31.1 fusion.115
  2094.9 24.6 all-reduce.42.cloned.1.call-done
  2119.6 14.5 fusion.116
  2134.0 35.2 %multiply_add_fusion.2 = f32[896,2432]{1,0:T(8,128)S(1)} fusion(f32[896,2432]{1,0:T(8,128)} %copy-done.93, f32[896,896]{1,0:T(8,128)S(1)} %fusion.116, f32[896,896]{1,0:T(8,128)S(1)} %copy-done.12), kind=kOutput, calls=%fused_computation.51 | convolution fusion | flops 23436148736 | bytes 23855104 | tf_op jit(solution)/shard_map/dot_general | solution.py:78
  2172.8 31.1 fusion.117
  2204.0 24.6 all-reduce.44.cloned.1.call-done
  2228.6 14.5 fusion.118
  2243.1 35.0 %multiply_add_fusion.1 = f32[896,2432]{1,0:T(8,128)S(1)} fusion(f32[896,2432]{1,0:T(8,128)} %copy-done.94, f32[896,896]{1,0:T(8,128)S(1)} %fusion.118, f32[896,896]{1,0:T(8,128)S(1)} %copy-done.13), kind=kOutput, calls=%fused_computation.50 | convolution fusion | flops 23436148736 | bytes 23855104 | tf_op jit(solution)/shard_map/dot_general | solution.py:78
  2281.6 31.1 fusion.119
  2312.8 24.6 all-reduce.46.cloned.1.call-done
  2337.4 14.5 fusion.120
  2351.9 35.2 %multiply_add_fusion = f32[896,2432]{1,0:T(8,128)S(1)} fusion(f32[896,2432]{1,0:T(8,128)} %copy-done.95, f32[896,896]{1,0:T(8,128)S(1)} %fusion.120, f32[896,896]{1,0:T(8,128)S(1)} %copy-done.14), kind=kOutput, calls=%fused_computation.49 | convolution fusion | flops 23436148736 | bytes 23855104 | tf_op jit(solution)/shard_map/dot_general | solution.py:78
  2390.6 31.1 fusion.121
  2421.8 24.6 all-reduce.48.cloned.1.call-done
  2446.4 14.5 fusion.122
  2460.9 33.5 add_convert_fusion
  2494.5 22.2 all-gather.28.cloned.1.call-done
  2516.7 10.8 convert_element_type.218
  2529.6 19.8 select_bitcast_fusion
  2571.8 7.4 fusion.69
  2594.2 580.6 %fusion.97 = (f32[32,896]{1,0:T(8,128)S(1)}, f32[32,896]{1,0:T(8,128)S(1)}, f32[32,4864]{1,0:T(8,128)}, f32[32,4864]{1,0:T(8,128)}) fusion(f32[896,896]{1,0:T(8,128)} %get-tuple-element.1073, f32[896,896]{1,0:T(8,128)S(1)} %get-tuple-element.1072, f32[896,4864]{1,0:T(8,128)} %get-tuple-element.1075, f32[896,4864]{1,0:T(8,128)} %get-tuple-element.1076), kind=kCustom, calls=%all-reduce-scatter.10 | all-reduce-scatter fusion | flops 11796481 | bytes 42762240
  3179.9 16.9 collective-permute-start.33
  3205.6 12.6 collective-permute-done.31
  3237.0 8.6 collective-permute-done.30
  3249.7 38.9 %all-reduce.19 = f32[2944]{0:T(1024)S(1)} all-reduce(f32[2944]{0:T(1024)} %constant_dynamic-update-slice_fusion.2), channel_id=18, replica_groups=mesh['ctx'=16,'fsdp'=2] {'ctx','fsdp'}, use_global_device_ids=true, to_apply=%region_49.50.clone | all-reduce | flops 2944 | bytes 23552
  3312.9 19.7 concatenate.69
  3332.6 18.2 collective-permute-done.39
  3350.8 20.2 concatenate.70
  (557 shorter events, 397.8 us)
Async XLA Ops:
  7.3 226.7 %all-gather.30.cloned.1.call-start = ((), (), s32[]{:S(2)}) async-start(), calls=%async_computation.13 | async-start | bytes 1892352 | tf_op jit(solution)/shard_map/all_gather | solution.py:151
  9.0 289.4 %all-gather.32.cloned.1.call-start = ((), (), s32[]{:S(2)}) async-start(), calls=%async_computation.14 | async-start | bytes 1892352 | tf_op jit(solution)/shard_map/all_gather | solution.py:154
  10.6 291.2 %all-gather.34.cloned.1.call-start = ((), (), s32[]{:S(2)}) async-start(), calls=%async_computation.15 | async-start | bytes 10272768 | tf_op jit(solution)/shard_map/all_gather | solution.py:155
  12.5 302.6 %all-gather.36.cloned.1.call-start = ((), (), s32[]{:S(2)}) async-start(), calls=%async_computation.16 | async-start | bytes 10272768 | tf_op jit(solution)/shard_map/all_gather | solution.py:156
  14.4 379.5 %all-gather.24.cloned.1.call-start = ((), (), s32[]{:S(2)}) async-start(), calls=%async_computation.3 | async-start | bytes 8988672 | tf_op jit(solution)/shard_map/all_gather | solution.py:157
  15.2 513.8 %reduce-scatter.30.cloned.1.call-start = ((), (), s32[]{:S(2)}) async-start(), calls=%async_computation.4 | async-start | bytes 1671168 | tf_op jit(solution)/shard_map/reduce_scatter | solution.py:325
  18.4 239.9 %copy-start.49 = (f32[64,64]{1,0:T(8,128)}, f32[64,64]{1,0:T(8,128)S(1)}, u32[]{:S(2)}) copy-start(f32[64,64]{1,0:T(8,128)S(1)} %get-tuple-element.1092) | copy-start | bytes 49156
  18.4 239.9 %copy-start.55 = (f32[64,64]{1,0:T(8,128)}, f32[64,64]{1,0:T(8,128)S(1)}, u32[]{:S(2)}) copy-start(f32[64,64]{1,0:T(8,128)S(1)} %get-tuple-element.1091) | copy-start | bytes 49156
  465.7 141.4 %reduce-scatter.32.cloned.1.call-start = ((), (), s32[]{:S(2)}) async-start(), calls=%async_computation.5 | async-start | bytes 1671168 | tf_op jit(solution)/shard_map/reduce_scatter | solution.py:326
  466.5 1047.4 %reduce-scatter.34.cloned.1.call-start = ((), (), s32[]{:S(2)}) async-start(), calls=%async_computation.21 | async-start | bytes 17977344
  474.8 1168.0 %all-gather.38.cloned.1.call-start = ((), (), s32[]{:S(2)}) async-start(), calls=%async_computation.17 | async-start | bytes 3784704 | tf_op jit(solution)/shard_map/all_gather | solution.py:385
  1325.2 15.9 collective-permute-start.2
  1327.2 13.9 collective-permute-start.1
  1329.1 12.0 collective-permute-start
  1333.6 7.5 collective-permute-start.3
  1343.4 299.4 %all-gather.40.cloned.1.call-start = ((), (), s32[]{:S(2)}) async-start(), calls=%async_computation.18 | async-start | bytes 3784704 | tf_op jit(solution)/shard_map/all_gather | solution.py:388
  1343.5 16.2 collective-permute-start.14
  1345.4 14.3 collective-permute-start.13
  1348.2 11.5 collective-permute-start.12
  1350.6 9.1 collective-permute-start.15
  1361.2 311.9 %all-gather.42.cloned.1.call-start = ((), (), s32[]{:S(2)}) async-start(), calls=%async_computation.19 | async-start | bytes 20545536 | tf_op jit(solution)/shard_map/all_gather | solution.py:389
  1361.2 50.8 %collective-permute-start.18 = (f32[32,4864]{1,0:T(8,128)S(1)}, f32[32,4864]{1,0:T(8,128)S(1)}, u32[]{:S(2)}, u32[]{:S(2)}) collective-permute-start(f32[32,4864]{1,0:T(8,128)S(1)} %copy-done.35), channel_id=1, source_target_pairs={{0,3},{1,4},{2,5},{3,6},{4,7},{5,8},{6,9},{7,10},{8,11},{9,12},{10... | collective-permute-start | bytes 1867784
  1363.1 48.9 %collective-permute-start.17 = (f32[32,4864]{1,0:T(8,128)S(1)}, f32[32,4864]{1,0:T(8,128)S(1)}, u32[]{:S(2)}, u32[]{:S(2)}) collective-permute-start(f32[32,4864]{1,0:T(8,128)S(1)} %copy-done.35), channel_id=1, source_target_pairs={{0,2},{1,3},{2,4},{3,5},{4,6},{5,7},{6,8},{7,9},{8,10},{9,11},{10,... | collective-permute-start | bytes 1867784
  1365.1 47.8 %collective-permute-start.16 = (f32[32,4864]{1,0:T(8,128)S(1)}, f32[32,4864]{1,0:T(8,128)S(1)}, u32[]{:S(2)}, u32[]{:S(2)}) collective-permute-start(f32[32,4864]{1,0:T(8,128)S(1)} %copy-done.35), channel_id=1, source_target_pairs={{0,1},{1,2},{2,3},{3,4},{4,5},{5,6},{6,7},{7,8},{8,9},{9,10},{10,1... | collective-permute-start | bytes 1867784
  1367.8 44.2 %collective-permute-start.19 = (f32[28,4864]{1,0:T(8,128)S(1)}, f32[28,4864]{1,0:T(8,128)S(1)}, u32[]{:S(2)}, u32[]{:S(2)}) collective-permute-start(f32[28,4864]{1,0:T(8,128)S(1)} %slice.81), channel_id=1, source_target_pairs={{0,4},{1,5},{2,6},{3,7},{4,8},{5,9},{6,10},{7,11},{8,12},{9,13},{1... | collective-permute-start | bytes 1634312
  1434.4 370.1 %all-gather.44.cloned.1.call-start = ((), (), s32[]{:S(2)}) async-start(), calls=%async_computation.20 | async-start | bytes 20545536 | tf_op jit(solution)/shard_map/all_gather | solution.py:390
  1434.4 57.0 %collective-permute-start.22 = (f32[32,4864]{1,0:T(8,128)S(1)}, f32[32,4864]{1,0:T(8,128)S(1)}, u32[]{:S(2)}, u32[]{:S(2)}) collective-permute-start(f32[32,4864]{1,0:T(8,128)S(1)} %copy-done.32), channel_id=1, source_target_pairs={{0,3},{1,4},{2,5},{3,6},{4,7},{5,8},{6,9},{7,10},{8,11},{9,12},{10... | collective-permute-start | bytes 1867784
  1436.3 55.1 %collective-permute-start.21 = (f32[32,4864]{1,0:T(8,128)S(1)}, f32[32,4864]{1,0:T(8,128)S(1)}, u32[]{:S(2)}, u32[]{:S(2)}) collective-permute-start(f32[32,4864]{1,0:T(8,128)S(1)} %copy-done.32), channel_id=1, source_target_pairs={{0,2},{1,3},{2,4},{3,5},{4,6},{5,7},{6,8},{7,9},{8,10},{9,11},{10,... | collective-permute-start | bytes 1867784
  1456.3 36.0 %collective-permute-start.20 = (f32[32,4864]{1,0:T(8,128)S(1)}, f32[32,4864]{1,0:T(8,128)S(1)}, u32[]{:S(2)}, u32[]{:S(2)}) collective-permute-start(f32[32,4864]{1,0:T(8,128)S(1)} %copy-done.32), channel_id=1, source_target_pairs={{0,1},{1,2},{2,3},{3,4},{4,5},{5,6},{6,7},{7,8},{8,9},{9,10},{10,1... | collective-permute-start | bytes 1867784
  1458.3 33.2 collective-permute-start.23
  1513.7 410.3 %all-gather.26.cloned.1.call-start = ((), (), s32[]{:S(2)}) async-start(), calls=%async_computation.6 | async-start | bytes 17977344 | tf_op jit(solution)/shard_map/all_gather | solution.py:391
  1516.0 494.8 %all-reduce.40.cloned.1.call-start = ((), (), s32[]{:S(2)}) async-start(), calls=%async_computation.7 | async-start | bytes 6422528 | tf_op jit(solution)/shard_map/psum | solution.py:414
  1516.0 29.7 collective-permute-start.10
  1518.0 30.6 collective-permute-start.9
  1534.8 15.7 collective-permute-start.8
  1536.7 7.1 collective-permute-start.11
  1538.7 57.6 %collective-permute-start.6 = (f32[32,128]{1,0:T(8,128)S(1)}, f32[32,128]{1,0:T(8,128)S(1)}, u32[]{:S(2)}, u32[]{:S(2)}) collective-permute-start(f32[32,128]{1,0:T(8,128)S(1)} %get-tuple-element.1031), channel_id=1, source_target_pairs={{0,3},{1,4},{2,5},{3,6},{4,7},{5,8},{6,9},{7,10},{8,11},{9,12},{10... | collective-permute-start | bytes 49160
  1543.8 52.5 %collective-permute-start.5 = (f32[32,128]{1,0:T(8,128)S(1)}, f32[32,128]{1,0:T(8,128)S(1)}, u32[]{:S(2)}, u32[]{:S(2)}) collective-permute-start(f32[32,128]{1,0:T(8,128)S(1)} %get-tuple-element.1031), channel_id=1, source_target_pairs={{0,2},{1,3},{2,4},{3,5},{4,6},{5,7},{6,8},{7,9},{8,10},{9,11},{10,... | collective-permute-start | bytes 49160
  1545.7 50.5 %collective-permute-start.4 = (f32[32,128]{1,0:T(8,128)S(1)}, f32[32,128]{1,0:T(8,128)S(1)}, u32[]{:S(2)}, u32[]{:S(2)}) collective-permute-start(f32[32,128]{1,0:T(8,128)S(1)} %get-tuple-element.1031), channel_id=1, source_target_pairs={{0,1},{1,2},{2,3},{3,4},{4,5},{5,6},{6,7},{7,8},{8,9},{9,10},{10,1... | collective-permute-start | bytes 49160
  1548.5 47.7 %collective-permute-start.7 = (f32[28,128]{1,0:T(8,128)S(1)}, f32[28,128]{1,0:T(8,128)S(1)}, u32[]{:S(2)}, u32[]{:S(2)}) collective-permute-start(f32[28,128]{1,0:T(8,128)S(1)} %slice.78), channel_id=1, source_target_pairs={{0,4},{1,5},{2,6},{3,7},{4,8},{5,9},{6,10},{7,11},{8,12},{9,13},{1... | collective-permute-start | bytes 43016
  1987.2 132.4 %all-reduce.42.cloned.1.call-start = ((), (), s32[]{:S(2)}) async-start(), calls=%async_computation.8 | async-start | bytes 6422528 | tf_op jit(solution)/shard_map/psum | solution.py:414
  2094.9 133.7 %all-reduce.44.cloned.1.call-start = ((), (), s32[]{:S(2)}) async-start(), calls=%async_computation.9 | async-start | bytes 6422528 | tf_op jit(solution)/shard_map/psum | solution.py:414
  2203.9 133.5 %all-reduce.46.cloned.1.call-start = ((), (), s32[]{:S(2)}) async-start(), calls=%async_computation.10 | async-start | bytes 6422528 | tf_op jit(solution)/shard_map/psum | solution.py:414
  2312.7 133.7 %all-reduce.48.cloned.1.call-start = ((), (), s32[]{:S(2)}) async-start(), calls=%async_computation.11 | async-start | bytes 6422528 | tf_op jit(solution)/shard_map/psum | solution.py:414
  2421.8 95.0 %all-gather.28.cloned.1.call-start = ((), (), s32[]{:S(2)}) async-start(), calls=%async_computation.12 | async-start | bytes 13074432 | tf_op jit(solution)/shard_map/all_gather | solution.py:418
  2494.4 880.8 %all-reduce.50.cloned.1.call-start = ((), (), s32[]{:S(2)}) async-start(), calls=%async_computation.22 | async-start | bytes 36700160
  2594.2 606.5 %copy-start.54 = (f32[3,64,128]{2,1,0:T(8,128)S(1)}, f32[3,64,128]{2,1,0:T(8,128)}, u32[]{:S(2)}) copy-start(f32[3,64,128]{2,1,0:T(8,128)} %reduce-scatter.30.cloned.1.call-done) | copy-start | bytes 294916
  3174.8 136.7 %copy-start.63 = (f32[28,896]{1,0:T(8,128)S(1)}, f32[28,896]{1,0:T(8,128)}, u32[]{:S(2)}) copy-start(f32[28,896]{1,0:T(8,128)} %param.35) | copy-start | bytes 301060
  3174.8 126.4 %collective-permute-start.34 = (f32[32,4864]{1,0:T(8,128)}, f32[32,4864]{1,0:T(8,128)S(1)}, u32[]{:S(2)}, u32[]{:S(2)}) collective-permute-start(f32[32,4864]{1,0:T(8,128)} %get-tuple-element.1022), channel_id=1, source_target_pairs={{0,3},{1,4},{2,5},{3,6},{4,7},{5,8},{6,9},{7,10},{8,11},{9,12},{10... | collective-permute-start | bytes 1867784
  3179.9 123.6 %collective-permute-start.33 = (f32[32,4864]{1,0:T(8,128)}, f32[32,4864]{1,0:T(8,128)S(1)}, u32[]{:S(2)}, u32[]{:S(2)}) collective-permute-start(f32[32,4864]{1,0:T(8,128)} %get-tuple-element.1022), channel_id=1, source_target_pairs={{0,2},{1,3},{2,4},{3,5},{4,6},{5,7},{6,8},{7,9},{8,10},{9,11},{10,... | collective-permute-start | bytes 1867784
  3196.8 21.4 collective-permute-start.31
  3198.7 21.9 collective-permute-start.27
  3201.6 25.8 collective-permute-start.26
  3218.2 12.4 collective-permute-start.25
  3220.7 77.5 %collective-permute-start.35 = (f32[28,4864]{1,0:T(8,128)}, f32[28,4864]{1,0:T(8,128)}, u32[]{:S(2)}, u32[]{:S(2)}) collective-permute-start(f32[28,4864]{1,0:T(8,128)} %slice.85), channel_id=1, source_target_pairs={{0,4},{1,5},{2,6},{3,7},{4,8},{5,9},{6,10},{7,11},{8,12},{9,13},{1... | collective-permute-start | bytes 1634312
  3227.4 7.7 collective-permute-start.24
  3230.6 15.1 collective-permute-start.30
  3235.1 55.6 %collective-permute-start.29 = (f32[32,896]{1,0:T(8,128)S(1)}, f32[32,896]{1,0:T(8,128)}, u32[]{:S(2)}, u32[]{:S(2)}) collective-permute-start(f32[32,896]{1,0:T(8,128)S(1)} %get-tuple-element.1021), channel_id=1, source_target_pairs={{0,2},{1,3},{2,4},{3,5},{4,6},{5,7},{6,8},{7,9},{8,10},{9,11},{10,... | collective-permute-start | bytes 344072
  3245.7 50.3 %collective-permute-start.28 = (f32[32,896]{1,0:T(8,128)S(1)}, f32[32,896]{1,0:T(8,128)}, u32[]{:S(2)}, u32[]{:S(2)}) collective-permute-start(f32[32,896]{1,0:T(8,128)S(1)} %get-tuple-element.1021), channel_id=1, source_target_pairs={{0,1},{1,2},{2,3},{3,4},{4,5},{5,6},{6,7},{7,8},{8,9},{9,10},{10,1... | collective-permute-start | bytes 344072
  3290.7 22.2 collective-permute-start.32
  3296.0 54.9 %collective-permute-start.38 = (f32[32,4864]{1,0:T(8,128)S(1)}, f32[32,4864]{1,0:T(8,128)}, u32[]{:S(2)}, u32[]{:S(2)}) collective-permute-start(f32[32,4864]{1,0:T(8,128)S(1)} %copy-done.33), channel_id=1, source_target_pairs={{0,3},{1,4},{2,5},{3,6},{4,7},{5,8},{6,9},{7,10},{8,11},{9,12},{10... | collective-permute-start | bytes 1867784
  3298.1 52.7 %collective-permute-start.37 = (f32[32,4864]{1,0:T(8,128)S(1)}, f32[32,4864]{1,0:T(8,128)}, u32[]{:S(2)}, u32[]{:S(2)}) collective-permute-start(f32[32,4864]{1,0:T(8,128)S(1)} %copy-done.33), channel_id=1, source_target_pairs={{0,2},{1,3},{2,4},{3,5},{4,6},{5,7},{6,8},{7,9},{8,10},{9,11},{10,... | collective-permute-start | bytes 1867784
  3301.2 49.6 %collective-permute-start.36 = (f32[32,4864]{1,0:T(8,128)S(1)}, f32[32,4864]{1,0:T(8,128)}, u32[]{:S(2)}, u32[]{:S(2)}) collective-permute-start(f32[32,4864]{1,0:T(8,128)S(1)} %copy-done.33), channel_id=1, source_target_pairs={{0,1},{1,2},{2,3},{3,4},{4,5},{5,6},{6,7},{7,8},{8,9},{9,10},{10,1... | collective-permute-start | bytes 1867784
  3303.5 47.3 %collective-permute-start.39 = (f32[28,4864]{1,0:T(8,128)}, f32[28,4864]{1,0:T(8,128)}, u32[]{:S(2)}, u32[]{:S(2)}) collective-permute-start(f32[28,4864]{1,0:T(8,128)} %slice.86), channel_id=1, source_target_pairs={{0,4},{1,5},{2,6},{3,7},{4,8},{5,9},{6,10},{7,11},{8,12},{9,13},{1... | collective-permute-start | bytes 1634312
  (101 other events, 1878.2 us)
Sparse Core Ops, SparseCore 0:
  11.5 56.4 all-gather.29
  71.4 54.6 all-gather.31
  129.5 97.1 all-gather.33
  230.0 83.3 all-gather.35
  316.7 77.2 all-gather.23
  465.8 63.1 reduce-scatter.29
  531.4 75.6 reduce-scatter.31
  610.0 420.5 reduce-scatter.33
  1343.6 95.4 all-gather.37
  1442.4 90.4 all-gather.39
  1536.2 136.8 all-gather.41
  1676.4 128.0 all-gather.43
  1807.9 116.1 all-gather.25
  1987.3 23.4 all-reduce.39
  2095.0 24.5 all-reduce.41
  2204.0 24.5 all-reduce.43
  2312.8 24.5 all-reduce.45
  2421.9 24.5 all-reduce.47
  2494.5 22.1 all-gather.27
  2549.5 458.2 all-reduce.49
where the time goes:
time: 3410 us; the launch traced here: 3390 us
  blocking collectives  1620 us (48%)
  waiting for transfers between devices  695 us (20%)
  matrix products  525 us (15%)
  local copies, waits for them, and re-layouts  280 us (8%)
  starting transfers between devices  145 us (4%)
  other arithmetic  101 us (3%)
    unnamed x4, blocking collectives  1380 us
    dot_general x10, matrix products, exact_product(): return jnp.dot(left_side, right_side, precision=lax.Precision.HIGHEST)  246 us
    unnamed x235, local copies, waits for them, and re-layouts  177 us
    dot_general x5, matrix products, exact_gram(): lax.dot_general(matrix, matrix, (((1,), (1,)), ((), ())), precision=lax.P...  158 us
    unnamed x42, starting transfers between devices  143 us
    all_gather x1, waiting for transfers between devices, on_device(): lax.all_gather(outgoing[5], ('ctx', 'fsdp'), axis=0, tiled=True)  131 us
    unnamed x62, waiting for transfers between devices  130 us
    psum x5, waiting for transfers between devices, on_device(): gram_matrix = lax.psum(exact_gram(current), 'fsdp')  122 us
  transfers between devices with their start and end apart: 60, of which 21 were waited for; matrix products, arithmetic and copies ran while one was open for 48% of the time, Pallas kernels for 0%

commit v1 on v0

v1 whole, which is shorter than its diff:
```python
import functools
import math

import jax
import jax.numpy as jnp
from jax import lax
from jax.experimental import pallas as pl
from jax.experimental.pallas import tpu as pltpu
from jax.sharding import Mesh
from jax.sharding import PartitionSpec as P

HEAD_DIM = 64
NS_STEPS = 5
LINE = 4
VMEM_LIMIT = 56 * 1024 * 1024

theta_base = 1000000.0
norm_eps = 1e-06
ns_coeffs = (3.4445, -4.775, 2.0315)
momentum_decay = 0.95
muon_rate = 1.5
plain_rate = 2.0

EVERY = ("r", "z", "xy", "f")
CTX = ("r", "z", "xy")
PLANE = ("xy", "f")
CHIPS = 4

f32 = jnp.float32
bf16 = jnp.bfloat16


def rope_tables(positions):
    frequency = theta_base ** (-jnp.arange(0, HEAD_DIM, 2, dtype=f32) / HEAD_DIM)
    angles = positions.astype(f32)[:, None] * frequency[None, :]
    return (jnp.cos(angles), jnp.sin(angles))


def dot_nn(left_side, right_side):
    return jnp.dot(left_side, right_side, preferred_element_type=f32)


def dot_tn(left_side, right_side):
    return lax.dot_general(
        left_side, right_side, (((0,), (0,)), ((), ())), preferred_element_type=f32
    )


def dot_nt(left_side, right_side):
    return lax.dot_general(
        left_side, right_side, (((1,), (1,)), ((), ())), preferred_element_type=f32
    )


def after(value, event):
    return lax.optimization_barrier((value, event))[0]


def exchange(parts, axes):
    return lax.all_to_all(parts, axes, split_axis=0, concat_axis=0, tiled=True)


def total(parts):
    return jnp.sum(parts.astype(f32), axis=0)


def swap(piece, axis, step, keep=None):
    count = lax.axis_size(axis)
    pairs = [(i, i ^ step) for i in range(count) if keep is None or keep(i, i ^ step)]
    return lax.ppermute(piece, axis, pairs)


def plane_swap(piece, step, depths):
    count = lax.axis_size("xy")
    pairs = [(z * count + i, z * count + (i ^ step)) for z in depths for i in range(count)]
    return lax.ppermute(piece, ("z", "xy"), pairs)


def gather_plane(piece):
    chips = [piece] + [swap(piece, "xy", step) for step in range(1, CHIPS)]
    return chips + [swap(each, "f", 1) for each in chips]


def place(parts, index):
    return lax.dynamic_index_in_dim(parts, index, 0, keepdims=False)


def gather_ctx(piece):
    if lax.axis_size("r") > 1:
        piece = lax.all_gather(piece, "r", axis=0, tiled=False)
    else:
        piece = piece[None]
    piece = jnp.concatenate([piece] + [swap(piece, "z", step) for step in range(1, LINE)], axis=0)
    return [piece] + [swap(piece, "xy", step) for step in range(1, CHIPS)]


def reduce_ctx(parts):
    repeat = lax.axis_size("r")
    chips = parts[0].astype(f32)
    for step in range(1, CHIPS):
        chips += swap(parts[step], "xy", step).astype(f32)
    chips = chips.reshape((LINE, repeat) + chips.shape[1:])
    low = chips.astype(bf16)
    own = chips[0]
    for step in range(1, LINE):
        own += swap(low[step], "z", step).astype(f32)
    if repeat > 1:
        own = lax.psum_scatter(own, "r", scatter_dimension=0, tiled=True)
    return own[0]


def plain_call(kernel, out_shape, scratch=(), **keywords):
    return pl.pallas_call(
        kernel,
        out_shape=out_shape,
        scratch_shapes=list(scratch),
        compiler_params=pltpu.CompilerParams(vmem_limit_bytes=VMEM_LIMIT),
        **keywords,
    )


def cost(flops, moved):
    return pl.CostEstimate(flops=int(flops), bytes_accessed=int(moved), transcendentals=0)


def like(shape, dtype):
    return jax.ShapeDtypeStruct(shape, dtype)


def turn(values):
    lane = lax.broadcasted_iota(jnp.int32, values.shape, 1)
    low_half = lane % HEAD_DIM < HEAD_DIM // 2
    right = pltpu.roll(values, HEAD_DIM // 2, 1)
    left = pltpu.roll(values, 2 * HEAD_DIM - HEAD_DIM // 2, 1)
    return jnp.where(low_half, left, right)


def normed(values):
    rescale = lax.rsqrt(jnp.mean(values * values, axis=1, keepdims=True) + norm_eps)
    return values * rescale, rescale


def norm_back(grad_normed, plain, rescale, gain):
    inner = grad_normed * gain
    grad_in = rescale * (inner - plain * jnp.mean(inner * plain, axis=1, keepdims=True))
    return grad_in, jnp.sum(grad_normed * plain, axis=0, keepdims=True)


def front_kernel(x_ref, w_ref, small_ref, cos_ref, sin_ref, q_ref, pair_ref, h_ref):
    seqs, heads, rows, _ = q_ref.shape
    width = x_ref.shape[1]
    wide = w_ref.shape[1] - width
    plain, _ = normed(x_ref[...].astype(f32))
    low = (plain * small_ref[:, :width]).astype(bf16)
    h_ref[...] = low
    lin = dot_nn(low, w_ref[:, :wide]) + small_ref[:, 2 * width :]
    pair = 2 * HEAD_DIM
    cosine, sine = cos_ref[...], sin_ref[...]
    for j in range(heads // 2 + 1):
        both = lin[:, j * pair : (j + 1) * pair]
        both = (both * cosine + turn(both) * sine).astype(bf16)
        for b in range(seqs):
            span = slice(b * rows, (b + 1) * rows)
            for k in range(2):
                head = both[span, k * HEAD_DIM : (k + 1) * HEAD_DIM]
                if j < heads // 2:
                    q_ref[b, 2 * j + k] = head
                else:
                    start = wide - pair + k * HEAD_DIM
                    value = lin[span, start : start + HEAD_DIM].astype(bf16)
                    pair_ref[b, k] = jnp.concatenate([head, value], axis=1)


def middle_kernel(o_ref, x_ref, w_ref, small_ref, low_ref, x1_ref, h_ref):
    seqs, heads, rows, _ = o_ref.shape
    width = x_ref.shape[1]
    pair = 2 * HEAD_DIM
    for b in range(seqs):
        for j in range(heads // 2):
            both = jnp.concatenate([o_ref[b, 2 * j], o_ref[b, 2 * j + 1]], axis=1)
            low_ref[b * rows : (b + 1) * rows, j * pair : (j + 1) * pair] = both
    wide = w_ref.shape[1] - width
    residual = x_ref[...].astype(f32) + dot_nn(low_ref[...], w_ref[:, wide:])
    x1_ref[...] = residual
    plain, _ = normed(residual)
    h_ref[...] = (plain * small_ref[:, width : 2 * width]).astype(bf16)


def fold_kernel(a_ref, b_ref, own_ref, *low_refs):
    rows = own_ref.shape[0]
    own_ref[...] = a_ref[:rows].astype(f32) + b_ref[:rows].astype(f32)
    for step, ref in enumerate(low_refs, 1):
        span = slice(step * rows, (step + 1) * rows)
        ref[...] = (a_ref[span].astype(f32) + b_ref[span].astype(f32)).astype(bf16)


def fold(first, second):
    rows, width = first.shape
    rows //= CHIPS
    return plain_call(
        fold_kernel, [like((rows, width), f32)] + [like((rows, width), bf16)] * (CHIPS - 1)
    )(first, second)


def join_kernel(qa_ref, qb_ref, ka_ref, kb_ref, own_ref, *low_refs):
    rows, wide = qa_ref.shape[2:]
    for step, ref in enumerate((own_ref,) + low_refs):
        query = qa_ref[step].astype(f32) + qb_ref[step].astype(f32)
        other = ka_ref[step].astype(f32) + kb_ref[step].astype(f32)
        ref[:, :rows, :wide] = query.astype(ref.dtype)
        ref[:, rows:, :wide] = jnp.zeros(ref[:, rows:, :wide].shape, ref.dtype)
        ref[:, :, wide:] = other.astype(ref.dtype)


def join(query_first, query_second, other_first, other_second):
    depth, rows, wide = query_first.shape[1:]
    shape = (depth, rows + 1, wide + other_first.shape[3])
    return plain_call(join_kernel, [like(shape, f32)] + [like(shape, bf16)] * (CHIPS - 1))(
        query_first, query_second, other_first, other_second
    )


def spread_kernel(own_ref, a_ref, b_ref, c_ref, out_ref, *low_refs):
    repeat = out_ref.shape[0]
    for step, ref in enumerate((out_ref,) + low_refs):
        for r in range(repeat):
            q = r * LINE + step
            value = own_ref[q] + a_ref[q].astype(f32) + b_ref[q].astype(f32) + c_ref[q].astype(f32)
            ref[r] = value.astype(ref.dtype)


def spread(own, arrived, repeat):
    shape = (repeat,) + own.shape[1:]
    return plain_call(spread_kernel, [like(shape, f32)] + [like(shape, bf16)] * (LINE - 1))(
        own, *arrived
    )


def step_kernel(core_ref, own_ref, a_ref, b_ref, c_ref, *refs):
    moments, grads, fresh_refs = refs[:4], refs[4:8], refs[8:12]
    small_ref, mine_ref, other_ref = refs[12:]
    rows = moments[0].shape[0]
    total_sum = own_ref[0] + a_ref[0].astype(f32) + b_ref[0].astype(f32) + c_ref[0].astype(f32)
    width = moments[0].shape[1]
    narrow = moments[1].shape[1]
    starts = (0, 2 * width, 2 * width + narrow, width)
    small_ref[...] = total_sum[rows:, 2 * width :]
    updates = []
    for m_ref, g_ref, n_ref, start in zip(moments, grads, fresh_refs, starts):
        grad = total_sum[:rows, start : start + m_ref.shape[1]]
        fresh = momentum_decay * m_ref[...] + grad
        g_ref[...] = grad
        n_ref[...] = fresh
        updates.append((grad + momentum_decay * fresh).astype(bf16))
    query, key, value, out = updates
    first = jnp.concatenate([query, key], axis=1)
    second = jnp.concatenate([out, value], axis=1)

    @pl.when(core_ref[0] == 0)
    def _():
        mine_ref[...] = first
        other_ref[...] = second

    @pl.when(core_ref[0] != 0)
    def _():
        mine_ref[...] = second
        other_ref[...] = first


def step_of(core, own, arrived, moments):
    rows = moments[0].shape[0]
    shapes = [like(m.shape, f32) for m in moments]
    pair_width = moments[0].shape[1] + moments[1].shape[1]
    vmem = pl.BlockSpec(memory_space=pltpu.VMEM)
    outs = plain_call(
        step_kernel,
        shapes
        + shapes
        + [like((1, 2 * moments[1].shape[1]), f32)]
        + [like((rows, pair_width), bf16)] * 2,
        in_specs=[pl.BlockSpec(memory_space=pltpu.SMEM)] + [vmem] * 8,
    )(core, own, *arrived, *moments)
    return outs[:4], outs[4:8], outs[8], outs[9], outs[10]


def turnback_kernel(
    own_ref, a_ref, b_ref, c_ref, x1_ref, dy_ref, w_ref, small_ref, dx_ref, da_ref, do_ref, gain_ref
):
    seqs, heads, rows, _ = do_ref.shape
    width = x1_ref.shape[1]
    wide = w_ref.shape[1] - width
    grad = own_ref[...] + a_ref[...].astype(f32) + b_ref[...].astype(f32) + c_ref[...].astype(f32)
    plain, rescale = normed(x1_ref[...])
    grad_in, grad_gain = norm_back(grad, plain, rescale, small_ref[:, width : 2 * width])
    gain_ref[...] = grad_gain
    grad_residual = dy_ref[...].astype(f32) + grad_in
    dx_ref[...] = grad_residual
    low = grad_residual.astype(bf16)
    da_ref[...] = low
    mixed = dot_nt(low, w_ref[:, wide:]).astype(bf16)
    for b in range(seqs):
        for j in range(heads):
            start = j * HEAD_DIM
            do_ref[b, j] = mixed[b * rows : (b + 1) * rows, start : start + HEAD_DIM]


def shard_rows(here_ref, refs, value, rows, column, first):
    chips, depth = refs[0].shape[:2]
    cores = len(refs)
    core, chip, line = here_ref[0], here_ref[1], here_ref[2]
    for k in range(cores):
        for target, ref in enumerate(refs):

            @pl.when((core ^ k) == target)
            def _():
                for q in range(depth):
                    for c in range(chips):
                        start = ((q * chips + c) * cores + k) * rows
                        at = (q // LINE) * LINE + ((q % LINE) ^ line)
                        piece = value[start : start + rows] if first else value(start // rows)
                        span = slice(0, rows) if first else slice(ref.shape[2] - 1, ref.shape[2])
                        ref[c ^ chip, at, span, column : column + piece.shape[1]] = piece


def query_kernel(
    here_ref, h_ref, dq_ref, o_ref, da_ref, cos_ref, sin_ref, lin_ref, own_ref, other_ref
):
    seqs, heads, rows, _ = dq_ref.shape
    width = h_ref.shape[1]
    pair = 2 * HEAD_DIM
    for b in range(seqs):
        span = slice(b * rows, (b + 1) * rows)
        cosine, sine = cos_ref[span], sin_ref[span]
        for j in range(heads // 2):
            both = jnp.concatenate([dq_ref[b, 2 * j], dq_ref[b, 2 * j + 1]], axis=1)
            both = both * cosine - turn(both) * sine
            lin_ref[span, j * pair : (j + 1) * pair] = both.astype(bf16)
    rows = own_ref.shape[2]
    query = dot_tn(h_ref[...], lin_ref[...]).astype(bf16)
    shard_rows(here_ref, (own_ref, other_ref), query, rows, 0, True)
    out = dot_tn(o_ref[...], da_ref[...]).astype(bf16)
    shard_rows(here_ref, (own_ref, other_ref), out, rows, width, True)


def back_kernel(
    here_ref,
    pair_ref,
    lin_ref,
    h_ref,
    x_ref,
    dx_ref,
    w_ref,
    small_ref,
    cos_ref,
    sin_ref,
    gain_ref,
    out_ref,
    own_ref,
    other_ref,
    all_lin,
    all_small,
):
    seqs, kv_heads, rows, pair = pair_ref.shape
    width = x_ref.shape[1]
    wide = w_ref.shape[1] - width
    all_lin[:, :width] = lin_ref[...]
    for b in range(seqs):
        span = slice(b * rows, (b + 1) * rows)
        first, second = pair_ref[b, 0], pair_ref[b, 1]
        keys = jnp.concatenate([first[:, :HEAD_DIM], second[:, :HEAD_DIM]], axis=1)
        values = jnp.concatenate([first[:, HEAD_DIM:], second[:, HEAD_DIM:]], axis=1)
        keys = keys * cos_ref[span] - turn(keys) * sin_ref[span]
        all_lin[span, width : width + pair] = keys.astype(bf16)
        all_lin[span, width + pair :] = values.astype(bf16)
    lin = all_lin[...]
    grad = dot_nt(lin, w_ref[:, :wide])
    plain, rescale = normed(x_ref[...].astype(f32))
    grad_in, grad_gain = norm_back(grad, plain, rescale, small_ref[:, :width])
    out_ref[...] = dx_ref[...] + grad_in
    all_small[:, :width] = grad_gain
    all_small[:, width : 2 * width] = gain_ref[...]
    all_small[:, 2 * width :] = jnp.sum(lin.astype(f32), axis=0, keepdims=True)
    refs = (own_ref, other_ref)
    chips, depth, rows, _ = own_ref.shape
    for ref in refs:
        ref[...] = jnp.zeros_like(ref)
    grads = dot_tn(h_ref[...], lin[:, width:]).astype(bf16)
    shard_rows(here_ref, refs, grads, rows - 1, 0, True)
    small_rows = all_small.shape[1] // (2 * chips * depth)

    def small_of(number):
        return all_small[:, number * small_rows : (number + 1) * small_rows].astype(bf16)

    shard_rows(here_ref, refs, small_of, 1, 0, False)


def softmax_keys(keys, queries, key_pos, query_pos):
    scores = dot_nt(keys, queries) * (HEAD_DIM ** (-0.5))
    masked = jnp.where(key_pos <= query_pos, scores, -1e30)
    terms = jnp.exp(masked - jnp.max(masked, axis=0, keepdims=True))
    return terms * (1.0 / jnp.sum(terms, axis=0, keepdims=True))


def joined_pairs(refs):
    return jnp.concatenate([ref[...].reshape(-1, ref.shape[-1]) for ref in refs], axis=0)


def attend_kernel(q_ref, *refs):
    kv_refs, (kpos_ref, qpos_ref, o_ref) = refs[:CHIPS], refs[CHIPS:]
    group, rows, width = q_ref.shape[1:]
    queries = q_ref[...].reshape(group * rows, width)
    pairs = joined_pairs(kv_refs)
    probs = softmax_keys(pairs[:, :width], queries, kpos_ref[...], qpos_ref[...]).astype(bf16)
    mixed = dot_nn(pairs.T[width:], probs)
    o_ref[...] = mixed.T.reshape(1, group, rows, width).astype(bf16)


def attend_back_kernel(q_ref, do_ref, *refs):
    kv_refs, (kpos_ref, qpos_ref, dq_ref), dkv_refs = (
        refs[:CHIPS],
        refs[CHIPS : CHIPS + 3],
        refs[CHIPS + 3 :],
    )
    group, rows, width = q_ref.shape[1:]
    queries = q_ref[...].reshape(group * rows, width)
    grads = do_ref[...].reshape(group * rows, width)
    pairs = joined_pairs(kv_refs)
    probs = softmax_keys(pairs[:, :width], queries, kpos_ref[...], qpos_ref[...])
    grad_probs = dot_nt(pairs[:, width:], grads)
    delta = jnp.sum(probs * grad_probs, axis=0, keepdims=True)
    grad_scores = (probs * (grad_probs - delta)).astype(bf16)
    scale = HEAD_DIM ** (-0.5)
    grad_keys = dot_nn(grad_scores, queries) * scale
    grad_values = dot_nn(probs.astype(bf16), grads)
    both = jnp.concatenate([grad_keys, grad_values], axis=1).astype(bf16)
    span = both.shape[0] // CHIPS
    for number, ref in enumerate(dkv_refs):
        ref[...] = both[number * span : (number + 1) * span].reshape(ref.shape)
    grad_queries = dot_nn(pairs.T[:width], grad_scores) * scale
    dq_ref[...] = grad_queries.T.reshape(dq_ref.shape)


def attention_specs(queries, pairs):
    _, heads, rows, _ = queries.shape
    chunks, _, kv_heads = pairs.shape[:3]
    group = heads // kv_heads
    length = CHIPS * chunks * rows
    q_spec = pl.BlockSpec((1, group, rows, HEAD_DIM), lambda b, h: (b, h, 0, 0))
    kv_spec = pl.BlockSpec((chunks, 1, 1, rows, 2 * HEAD_DIM), lambda b, h: (0, b, h, 0, 0))
    kpos_spec = pl.BlockSpec((length, 1), lambda b, h: (0, 0))
    qpos_spec = pl.BlockSpec((1, group * rows), lambda b, h: (0, 0))
    return q_spec, kv_spec, kpos_spec, qpos_spec


def attend(queries, pairs, key_pos, query_pos):
    q_spec, kv_spec, kpos_spec, qpos_spec = attention_specs(queries, pairs[0])
    scores = queries.shape[0] * queries.shape[1] * queries.shape[2] * key_pos.shape[0]
    return plain_call(
        attend_kernel,
        like(queries.shape, bf16),
        grid=(queries.shape[0], pairs[0].shape[2]),
        in_specs=[q_spec] + [kv_spec] * CHIPS + [kpos_spec, qpos_spec],
        out_specs=q_spec,
        cost_estimate=cost(scores * 16 * HEAD_DIM, scores * 8),
    )(queries, *pairs, key_pos, query_pos)


def attend_back(queries, grads, pairs, key_pos, query_pos):
    q_spec, kv_spec, kpos_spec, qpos_spec = attention_specs(queries, pairs[0])
    scores = queries.shape[0] * queries.shape[1] * queries.shape[2] * key_pos.shape[0]
    outs = plain_call(
        attend_back_kernel,
        [like(queries.shape, f32)] + [like(pairs[0].shape, bf16)] * CHIPS,
        grid=(queries.shape[0], pairs[0].shape[2]),
        in_specs=[q_spec, q_spec] + [kv_spec] * CHIPS + [kpos_spec, qpos_spec],
        out_specs=[q_spec] + [kv_spec] * CHIPS,
        cost_estimate=cost(scores * 40 * HEAD_DIM, scores * 12),
    )(queries, grads, *pairs, key_pos, query_pos)
    return outs[0], outs[1:]


def feed_kernel(count, *refs):
    h_refs, (order_ref, dy_ref, wgu_ref, wd_ref) = refs[:count], refs[count : count + 4]
    y_refs = refs[count + 4 : count + 6]
    dh_refs = refs[count + 6 : count + 8]
    gg_ref, gu_ref, gd_ref, agu, ad, h_all, dy_all, sems = refs[count + 8 :]
    step = pl.program_id(0)
    rows = h_refs[0].shape[0]
    tile = y_refs[0].shape[0]
    each = tile // rows

    def copies(number):
        span = pl.ds(number * rows, rows)
        return (
            pltpu.make_async_copy(h_refs[number], h_all.at[span], sems.at[0, number]),
            pltpu.make_async_copy(dy_ref.at[order_ref[number]], dy_all.at[span], sems.at[1, number]),
        )

    @pl.when(step == 0)
    def _():
        for number in range(count):
            for copy in copies(number):
                copy.start()
        agu[...] = jnp.zeros_like(agu)
        ad[...] = jnp.zeros_like(ad)

    for number in range(count):

        @pl.when(step == number // each)
        def _():
            for copy in copies(number):
                copy.wait()

    start = pl.multiple_of(step * tile, tile)
    normed_rows = h_all[pl.ds(start, tile)]
    grads = dy_all[pl.ds(start, tile)]
    units = wgu_ref.shape[3]
    gate_mat = wgu_ref[:, 0].reshape(-1, units)
    up_mat = wgu_ref[:, 1].reshape(-1, units)
    gate = dot_nn(normed_rows, gate_mat)
    up = dot_nn(normed_rows, up_mat)
    sigmoid = 1.0 / (1.0 + jnp.exp(-gate))
    silu = gate * sigmoid
    hidden = (silu * up).astype(bf16)
    grad_hidden = dot_nt(grads, wd_ref[...])
    grad_gate = (grad_hidden * up * sigmoid * (1.0 + gate * (1.0 - sigmoid))).astype(bf16)
    grad_up = (grad_hidden * silu).astype(bf16)
    dh = (dot_nt(grad_gate, gate_mat) + dot_nt(grad_up, up_mat)).astype(bf16)
    y = dot_nn(hidden, wd_ref[...]).astype(bf16)
    for core in range(2):

        @pl.when(step // (pl.num_programs(0) // 2) == core)
        def _():
            y_refs[core][...] = y
            dh_refs[core][...] = dh

    agu[0] += dot_tn(normed_rows, grad_gate)
    agu[1] += dot_tn(normed_rows, grad_up)
    ad[...] += dot_tn(hidden, grads)

    @pl.when(step == pl.num_programs(0) - 1)
    def _():
        gg_ref[...] = agu[0].astype(bf16)
        gu_ref[...] = agu[1].astype(bf16)
        gd_ref[...] = ad[...].astype(bf16)


def feed_forward(normed_rows, order, grads, gate_up, down_mat):
    count = len(normed_rows)
    rows, width = normed_rows[0].shape
    units = gate_up.shape[3]
    tokens = count * rows
    tile = CHIPS * rows
    steps = count // CHIPS
    half = tokens // 2
    first = pl.BlockSpec((tile, width), lambda t: (jnp.minimum(t, steps // 2 - 1), 0))
    second = pl.BlockSpec((tile, width), lambda t: (jnp.maximum(t - steps // 2, 0), 0))
    weights = pl.BlockSpec(gate_up.shape, lambda t: (0, 0, 0, 0))
    wide = pl.BlockSpec((width, units), lambda t: (0, 0))
    tall = pl.BlockSpec((units, width), lambda t: (0, 0))
    anywhere = pl.BlockSpec(memory_space=pl.ANY)
    outs = plain_call(
        functools.partial(feed_kernel, count),
        [like((half, width), bf16)] * 4
        + [like((width, units), bf16)] * 2
        + [like((units, width), bf16)],
        [
            pltpu.VMEM((2, width, units), f32),
            pltpu.VMEM((units, width), f32),
            pltpu.VMEM((tokens, width), bf16),
            pltpu.VMEM((tokens, width), bf16),
            pltpu.SemaphoreType.DMA((2, count)),
        ],
        grid=(steps,),
        in_specs=[anywhere] * count
        + [pl.BlockSpec(memory_space=pltpu.SMEM), anywhere, weights, tall],
        out_specs=[first, second, first, second, wide, wide, tall],
        cost_estimate=cost(36 * tokens * width * units, 8 * tokens * width + 12 * units * width),
    )(*normed_rows, order, grads, gate_up, down_mat)
    return outs[:2], outs[2:4], outs[4:]


def update_kernel(span, in_ref, mg_ref, mu_ref, gg_ref, gu_ref, ng_ref, nu_ref, u_ref):
    plane, _, _, units = in_ref.shape
    depth = units // span
    triples = ((mg_ref, gg_ref, ng_ref), (mu_ref, gu_ref, nu_ref))
    for which, (m_ref, g_ref, n_ref) in enumerate(triples):
        for q in range(depth):
            for p in range(plane):
                start = (q * plane + p) * span
                piece = in_ref[p, which, :, q * span : (q + 1) * span]
                g_ref[:, start : start + span] = piece.astype(f32)
        grad = g_ref[...]
        fresh = momentum_decay * m_ref[...] + grad
        n_ref[...] = fresh
        u_ref[which] = (grad + momentum_decay * fresh).astype(bf16)


def wide_update(arrived, moment_gate, moment_up, span):
    rows, columns = moment_gate.shape
    return plain_call(
        functools.partial(update_kernel, span),
        [like((rows, columns), f32)] * 4 + [like((2, rows, columns), bf16)],
    )(arrived, moment_gate, moment_up)


def row_spans(size):
    first = size % 256
    bounds = ([0, first] if first else [0]) + list(range(first + 256, size + 1, 256))
    return list(zip(bounds[:-1], bounds[1:]))


def poly_scratch(count, size):
    return [pltpu.VMEM((count, size, size), bf16)] * 6 + [pltpu.VMEM((2, count, size, size), bf16)] * 2


def poly_core(count, size, load, write, scratch):
    a_hi, a_lo, p_hi, p_lo, t_hi, t_lo, q_hi, q_lo = scratch
    alpha_term, beta_term, gamma_term = ns_coeffs
    spans = row_spans(size)

    def eye_of(start, stop):
        row = lax.broadcasted_iota(jnp.int32, (stop - start, size - start), 0)
        col = lax.broadcasted_iota(jnp.int32, (stop - start, size - start), 1)
        return row == col

    def store(high, low, i, start, stop, value):
        rounded = value.astype(bf16)
        rest = (value - rounded.astype(f32)).astype(bf16)
        high[i, start:stop, start:] = rounded
        low[i, start:stop, start:] = rest
        if stop < size:
            turned = value[:, stop - start :].T
            rounded = turned.astype(bf16)
            high[i, stop:, start:stop] = rounded
            low[i, stop:, start:stop] = (turned - rounded.astype(f32)).astype(bf16)

    def product(left, right, i, start, stop):
        left_hi, left_lo = left[0][i, start:stop, :], left[1][i, start:stop, :]
        right_hi, right_lo = right[0][i, :, start:], right[1][i, :, start:]
        return (
            dot_nn(left_hi, right_lo) + dot_nn(left_lo, right_hi) + dot_nn(left_hi, right_hi)
        )

    grams = (a_hi, a_lo)
    poly = (p_hi, p_lo)
    once = (t_hi, t_lo)
    inverses = []
    for i in range(count):
        squares = jnp.zeros((1, 1), f32)
        for start, stop in spans:
            diagonal = jnp.where(eye_of(start, stop), load(i, start, stop), 0.0)
            squares += jnp.sum(jnp.sum(diagonal, axis=1, keepdims=True), axis=0, keepdims=True)
        inverse = 1.0 / (jnp.sqrt(squares) + 1e-07)
        inverses.append(inverse)
        for start, stop in spans:
            store(*grams, i, start, stop, load(i, start, stop) * (inverse * inverse))

    for sweep in range(NS_STEPS):
        now, later = sweep % 2, (sweep + 1) % 2
        old = (q_hi.at[later], q_lo.at[later])
        new = (q_hi.at[now], q_lo.at[now])
        for start, stop in spans:
            for i in range(count):
                value = gamma_term * product(grams, grams, i, start, stop)
                mine = a_hi[i, start:stop, start:].astype(f32)
                mine += a_lo[i, start:stop, start:].astype(f32)
                value += beta_term * mine
                value += jnp.where(eye_of(start, stop), alpha_term, 0.0)
                store(*poly, i, start, stop, value)
                if sweep == 0:
                    store(*new, i, start, stop, value * inverses[i])
        last = sweep == NS_STEPS - 1
        if sweep > 0:
            for start, stop in spans:
                for i in range(count):
                    value = product(old, poly, i, start, stop)
                    if not last:
                        store(*new, i, start, stop, value)
                    else:
                        write(i, slice(start, stop), slice(start, size), value)
                        if stop < size:
                            turned = value[:, stop - start :].T
                            write(i, slice(stop, size), slice(start, stop), turned)
        if not last:
            for left, target in ((grams, once), (once, grams)):
                for start, stop in spans:
                    for i in range(count):
                        store(*target, i, start, stop, product(left, poly, i, start, stop))


def load_blocks(refs, target, sem):
    rows = refs[0].shape[0]
    return [
        pltpu.make_async_copy(ref, target.at[pl.ds(number * rows, rows)], sem.at[number])
        for number, ref in enumerate(refs)
    ]


def gram_kernel(mode_ref, *refs):
    groups = [refs[:CHIPS], refs[CHIPS : 2 * CHIPS], refs[2 * CHIPS : 3 * CHIPS]]
    out_ref, narrow_ref, *scratch, sem = refs[3 * CHIPS :]
    spans = row_spans(out_ref.shape[0])
    for number, (group, whole) in enumerate(zip(groups, scratch)):

        @pl.when(mode_ref[0] == number)
        def _():
            copies = load_blocks(group, whole, sem)
            for copy in copies:
                copy.start()
            for copy in copies:
                copy.wait()
            for start, stop in spans:
                if number == 1:
                    block = dot_tn(whole[:, start:stop], whole[:, start:])
                elif number == 0:
                    block = dot_nt(whole[start:stop], whole[start:])
                else:
                    size = out_ref.shape[0]
                    block = dot_nt(whole[start:stop, :size], whole[start:, :size])
                out_ref[start:stop, start:] = block
            if number == 2:
                narrow = whole[:, out_ref.shape[0] :]
                narrow_ref[...] = dot_tn(narrow, narrow)


def gram_of(mode, wide, tall, square):
    size = tall[0].shape[1]
    narrow = square[0].shape[1] - size
    spec = [pl.BlockSpec(memory_space=pltpu.SMEM)]
    spec += [pl.BlockSpec(memory_space=pl.ANY)] * (3 * CHIPS)
    groups = (wide, tall, square)
    scratch = [
        pltpu.VMEM((CHIPS * group[0].shape[0], group[0].shape[1]), bf16) for group in groups
    ]
    return plain_call(
        gram_kernel,
        [like((size, size), f32), like((narrow, narrow), f32)],
        scratch + [pltpu.SemaphoreType.DMA((CHIPS,))],
        in_specs=spec,
        cost_estimate=cost(4 * size * size * size * 3, 8 * size * size),
    )(mode, *wide, *tall, *square)


def ortho_kernel(mode_ref, a_ref, b_ref, n_ref, *refs):
    wide, tall, square = refs[:CHIPS], refs[CHIPS : CHIPS + 1], refs[CHIPS + 1 : 2 * CHIPS + 1]
    outs = refs[2 * CHIPS + 1 : 2 * CHIPS + 4]
    q_ref, k_ref, *wholes, sem = refs[2 * CHIPS + 4 : 2 * CHIPS + 10]
    scratch = refs[2 * CHIPS + 10 : 2 * CHIPS + 18]
    narrow_scratch = refs[2 * CHIPS + 18 :]
    groups = (wide, tall, square)
    for number, (group, whole) in enumerate(zip(groups, wholes)):

        @pl.when(mode_ref[0] == number)
        def _():
            for copy in load_blocks(group, whole, sem):
                copy.start()

    def load(i, start, stop):
        return a_ref[start:stop, start:] + b_ref[start:stop, start:]

    def write(i, rows, columns, value):
        q_ref[rows, columns] = value.astype(bf16)

    size = a_ref.shape[0]
    poly_core(1, size, load, write, scratch)

    @pl.when(mode_ref[0] == 2)
    def _():
        def narrow_load(i, start, stop):
            return n_ref[start:stop, start:]

        def narrow_write(i, rows, columns, value):
            k_ref[rows, columns] = value.astype(bf16)

        poly_core(1, n_ref.shape[0], narrow_load, narrow_write, narrow_scratch)

    for number, (group, whole, out_ref) in enumerate(zip(groups, wholes, outs)):

        @pl.when(mode_ref[0] == number)
        def _():
            for copy in load_blocks(group, whole, sem):
                copy.wait()
            if number == 1:
                out_ref[...] = dot_nn(whole[...], q_ref[...]).astype(bf16)
            elif number == 0:
                rows = q_ref[: out_ref.shape[0], :]
                out_ref[...] = dot_nn(rows, whole[...]).astype(bf16)
            else:
                count = out_ref.shape[0]
                rows = q_ref[:count, :]
                out_ref[:, :size] = dot_nn(rows, whole[:, :size]).astype(bf16)
                out_ref[:, size:] = dot_nn(whole[:count, size:], k_ref[...]).astype(bf16)


def ortho_of(mode, gram, other, narrow, wide, tall, square):
    size = gram.shape[0]
    vmem = pl.BlockSpec(memory_space=pltpu.VMEM)
    spec = [pl.BlockSpec(memory_space=pltpu.SMEM), vmem, vmem, vmem]
    spec += [pl.BlockSpec(memory_space=pl.ANY)] * (2 * CHIPS + 1)
    return plain_call(
        ortho_kernel,
        [like(wide[0].shape, bf16), like(tall.shape, bf16), like(square[0].shape, bf16)],
        [
            pltpu.VMEM((size, size), bf16),
            pltpu.VMEM(narrow.shape, bf16),
            pltpu.VMEM((size, wide[0].shape[1]), bf16),
            pltpu.VMEM(tall.shape, bf16),
            pltpu.VMEM((size, square[0].shape[1]), bf16),
            pltpu.SemaphoreType.DMA((CHIPS,)),
        ]
        + poly_scratch(1, size)
        + poly_scratch(1, narrow.shape[0]),
        in_specs=spec,
        cost_estimate=cost(100 * size * size * size, 8 * size * size),
    )(mode, gram, other, narrow, *wide, tall, *square)


def on_device(
    tokens_in,
    cotangent,
    block_order,
    weight_query,
    weight_key,
    weight_value,
    weight_out,
    weight_gate,
    weight_up,
    weight_down,
    moment_query,
    moment_key,
    moment_value,
    moment_out,
    moment_gate,
    moment_up,
    moment_down,
    small_params,
):
    repeat = lax.axis_size("r")
    cores = lax.axis_size("f")
    plane = CHIPS * cores
    ctx_count = repeat * LINE * CHIPS
    device_count = ctx_count * cores
    depth_count = repeat * LINE
    r_index = lax.axis_index("r")
    z_index = lax.axis_index("z")
    xy_index = lax.axis_index("xy")
    f_index = lax.axis_index("f")
    ctx_index = (r_index * LINE + z_index) * CHIPS + xy_index

    seq_count, seq_rows, width = tokens_in.shape
    seq_length = seq_rows * ctx_count
    block_rows = seq_rows // 2
    all_tokens = seq_count * cores * seq_length
    row_count = seq_count * seq_rows
    kv_width = weight_key.shape[1]
    head_count = width // HEAD_DIM
    kv_count = kv_width // HEAD_DIM
    group = head_count // kv_count
    part_rows = weight_query.shape[0]
    hidden_width = weight_gate.shape[1]
    down_rows = weight_down.shape[0]
    units = depth_count * down_rows
    small_rows = small_params.shape[0]
    both_width = 2 * (width + kv_width)

    front = jnp.concatenate([weight_query, weight_key, weight_value, weight_out], axis=1)
    small_line = jnp.pad(small_params, (0, both_width - small_rows))[None, :]
    front = jnp.concatenate([front, small_line], axis=0).astype(bf16)
    front_all = lax.all_gather(front, EVERY, axis=0, tiled=False)

    def by_unit(weight):
        return weight.astype(bf16).reshape(part_rows, depth_count, plane, down_rows)

    gate_up = jnp.stack([by_unit(weight_gate), by_unit(weight_up)], axis=0)
    gate_up = gate_up.transpose(3, 0, 1, 2, 4).reshape(plane, 2, part_rows, units)
    gate_up = exchange(gate_up, PLANE)
    front_all, gate_up = lax.optimization_barrier((front_all, gate_up))
    gate_up = gate_up.transpose(1, 0, 2, 3).reshape(2, plane * part_rows, units)
    unit_rows = gate_up
    gate_up = lax.all_gather(gate_up, ("r", "z"), axis=0, tiled=False)
    if repeat > 1:
        gate_up = gate_up.transpose(1, 0, 2, 3).reshape(1, 2, width, units)
    down_mat = lax.all_gather(weight_down.astype(bf16), ("r", "z"), axis=0, tiled=True)

    attn_mats = front_all[:, :part_rows, :].reshape(width, both_width)
    small_vals = front_all[:, part_rows, :small_rows].reshape(1, -1).astype(f32)

    stored = jnp.arange(block_rows, dtype=jnp.int32)
    places = jnp.arange(ctx_count, dtype=jnp.int32)
    xy_places = xy_index ^ (places // (LINE * repeat))
    z_places = z_index ^ (places // repeat % LINE)
    places = ((places % repeat) * LINE + z_places) * CHIPS + xy_places
    blocks = block_order.reshape(ctx_count, 2)[places].reshape(2 * ctx_count)
    key_pos = (blocks[:, None] * block_rows + stored[None, :]).reshape(seq_length, 1)
    own_blocks = lax.dynamic_slice_in_dim(block_order, 2 * ctx_index, 2)
    query_pos = (own_blocks[:, None] * block_rows + stored[None, :]).reshape(seq_rows)
    cosine, sine = rope_tables(query_pos)
    cosine = jnp.tile(cosine, (seq_count, 4))
    sine = jnp.tile(jnp.concatenate([-sine, sine], axis=1), (seq_count, 2))
    query_pos = jnp.tile(query_pos, group)[None, :]
    front_all, key_pos, query_pos, cosine, sine = lax.optimization_barrier(
        (front_all, key_pos, query_pos, cosine, sine)
    )

    inputs = tokens_in.reshape(row_count, width)
    grad_low = cotangent.reshape(row_count, width)
    grads_plane = lax.all_gather(after(grad_low, unit_rows), PLANE, axis=0, tiled=False)
    heads_shape = (seq_count, head_count, seq_rows, HEAD_DIM)
    pairs_shape = (seq_count, kv_count, seq_rows, 2 * HEAD_DIM)
    rows_shape = (row_count, width)
    queries, pairs, normed_one = plain_call(
        front_kernel,
        [like(heads_shape, bf16), like(pairs_shape, bf16), like(rows_shape, bf16)],
        cost_estimate=cost(6 * row_count * width * both_width, 8 * width * width),
    )(inputs, attn_mats, small_vals, cosine, sine)
    pairs_all = gather_ctx(pairs)
    mixed = attend(queries, pairs_all, key_pos, query_pos)
    attn_low, residual, normed_two = plain_call(
        middle_kernel,
        [like(rows_shape, bf16), like(rows_shape, f32), like(rows_shape, bf16)],
        cost_estimate=cost(6 * row_count * width * width, 8 * width * width),
    )(mixed, inputs, attn_mats, small_vals)
    normed_plane = gather_plane(normed_two)

    cores_here = [f_index ^ (number // CHIPS) for number in range(plane)]
    chips_here = [xy_index ^ (number % CHIPS) for number in range(plane)]
    order = jnp.stack([chip * cores + core for chip, core in zip(chips_here, cores_here)])
    part_y, part_dh, feed_grads = feed_forward(
        normed_plane, order, grads_plane, gate_up, down_mat
    )
    own_dh, *low_dh = fold(part_dh[0], swap(part_dh[1], "f", 1))
    arrived = [swap(piece, "xy", step) for step, piece in enumerate(low_dh, 1)]

    def by_line(part):
        part = part.reshape((repeat, LINE, -1) + part.shape[1:])
        return part.transpose(1, 0, 2, 3)

    line_gate = exchange(by_line(after(feed_grads[0], own_dh)), "z")
    arrived, line_gate = lax.optimization_barrier((arrived, line_gate))
    line_up = exchange(by_line(after(feed_grads[1], line_gate)), "z")
    grad_residual, grad_attn, grad_mixed, grad_gain_two = plain_call(
        turnback_kernel,
        [like(rows_shape, f32), like(rows_shape, bf16), like(heads_shape, bf16), like((1, width), f32)],
        cost_estimate=cost(6 * row_count * width * width, 8 * width * width),
    )(own_dh, *arrived, residual, grad_low, attn_mats, small_vals)
    grad_queries, part_pairs = attend_back(queries, grad_mixed, pairs_all, key_pos, query_pos)
    grad_queries, line_up = lax.optimization_barrier((grad_queries, line_up))
    line_down = exchange(by_line(after(feed_grads[2], line_up)), "z")

    here = jnp.stack([f_index, xy_index, z_index])
    vmem = pl.BlockSpec(memory_space=pltpu.VMEM)
    smem = pl.BlockSpec(memory_space=pltpu.SMEM)
    part_shape = (CHIPS, depth_count, part_rows, 2 * width)
    grad_query_lin, query_own, query_other = plain_call(
        query_kernel,
        [like(rows_shape, bf16), like(part_shape, bf16), like(part_shape, bf16)],
        in_specs=[smem] + [vmem] * 6,
        cost_estimate=cost(12 * row_count * width * width, 8 * width * width),
    )(here, normed_one, grad_queries, attn_low, grad_attn, cosine, sine)
    query_other = swap(query_other, "f", 1)

    part_gu = jnp.stack([total(line_gate), total(line_up)], axis=1)
    if repeat > 1:
        part_gu = lax.psum_scatter(part_gu, "r", scatter_dimension=0, tiled=True)
    part_gu = part_gu.astype(bf16).reshape(2, plane, part_rows, units).transpose(1, 0, 2, 3)
    sum_gate, sum_up, fresh_gate, fresh_up, wide_updates = wide_update(
        exchange(part_gu, PLANE), moment_gate, moment_up, down_rows
    )

    own_pairs, line_down = lax.optimization_barrier((reduce_ctx(part_pairs), line_down))
    part_shape = (CHIPS, depth_count, part_rows + 1, 2 * kv_width)
    input_grad, other_own, other_other = plain_call(
        back_kernel,
        [like(rows_shape, f32), like(part_shape, bf16), like(part_shape, bf16)],
        [
            pltpu.VMEM((row_count, width + 2 * kv_width), bf16),
            pltpu.VMEM((1, small_vals.shape[1]), f32),
        ],
        in_specs=[smem] + [vmem] * 10,
        cost_estimate=cost(6 * row_count * width * width, 8 * width * width),
    )(
        here,
        own_pairs,
        grad_query_lin,
        normed_one,
        inputs,
        grad_residual,
        attn_mats,
        small_vals,
        cosine,
        sine,
        grad_gain_two,
    )
    input_grad = input_grad.reshape(seq_count, seq_rows, width)
    own_sum, *low_sums = join(query_own, query_other, other_own, swap(other_other, "f", 1))
    low_sums = [swap(piece, "xy", step) for step, piece in enumerate(low_sums, 1)]
    own_sum, *low_sums = spread(own_sum, low_sums, repeat)
    low_sums = [swap(piece, "z", step) for step, piece in enumerate(low_sums, 1)]
    if repeat > 1:
        for piece in low_sums:
            own_sum += piece.astype(f32)
        own_sum = lax.psum_scatter(own_sum, "r", scatter_dimension=0, tiled=True)
        low_sums = [jnp.zeros(own_sum.shape, bf16)] * (LINE - 1)
    attn_sums, attn_fresh, small_line, mine, other = step_of(
        f_index.reshape(1),
        own_sum,
        low_sums,
        (moment_query, moment_key, moment_value, moment_out),
    )
    sum_small = small_line[0, :small_rows]

    sum_down = total(line_down)
    if repeat > 1:
        sum_down = lax.psum_scatter(sum_down, "r", scatter_dimension=0, tiled=True)
    sum_down = sum_down.reshape(down_rows, width)
    fresh_down = momentum_decay * moment_down + sum_down
    update_down = (sum_down + momentum_decay * fresh_down).astype(bf16)

    masters = (
        weight_query,
        weight_key,
        weight_value,
        weight_out,
        weight_gate,
        weight_up,
        weight_down,
    )
    new_moments = (*attn_fresh, fresh_gate, fresh_up, fresh_down)
    summed = (*attn_sums, sum_gate, sum_up, sum_down)

    half = hidden_width // cores
    all_rows = repeat * part_rows

    def whole_rows(piece, axis):
        if repeat > 1:
            piece = lax.all_gather(piece, "r", axis=axis, tiled=True)
        return piece

    def core_order(mine, other, axis):
        first = jnp.where(f_index == 0, mine, other)
        second = jnp.where(f_index == 0, other, mine)
        return jnp.concatenate([first, second], axis=axis)

    def to_line(piece, planes):
        def keep(source, target):
            return target in planes

        here = piece
        if len(planes) > 1:
            here = place(piece, jnp.minimum(z_index, 1))
        parts = [here]
        for step in range(1, LINE):
            chunk = piece
            if len(planes) > 1:
                chunk = place(piece, (z_index ^ step) % 2)
            parts.append(swap(chunk, "z", step, keep))
        return jnp.concatenate(parts, axis=0)

    def over_chips(rows, planes):
        return [rows] + [plane_swap(rows, step, planes) for step in range(1, CHIPS)]

    tall = over_chips(to_line(whole_rows(update_down, 0), (2,)), (2,))
    wide_updates = whole_rows(wide_updates, 1)
    wide_mine = lax.dynamic_slice_in_dim(wide_updates, f_index * half, half, 2)
    wide_other = lax.dynamic_slice_in_dim(wide_updates, (1 - f_index) * half, half, 2)
    wide_rows = core_order(wide_mine, swap(wide_other, "f", 1), 1)
    wide = over_chips(to_line(wide_rows, (0, 1)), (0, 1))
    mine = whole_rows(mine, 0)
    other = whole_rows(other, 0)
    both = core_order(mine, swap(other, "f", 1), 0)
    square = over_chips(to_line(both, (3,)), (3,))

    y_first, y_second = after(tuple(part_y), query_own)
    y_second = swap(y_second, "f", 1)
    own_y, *low_y = fold(*after((y_first, y_second), other_own))

    mode = jnp.maximum(z_index - 1, 0).reshape(1)
    mode, own_y, low_y = lax.optimization_barrier((mode, own_y, low_y))
    gram, narrow = gram_of(mode, wide, tall, square)
    low_y = after(low_y, gram)
    arrived_y = [swap(piece, "xy", step) for step, piece in enumerate(low_y, 1)]
    line_pairs = [(z * cores + i, z * cores + 1 - i) for z in range(LINE - 1) for i in range(cores)]
    gram_other = lax.ppermute(gram, ("z", "f"), line_pairs)
    wide_o, tall_o, square_o = ortho_of(
        mode, gram, gram_other, narrow, wide, tall[0], square
    )
    arrived_y = after(arrived_y, square_o)

    def from_line(piece, planes):
        parts = piece.reshape((LINE, -1) + piece.shape[1:])

        def keep(source, target):
            return source in planes

        arrived = [parts[0]] + [
            swap(parts[step], "z", step, keep) for step in range(1, LINE)
        ]
        chosen = []
        for number in planes:
            which = z_index ^ number
            value = arrived[0]
            for step in range(1, LINE):
                value = jnp.where(which == step, arrived[step], value)
            chosen.append(value)
        return chosen

    def own_of(piece, core, axis):
        start = core * all_rows + r_index * part_rows
        return lax.dynamic_slice_in_dim(piece, start, part_rows, axis)

    square_o = from_line(square_o, (3,))[0]
    wide_o = jnp.stack(from_line(wide_o, (0, 1)), axis=0)
    tall_o = from_line(tall_o, (2,))[0]
    if repeat > 1:
        tall_o = lax.dynamic_slice_in_dim(tall_o, r_index * down_rows, down_rows, 0)
    mine = own_of(square_o, f_index, 0)
    other = swap(own_of(square_o, 1 - f_index, 0), "f", 1)
    first = jnp.where(f_index == 0, mine, other)
    second = jnp.where(f_index == 0, other, mine)
    wide_mine = own_of(wide_o, f_index, 1)
    wide_other = swap(own_of(wide_o, 1 - f_index, 1), "f", 1)
    ortho_wide = core_order(wide_mine, wide_other, 2)

    activations = residual + own_y
    for piece in arrived_y:
        activations += piece.astype(f32)
    activations = activations.astype(bf16).reshape(seq_count, seq_rows, width)

    orthogonal = (
        first[:, :width],
        first[:, width:],
        second[:, width:],
        second[:, :width],
        ortho_wide[0],
        ortho_wide[1],
        tall_o,
    )
    new_masters = []
    for master, piece in zip(masters, orthogonal):
        factor = math.sqrt(max(1.0, master.shape[1] / (master.shape[0] * device_count)))
        new_masters.append(master - (muon_rate * factor) * piece.astype(f32))
    new_small = small_params - plain_rate / math.sqrt(all_tokens) * sum_small
    return (
        activations,
        input_grad,
        *summed,
        *new_masters,
        *new_moments,
        sum_small,
        new_small,
    )


def solution(mesh):
    cores = mesh.shape["fsdp"]
    chips = mesh.shape["ctx"] // (4 * LINE)
    fine = Mesh(mesh.devices.reshape(chips, LINE, 4, cores), EVERY)
    token_spec = P("f", CTX, None)
    shard_spec = P(EVERY, None)
    return jax.shard_map(
        on_device,
        mesh=fine,
        in_specs=(token_spec, token_spec, P()) + (shard_spec,) * 14 + (P(EVERY),),
        out_specs=(token_spec, token_spec) + (shard_spec,) * 21 + (P(EVERY), P(EVERY)),
        check_vma=False,
    )
```

time: 3410 us -> 634 us (0.19)
  blocking collectives: 1620 us -> 0 us
  matrix products: 525 us -> 0 us
  waiting for transfers between devices: 695 us -> 236 us
  local copies, waits for them, and re-layouts: 280 us -> 33.6 us
  Pallas kernels: 0 us -> 170 us
  other arithmetic: 101 us -> 22.5 us
    unnamed x4 -> x0, blocking collectives: 1380 us -> none
    dot_general x54 -> x0, matrix products: 525 us -> none  [the longest x10 246 us: exact_product(): return jnp.dot(left_side, right_side, precision=lax.Precision.HIGHEST)]
    all_gather x11 -> x4, waiting for transfers between devices: 346 us -> 74 us  [the longest x1 43.4 us: on_device(): front_all = lax.all_gather(front, EVERY, axis=0, tiled=False)]
    all_gather x6 -> x0, blocking collectives: 246 us -> none  [the longest x1 45.4 us: on_device(): lax.all_gather(outgoing[1], ('ctx', 'fsdp'), axis=0, tiled=True)]
    unnamed x235 -> x112, local copies, waits for them, and re-layouts: 177 us -> 5 us
    pallas_call x0 -> x16, Pallas kernels: none -> 170 us  [the longest x1 67.2 us: ortho_of(): plain_call(ortho_kernel, [like(wide[0].shape, bf16), like(tall.shape, bf1...]
    ppermute x0 -> x67, waiting for transfers between devices: none -> 144 us  [the longest x57 135 us: swap(): return lax.ppermute(piece, axis, pairs)]
    unnamed x42 -> x0, starting transfers between devices: 143 us -> none
  transfers between devices with their start and end apart: 60 -> 76, of which waited for: 21 -> 32; matrix products, arithmetic and copies ran while one was open for 48% -> 7% of each run, Pallas kernels for 0% -> 21%
where the time goes in v1:
time: 634 us; the launch traced here: 625 us
  waiting for transfers between devices  236 us (37%)
  Pallas kernels  170 us (27%)
  starting transfers between devices  147 us (23%)
  local copies, waits for them, and re-layouts  33.6 us (5%)
  other arithmetic  22.5 us (4%)
  between operations  15.4 us (2%)
    ppermute x57, waiting for transfers between devices, swap(): return lax.ppermute(piece, axis, pairs)  135 us
    ppermute x57, starting transfers between devices, swap(): return lax.ppermute(piece, axis, pairs)  98.9 us
    pallas_call x1, Pallas kernels, ortho_of(): plain_call(ortho_kernel, [like(wide[0].shape, bf16), like(tall.shape, bf1...  67.2 us
    all_gather x1, waiting for transfers between devices, on_device(): front_all = lax.all_gather(front, EVERY, axis=0, tiled=False)  43.4 us
    all_gather x1, waiting for transfers between devices, on_device(): gate_up = lax.all_gather(gate_up, ('r', 'z'), axis=0, tiled=False)  30.6 us
    pallas_call x1, Pallas kernels, feed_forward(): plain_call(functools.partial(feed_kernel, count), [like((half, width), bf...  29.8 us
    all_to_all x5, starting transfers between devices, exchange(): return lax.all_to_all(parts, axes, split_axis=0, concat_axis=0, tiled=True)  27.2 us
    ppermute x9, starting transfers between devices, plane_swap(): return lax.ppermute(piece, ('z', 'xy'), pairs)  18.6 us
  transfers between devices with their start and end apart: 76, of which 32 were waited for; matrix products, arithmetic and copies ran while one was open for 7% of the time, Pallas kernels for 21%

profile of v1, /device:TPU:25, one launch (start us, length us, event | category | flops | bytes accessed | tf_op | source)
XLA Modules:
  0.0 625.2 jit_solution(8360949033116883388)
XLA Ops:
  19.3 4.4 all-to-all-start
  23.9 6.8 %all-to-all-done = bf16[8,2,28,608]{3,1,2,0:T(2,128)(2,1)S(1)} async-done(((bf16[8,2,28,608]{3,1,2,0:T(2,128)(2,1)}), bf16[8,2,28,608]{3,1,2,0:T(2,128)(2,1)S(1)}, u32[]{:S(2)}, u32[]{:S(2)}) %all-to-all-start) | async-done | bytes 544800 | tf_op jit(solution)/shard_map/all_to_all | solution.py:60
  30.7 43.4 %all-gather.6.cloned.1.call-done = bf16[32,29,2048]{2,1,0:T(8,128)(2,1)} async-done(((bf16[1,29,2048]{2,1,0:T(8,128)(2,1)}), bf16[32,29,2048]{2,1,0:T(8,128)(2,1)}) %all-gather.6.cloned.1.call-update) | async-done | bytes 3801104 | tf_op jit(solution)/shard_map/all_gather | solution.py:870
  78.8 5.9 reshape.356.w_ref
  86.3 4.2 shard_map.369
  94.0 7.8 %collective-permute-done = bf16[1,3,2,64,128]{4,3,2,1,0:T(8,128)(2,1)S(1)} collective-permute-done((bf16[1,3,2,64,128]{4,3,2,1,0:T(8,128)(2,1)}, bf16[1,3,2,64,128]{4,3,2,1,0:T(8,128)(2,1)S(1)}, u32[]{:S(2)}, u32[]{:S(2)}) %collective-permute-start) | collective-permute-done | bytes 98336 | tf_op jit(solution)/shard_map/ppermute | solution.py:70
  103.3 3.9 collective-permute-done.2
  111.8 5.8 collective-permute-done.3.refs_1_
  118.3 10.7 %collective-permute-done.5.refs_3_ = bf16[4,3,2,64,128]{4,3,2,1,0:T(8,128)(2,1)S(1)} collective-permute-done((bf16[4,3,2,64,128]{4,3,2,1,0:T(8,128)(2,1)S(1)}, bf16[4,3,2,64,128]{4,3,2,1,0:T(8,128)(2,1)S(1)}, u32[]{:S(2)}, u32[]{:S(2)}) %collective-permute-start.5) | collective-permute-done | bytes 393248 | tf_op jit(solution)/shard_map/ppermute | solution.py:70
  129.8 9.8 %shard_map.370.o_ref = bf16[3,14,64,64]{3,2,1,0:T(8,128)(2,1)} custom-call(bf16[3,14,64,64]{3,2,1,0:T(8,128)(2,1)} %get-tuple-element.125.q_ref, bf16[4,3,2,64,128]{4,3,2,1,0:T(8,128)(2,1)} %copy-done.23, bf16[4,3,2,64,128]{4,3,2,1,0:T(8,128)(2,1)} %copy-done.43, bf16[4,3,2,64,128]{4,3,2,1,0:T(8,128)(2,1)} %copy-done.44, ...), custom_call_target="tpu_custom_call" | custom-call | flops 2818572288 | bytes 22020096 | tf_op jit(solution)/shard_map/pallas_call | solution.py:458
  139.6 4.4 shard_map.371
  146.7 4.1 collective-permute-start.9
  150.8 5.7 collective-permute-done.6.refs_1_
  156.5 2.9 collective-permute-start.10
  159.4 5.3 collective-permute-done.8.refs_3_
  164.7 7.2 %collective-permute-start.12 = (bf16[192,896]{1,0:T(8,128)(2,1)S(1)}, bf16[192,896]{1,0:T(8,128)(2,1)S(1)}, u32[]{:S(2)}, u32[]{:S(2)}) collective-permute-start(bf16[192,896]{1,0:T(8,128)(2,1)S(1)} %collective-permute-done.8.refs_3_), channel_id=1, source_target_pairs={{0,1},{1,0},{2,3},{3,2},{4,5},{5,4},{6,7},{7,6},{8,9},{9,8},{10,11... | collective-permute-start | bytes 1032200 | tf_op jit(solution)/shard_map/ppermute | solution.py:70
  173.4 30.6 %all-gather.8.cloned.1.call-done.refs_10_ = bf16[4,2,224,608]{3,2,1,0:T(8,128)(2,1)} async-done(((bf16[1,2,224,608]{3,2,1,0:T(8,128)(2,1)}), bf16[4,2,224,608]{3,2,1,0:T(8,128)(2,1)}) %all-gather.8.cloned.1.call-update) | async-done | bytes 2179088 | tf_op jit(solution)/shard_map/all_gather | solution.py:881
  204.1 29.8 %shard_map.372 = (bf16[768,896]{1,0:T(8,128)(2,1)}, bf16[768,896]{1,0:T(8,128)(2,1)}, bf16[768,896]{1,0:T(8,128)(2,1)}, bf16[768,896]{1,0:T(8,128)(2,1)}, bf16[8...) custom-call(bf16[192,896]{1,0:T(8,128)(2,1)} %get-tuple-element.130.refs_0_, ...), custom_call_target="tpu_custom_call" | custom-call | flops 30123491328 | bytes 17547264 | tf_op jit(solution)/shard_map/pallas_call | solution.py:562
  234.4 3.0 collective-permute-done.13.b_ref
  238.5 3.0 shard_map.373
  241.5 6.3 %all-to-all-start.1 = ((bf16[4,1,224,608]{3,2,1,0:T(8,128)(2,1)}), bf16[4,1,224,608]{3,2,1,0:T(8,128)(2,1)S(1)}, u32[]{:S(2)}, u32[]{:S(2)}) async-start(bf16[4,1,224,608]{3,2,1,0:T(8,128)(2,1)} %bitcast.22), calls=%async_computation.1 | async-start | bytes 2293760 | tf_op jit(solution)/shard_map/all_to_all | solution.py:60
  250.5 6.3 %collective-permute-done.14.a_ref = bf16[192,896]{1,0:T(8,128)(2,1)S(1)} collective-permute-done((bf16[192,896]{1,0:T(8,128)(2,1)S(1)}, bf16[192,896]{1,0:T(8,128)(2,1)S(1)}, u32[]{:S(2)}, u32[]{:S(2)}) %collective-permute-start.14) | collective-permute-done | bytes 344096 | tf_op jit(solution)/shard_map/ppermute | solution.py:70
  257.6 7.5 %collective-permute-done.16.c_ref = bf16[192,896]{1,0:T(8,128)(2,1)S(1)} collective-permute-done((bf16[192,896]{1,0:T(8,128)(2,1)S(1)}, bf16[192,896]{1,0:T(8,128)(2,1)S(1)}, u32[]{:S(2)}, u32[]{:S(2)}) %collective-permute-start.16) | collective-permute-done | bytes 344096 | tf_op jit(solution)/shard_map/ppermute | solution.py:70
  265.1 8.2 %all-to-all-done.1 = bf16[4,1,224,608]{3,2,1,0:T(8,128)(2,1)S(1)} async-done(((bf16[4,1,224,608]{3,2,1,0:T(8,128)(2,1)}), bf16[4,1,224,608]{3,2,1,0:T(8,128)(2,1)S(1)}, u32[]{:S(2)}, u32[]{:S(2)}) %all-to-all-start.1) | async-done | bytes 1089568 | tf_op jit(solution)/shard_map/all_to_all | solution.py:60
  273.3 6.0 all-to-all-start.2
  279.3 4.9 shard_map.374
  284.2 16.1 %shard_map.375 = (f32[3,14,64,64]{3,2,1,0:T(8,128)}, bf16[4,3,2,64,128]{4,3,2,1,0:T(8,128)(2,1)}, bf16[4,3,2,64,128]{4,3,2,1,0:T(8,128)(2,1)}, bf16[4,3,2,64,128...) custom-call(bf16[3,14,64,64]{3,2,1,0:T(8,128)(2,1)} %get-tuple-element.125.q_ref, ...), custom_call_target="tpu_custom_call" | custom-call | flops 7046430720 | bytes 33030144 | tf_op jit(solution)/shard_map/pallas_call | solution.py:471
  305.9 6.0 all-to-all-start.4
  311.9 7.4 %collective-permute-done.20 = bf16[4,3,2,64,128]{4,3,2,1,0:T(8,128)(2,1)} collective-permute-done((bf16[4,3,2,64,128]{4,3,2,1,0:T(8,128)(2,1)}, bf16[4,3,2,64,128]{4,3,2,1,0:T(8,128)(2,1)}, u32[]{:S(2)}, u32[]{:S(2)}) %collective-permute-start.20) | collective-permute-done | bytes 393248 | tf_op jit(solution)/shard_map/ppermute | solution.py:70
  321.8 3.0 collective-permute-start.23
  324.7 1.8 all-to-all-done.4
  326.6 4.5 all-to-all-start.3
  332.0 3.5 shard_map.379
  336.5 4.0 collective-permute-start.24
  340.5 6.0 shard_map.376
  346.6 4.0 copy.89
  354.9 3.4 collective-permute-start.26
  358.3 1.9 collective-permute-start.27
  360.3 5.2 shard_map.377
  368.8 3.8 shard_map.380
  379.4 6.5 %collective-permute-done.39.a_ref = bf16[4,29,2048]{2,1,0:T(8,128)(2,1)S(1)} collective-permute-done((bf16[4,29,2048]{2,1,0:T(8,128)(2,1)}, bf16[4,29,2048]{2,1,0:T(8,128)(2,1)S(1)}, u32[]{:S(2)}, u32[]{:S(2)}) %collective-permute-start.39) | collective-permute-done | bytes 475168 | tf_op jit(solution)/shard_map/ppermute | solution.py:70
  386.8 11.8 %collective-permute-done.41.c_ref = bf16[4,29,2048]{2,1,0:T(8,128)(2,1)S(1)} collective-permute-done((bf16[4,29,2048]{2,1,0:T(8,128)(2,1)}, bf16[4,29,2048]{2,1,0:T(8,128)(2,1)S(1)}, u32[]{:S(2)}, u32[]{:S(2)}) %collective-permute-start.41) | collective-permute-done | bytes 475168 | tf_op jit(solution)/shard_map/ppermute | solution.py:70
  399.4 2.6 shard_map.381
  402.9 2.6 collective-permute-start.44
  406.4 2.5 collective-permute-start.31
  408.9 8.9 %collective-permute-done.43.b_ref = bf16[1,29,2048]{2,1,0:T(8,128)(2,1)S(1)} collective-permute-done((bf16[1,29,2048]{2,1,0:T(8,128)(2,1)}, bf16[1,29,2048]{2,1,0:T(8,128)(2,1)S(1)}, u32[]{:S(2)}, u32[]{:S(2)}) %collective-permute-start.43) | collective-permute-done | bytes 118816 | tf_op jit(solution)/shard_map/ppermute | solution.py:70
  419.2 2.2 shard_map.382
  431.4 10.9 %collective-permute-done.46 = bf16[56,1024]{1,0:T(8,128)(2,1)S(1)} collective-permute-done((bf16[56,1024]{1,0:T(8,128)(2,1)S(1)}, bf16[56,1024]{1,0:T(8,128)(2,1)S(1)}, u32[]{:S(2)}, u32[]{:S(2)}) %collective-permute-start.46) | collective-permute-done | bytes 114720 | tf_op jit(solution)/shard_map/ppermute | solution.py:70
  446.1 3.5 collective-permute-done.48
  451.5 3.0 collective-permute-start.49
  454.5 1.9 collective-permute-start.50
  456.4 3.4 collective-permute-start.51
  459.9 3.0 shard_map.378
  463.0 4.4 collective-permute-done.50.refs_10_.refs_7_
  467.4 4.3 collective-permute-done.51.refs_11_.refs_8_
  472.5 4.7 shard_map.383
  477.3 2.6 collective-permute-start.55
  483.1 67.2 %shard_map.384 = (bf16[224,2432]{1,0:T(8,128)(2,1)}, bf16[608,896]{1,0:T(8,128)(2,1)}, bf16[224,1024]{1,0:T(8,128)(2,1)}) custom-call(s32[1]{0:T(128)} %bitcast.5.mode_ref, f32[896,896]{1,0:T(8,128)} %get-tuple-element.194.a_ref, f32[896,896]{1,0:T(8,128)} %collective-permute-done.55.b_ref, f32[128,128]{1,0:T(8,128)} %get-tuple-element.198.n_ref, ...), custom_call_target="tpu_custom_call" | custom-call | flops 71932313600 | bytes 6422528 | tf_op jit(solution)/shard_map/pallas_call | solution.py:801
  551.7 7.7 %collective-permute-start.56 = (bf16[56,1024]{1,0:T(8,128)(2,1)S(1)}, bf16[56,1024]{1,0:T(8,128)(2,1)S(1)}, u32[]{:S(2)}, u32[]{:S(2)}) collective-permute-start(bf16[56,1024]{1,0:T(8,128)(2,1)S(1)} %get-tuple-element.245), channel_id=1, source_target_pairs={{24,0},{25,1},{26,2},{27,3},{28,4},{29,5},{30,6},{31,7}} | collective-permute-start | bytes 344072 | tf_op jit(solution)/shard_map/ppermute | solution.py:70
  559.4 12.9 %collective-permute-start.57 = (bf16[56,1024]{1,0:T(8,128)(2,1)S(1)}, bf16[56,1024]{1,0:T(8,128)(2,1)S(1)}, u32[]{:S(2)}, u32[]{:S(2)}) collective-permute-start(bf16[56,1024]{1,0:T(8,128)(2,1)S(1)} %get-tuple-element.244), channel_id=1, source_target_pairs={{24,8},{25,9},{26,10},{27,11},{28,12},{29,13},{30,14},{31,15}} | collective-permute-start | bytes 344072 | tf_op jit(solution)/shard_map/ppermute | solution.py:70
  572.4 8.0 %collective-permute-start.58 = (bf16[56,1024]{1,0:T(8,128)(2,1)S(1)}, bf16[56,1024]{1,0:T(8,128)(2,1)S(1)}, u32[]{:S(2)}, u32[]{:S(2)}) collective-permute-start(bf16[56,1024]{1,0:T(8,128)(2,1)S(1)} %get-tuple-element.243), channel_id=1, source_target_pairs={{24,16},{25,17},{26,18},{27,19},{28,20},{29,21},{30,22},{31,23}} | collective-permute-start | bytes 344072 | tf_op jit(solution)/shard_map/ppermute | solution.py:70
  588.3 4.7 collective-permute-done.60
  594.3 15.1 %collective-permute-done.61 = bf16[56,2432]{1,0:T(8,128)(2,1)S(1)} collective-permute-done((bf16[56,2432]{1,0:T(8,128)(2,1)S(1)}, bf16[56,2432]{1,0:T(8,128)(2,1)S(1)}, u32[]{:S(2)}, u32[]{:S(2)}) %collective-permute-start.61) | collective-permute-done | bytes 272416 | tf_op jit(solution)/shard_map/ppermute | solution.py:70
  611.9 4.0 collective-permute-done.66
  (307 shorter events, 102.9 us)
Async XLA Ops:
  7.2 66.9 %all-gather.6.cloned.1.call-start = ((), (), s32[]{:S(2)}) async-start(), calls=%async_computation.5 | async-start | bytes 4325376 | tf_op jit(solution)/shard_map/all_gather | solution.py:870
  12.0 160.6 %all-gather.10.cloned.1.call-start = ((), (), s32[]{:S(2)}) async-start(), calls=%async_computation.7 | async-start | bytes 1361920 | tf_op jit(solution)/shard_map/all_gather | solution.py:884
  12.8 159.7 %all-gather.12.cloned.1.call-start = ((), (), s32[]{:S(2)}) async-start(), calls=%async_computation.8 | async-start | bytes 3096576 | tf_op jit(solution)/shard_map/all_gather | solution.py:908
  19.3 11.4 %all-to-all-start = ((bf16[8,2,28,608]{3,1,2,0:T(2,128)(2,1)}), bf16[8,2,28,608]{3,1,2,0:T(2,128)(2,1)S(1)}, u32[]{:S(2)}, u32[]{:S(2)}) async-start(bf16[8,2,28,608]{3,1,2,0:T(2,128)(2,1)} %copy.76), calls=%async_computation | async-start | bytes 1146880 | tf_op jit(solution)/shard_map/all_to_all | solution.py:60
  23.7 180.3 %all-gather.8.cloned.1.call-start = ((), (), s32[]{:S(2)}) async-start(), calls=%async_computation.6 | async-start | bytes 2867200 | tf_op jit(solution)/shard_map/all_gather | solution.py:881
  90.5 11.3 %collective-permute-start = (bf16[1,3,2,64,128]{4,3,2,1,0:T(8,128)(2,1)}, bf16[1,3,2,64,128]{4,3,2,1,0:T(8,128)(2,1)S(1)}, u32[]{:S(2)}, u32[]{:S(2)}) collective-permute-start(bf16[1,3,2,64,128]{4,3,2,1,0:T(8,128)(2,1)} %bitcast.72), channel_id=1, source_target_pairs={{0,8},{8,0},{16,24},{24,16},{1,9},{9,1},{17,25},{25,17},{2,10},{10... | collective-permute-start | bytes 294920 | tf_op jit(solution)/shard_map/ppermute | solution.py:70
  91.4 11.9 %collective-permute-start.1 = (bf16[1,3,2,64,128]{4,3,2,1,0:T(8,128)(2,1)}, bf16[1,3,2,64,128]{4,3,2,1,0:T(8,128)(2,1)S(1)}, u32[]{:S(2)}, u32[]{:S(2)}) collective-permute-start(bf16[1,3,2,64,128]{4,3,2,1,0:T(8,128)(2,1)} %bitcast.73), channel_id=1, source_target_pairs={{0,16},{8,24},{16,0},{24,8},{1,17},{9,25},{17,1},{25,9},{2,18},{10... | collective-permute-start | bytes 294920 | tf_op jit(solution)/shard_map/ppermute | solution.py:70
  92.4 14.7 %collective-permute-start.2 = (bf16[1,3,2,64,128]{4,3,2,1,0:T(8,128)(2,1)}, bf16[1,3,2,64,128]{4,3,2,1,0:T(8,128)(2,1)S(1)}, u32[]{:S(2)}, u32[]{:S(2)}) collective-permute-start(bf16[1,3,2,64,128]{4,3,2,1,0:T(8,128)(2,1)} %bitcast.74), channel_id=1, source_target_pairs={{0,24},{8,16},{16,8},{24,0},{1,25},{9,17},{17,9},{25,1},{2,26},{10... | collective-permute-start | bytes 294920 | tf_op jit(solution)/shard_map/ppermute | solution.py:70
  108.1 9.6 %collective-permute-start.3 = (bf16[4,3,2,64,128]{4,3,2,1,0:T(8,128)(2,1)S(1)}, bf16[4,3,2,64,128]{4,3,2,1,0:T(8,128)(2,1)S(1)}, u32[]{:S(2)}, u32[]{:S(2)}) collective-permute-start(bf16[4,3,2,64,128]{4,3,2,1,0:T(8,128)(2,1)S(1)} %pad_maximum_fusion.2.refs_0_), channel_id=1, source_target_pairs={{0,2},{2,0},{4,6},{6,4},{1,3},{3,1},{5,7},{7,5},{8,10},{10,8},{12,... | collective-permute-start | bytes 1179656 | tf_op jit(solution)/shard_map/ppermute | solution.py:70
  109.1 9.2 %collective-permute-start.4 = (bf16[4,3,2,64,128]{4,3,2,1,0:T(8,128)(2,1)S(1)}, bf16[4,3,2,64,128]{4,3,2,1,0:T(8,128)(2,1)S(1)}, u32[]{:S(2)}, u32[]{:S(2)}) collective-permute-start(bf16[4,3,2,64,128]{4,3,2,1,0:T(8,128)(2,1)S(1)} %pad_maximum_fusion.2.refs_0_), channel_id=1, source_target_pairs={{0,4},{2,6},{4,0},{6,2},{1,5},{3,7},{5,1},{7,3},{8,12},{10,14},{12... | collective-permute-start | bytes 1179656 | tf_op jit(solution)/shard_map/ppermute | solution.py:70
  109.6 19.5 %collective-permute-start.5 = (bf16[4,3,2,64,128]{4,3,2,1,0:T(8,128)(2,1)S(1)}, bf16[4,3,2,64,128]{4,3,2,1,0:T(8,128)(2,1)S(1)}, u32[]{:S(2)}, u32[]{:S(2)}) collective-permute-start(bf16[4,3,2,64,128]{4,3,2,1,0:T(8,128)(2,1)S(1)} %pad_maximum_fusion.2.refs_0_), channel_id=1, source_target_pairs={{0,6},{2,4},{4,2},{6,0},{1,7},{3,5},{5,3},{7,1},{8,14},{10,12},{12... | collective-permute-start | bytes 1179656 | tf_op jit(solution)/shard_map/ppermute | solution.py:70
  144.0 12.4 %collective-permute-start.6 = (bf16[192,896]{1,0:T(8,128)(2,1)}, bf16[192,896]{1,0:T(8,128)(2,1)S(1)}, u32[]{:S(2)}, u32[]{:S(2)}) collective-permute-start(bf16[192,896]{1,0:T(8,128)(2,1)} %get-tuple-element.130.refs_0_), channel_id=1, source_target_pairs={{0,2},{2,0},{4,6},{6,4},{1,3},{3,1},{5,7},{7,5},{8,10},{10,8},{12,... | collective-permute-start | bytes 1032200 | tf_op jit(solution)/shard_map/ppermute | solution.py:70
  144.0 15.3 %collective-permute-start.7 = (bf16[192,896]{1,0:T(8,128)(2,1)}, bf16[192,896]{1,0:T(8,128)(2,1)S(1)}, u32[]{:S(2)}, u32[]{:S(2)}) collective-permute-start(bf16[192,896]{1,0:T(8,128)(2,1)} %get-tuple-element.130.refs_0_), channel_id=1, source_target_pairs={{0,4},{2,6},{4,0},{6,2},{1,5},{3,7},{5,1},{7,3},{8,12},{10,14},{12... | collective-permute-start | bytes 1032200 | tf_op jit(solution)/shard_map/ppermute | solution.py:70
  145.8 18.9 %collective-permute-start.8 = (bf16[192,896]{1,0:T(8,128)(2,1)}, bf16[192,896]{1,0:T(8,128)(2,1)S(1)}, u32[]{:S(2)}, u32[]{:S(2)}) collective-permute-start(bf16[192,896]{1,0:T(8,128)(2,1)} %get-tuple-element.130.refs_0_), channel_id=1, source_target_pairs={{0,6},{2,4},{4,2},{6,0},{1,7},{3,5},{5,3},{7,1},{8,14},{10,12},{12... | collective-permute-start | bytes 1032200 | tf_op jit(solution)/shard_map/ppermute | solution.py:70
  146.7 25.9 %collective-permute-start.9 = (bf16[192,896]{1,0:T(8,128)(2,1)}, bf16[192,896]{1,0:T(8,128)(2,1)S(1)}, u32[]{:S(2)}, u32[]{:S(2)}) collective-permute-start(bf16[192,896]{1,0:T(8,128)(2,1)} %get-tuple-element.130.refs_0_), channel_id=1, source_target_pairs={{0,1},{1,0},{2,3},{3,2},{4,5},{5,4},{6,7},{7,6},{8,9},{9,8},{10,11... | collective-permute-start | bytes 1032200 | tf_op jit(solution)/shard_map/ppermute | solution.py:70
  156.5 16.1 %collective-permute-start.10 = (bf16[192,896]{1,0:T(8,128)(2,1)S(1)}, bf16[192,896]{1,0:T(8,128)(2,1)S(1)}, u32[]{:S(2)}, u32[]{:S(2)}) collective-permute-start(bf16[192,896]{1,0:T(8,128)(2,1)S(1)} %collective-permute-done.6.refs_1_), channel_id=1, source_target_pairs={{0,1},{1,0},{2,3},{3,2},{4,5},{5,4},{6,7},{7,6},{8,9},{9,8},{10,11... | collective-permute-start | bytes 1032200 | tf_op jit(solution)/shard_map/ppermute | solution.py:70
  159.3 13.3 %collective-permute-start.11 = (bf16[192,896]{1,0:T(8,128)(2,1)S(1)}, bf16[192,896]{1,0:T(8,128)(2,1)S(1)}, u32[]{:S(2)}, u32[]{:S(2)}) collective-permute-start(bf16[192,896]{1,0:T(8,128)(2,1)S(1)} %collective-permute-done.7.refs_2_), channel_id=1, source_target_pairs={{0,1},{1,0},{2,3},{3,2},{4,5},{5,4},{6,7},{7,6},{8,9},{9,8},{10,11... | collective-permute-start | bytes 1032200 | tf_op jit(solution)/shard_map/ppermute | solution.py:70
  241.5 31.8 %all-to-all-start.1 = ((bf16[4,1,224,608]{3,2,1,0:T(8,128)(2,1)}), bf16[4,1,224,608]{3,2,1,0:T(8,128)(2,1)S(1)}, u32[]{:S(2)}, u32[]{:S(2)}) async-start(bf16[4,1,224,608]{3,2,1,0:T(8,128)(2,1)} %bitcast.22), calls=%async_computation.1 | async-start | bytes 2293760 | tf_op jit(solution)/shard_map/all_to_all | solution.py:60
  247.8 9.0 %collective-permute-start.14 = (bf16[192,896]{1,0:T(8,128)(2,1)S(1)}, bf16[192,896]{1,0:T(8,128)(2,1)S(1)}, u32[]{:S(2)}, u32[]{:S(2)}) collective-permute-start(bf16[192,896]{1,0:T(8,128)(2,1)S(1)} %copy-done.55), channel_id=1, source_target_pairs={{0,2},{2,0},{4,6},{6,4},{1,3},{3,1},{5,7},{7,5},{8,10},{10,8},{12,... | collective-permute-start | bytes 1032200 | tf_op jit(solution)/shard_map/ppermute | solution.py:70
  250.2 14.9 %collective-permute-start.16 = (bf16[192,896]{1,0:T(8,128)(2,1)S(1)}, bf16[192,896]{1,0:T(8,128)(2,1)S(1)}, u32[]{:S(2)}, u32[]{:S(2)}) collective-permute-start(bf16[192,896]{1,0:T(8,128)(2,1)S(1)} %copy-done.53), channel_id=1, source_target_pairs={{0,6},{2,4},{4,2},{6,0},{1,7},{3,5},{5,3},{7,1},{8,14},{10,12},{12... | collective-permute-start | bytes 1032200 | tf_op jit(solution)/shard_map/ppermute | solution.py:70
  273.3 30.7 %all-to-all-start.2 = ((bf16[4,1,224,608]{3,2,1,0:T(8,128)(2,1)}), bf16[4,1,224,608]{3,2,1,0:T(8,128)(2,1)S(1)}, u32[]{:S(2)}, u32[]{:S(2)}) async-start(bf16[4,1,224,608]{3,2,1,0:T(8,128)(2,1)} %bitcast.24), calls=%async_computation.2 | async-start | bytes 2293760 | tf_op jit(solution)/shard_map/all_to_all | solution.py:60
  300.3 11.5 %collective-permute-start.18 = (bf16[4,3,2,64,128]{4,3,2,1,0:T(8,128)(2,1)}, bf16[4,3,2,64,128]{4,3,2,1,0:T(8,128)(2,1)S(1)}, u32[]{:S(2)}, u32[]{:S(2)}) collective-permute-start(bf16[4,3,2,64,128]{4,3,2,1,0:T(8,128)(2,1)} %get-tuple-element.158), channel_id=1, source_target_pairs={{0,2},{2,0},{4,6},{6,4},{1,3},{3,1},{5,7},{7,5},{8,10},{10,8},{12,... | collective-permute-start | bytes 1179656 | tf_op jit(solution)/shard_map/ppermute | solution.py:70
  301.6 10.3 %collective-permute-start.19 = (bf16[4,3,2,64,128]{4,3,2,1,0:T(8,128)(2,1)}, bf16[4,3,2,64,128]{4,3,2,1,0:T(8,128)(2,1)S(1)}, u32[]{:S(2)}, u32[]{:S(2)}) collective-permute-start(bf16[4,3,2,64,128]{4,3,2,1,0:T(8,128)(2,1)} %get-tuple-element.159), channel_id=1, source_target_pairs={{0,4},{2,6},{4,0},{6,2},{1,5},{3,7},{5,1},{7,3},{8,12},{10,14},{12... | collective-permute-start | bytes 1179656 | tf_op jit(solution)/shard_map/ppermute | solution.py:70
  302.8 16.4 %collective-permute-start.20 = (bf16[4,3,2,64,128]{4,3,2,1,0:T(8,128)(2,1)}, bf16[4,3,2,64,128]{4,3,2,1,0:T(8,128)(2,1)}, u32[]{:S(2)}, u32[]{:S(2)}) collective-permute-start(bf16[4,3,2,64,128]{4,3,2,1,0:T(8,128)(2,1)} %get-tuple-element.160), channel_id=1, source_target_pairs={{0,6},{2,4},{4,2},{6,0},{1,7},{3,5},{5,3},{7,1},{8,14},{10,12},{12... | collective-permute-start | bytes 1179656 | tf_op jit(solution)/shard_map/ppermute | solution.py:70
  305.9 20.7 %all-to-all-start.4 = ((bf16[8,2,28,608]{3,1,2,0:T(2,128)(2,1)}), bf16[8,2,28,608]{3,1,2,0:T(2,128)(2,1)S(1)}, u32[]{:S(2)}, u32[]{:S(2)}) async-start(bf16[8,2,28,608]{3,1,2,0:T(2,128)(2,1)} %copy.87), calls=%async_computation.4 | async-start | bytes 1146880 | tf_op jit(solution)/shard_map/all_to_all | solution.py:60
  321.2 29.3 %collective-permute-start.21 = (bf16[1,3,2,64,128]{4,3,2,1,0:T(8,128)(2,1)}, bf16[1,3,2,64,128]{4,3,2,1,0:T(8,128)(2,1)}, u32[]{:S(2)}, u32[]{:S(2)}) collective-permute-start(bf16[1,3,2,64,128]{4,3,2,1,0:T(8,128)(2,1)} %get-tuple-element.246), channel_id=1, source_target_pairs={{0,8},{8,0},{16,24},{24,16},{1,9},{9,1},{17,25},{25,17},{2,10},{10... | collective-permute-start | bytes 294920 | tf_op jit(solution)/shard_map/ppermute | solution.py:70
  321.5 29.1 %collective-permute-start.22 = (bf16[1,3,2,64,128]{4,3,2,1,0:T(8,128)(2,1)}, bf16[1,3,2,64,128]{4,3,2,1,0:T(8,128)(2,1)}, u32[]{:S(2)}, u32[]{:S(2)}) collective-permute-start(bf16[1,3,2,64,128]{4,3,2,1,0:T(8,128)(2,1)} %get-tuple-element.248), channel_id=1, source_target_pairs={{0,16},{8,24},{16,0},{24,8},{1,17},{9,25},{17,1},{25,9},{2,18},{10... | collective-permute-start | bytes 294920 | tf_op jit(solution)/shard_map/ppermute | solution.py:70
  321.8 28.8 %collective-permute-start.23 = (bf16[1,3,2,64,128]{4,3,2,1,0:T(8,128)(2,1)}, bf16[1,3,2,64,128]{4,3,2,1,0:T(8,128)(2,1)}, u32[]{:S(2)}, u32[]{:S(2)}) collective-permute-start(bf16[1,3,2,64,128]{4,3,2,1,0:T(8,128)(2,1)} %get-tuple-element.247), channel_id=1, source_target_pairs={{0,24},{8,16},{16,8},{24,0},{1,25},{9,17},{17,9},{25,1},{2,26},{10... | collective-permute-start | bytes 294920 | tf_op jit(solution)/shard_map/ppermute | solution.py:70
  326.6 33.7 %all-to-all-start.3 = ((bf16[4,1,152,896]{3,2,1,0:T(8,128)(2,1)}), bf16[4,1,152,896]{3,2,1,0:T(8,128)(2,1)S(1)}, u32[]{:S(2)}, u32[]{:S(2)}) async-start(bf16[4,1,152,896]{3,2,1,0:T(8,128)(2,1)} %bitcast.27), calls=%async_computation.3 | async-start | bytes 2179072 | tf_op jit(solution)/shard_map/all_to_all | solution.py:60
  336.5 15.8 %collective-permute-start.24 = (bf16[2,28,2432]{2,1,0:T(8,128)(2,1)S(1)}, bf16[2,28,2432]{2,1,0:T(8,128)(2,1)S(1)}, u32[]{:S(2)}, u32[]{:S(2)}) collective-permute-start(bf16[2,28,2432]{2,1,0:T(8,128)(2,1)S(1)} %constant_dynamic-slice_fusion.1), channel_id=1, source_target_pairs={{0,1},{1,0},{2,3},{3,2},{4,5},{5,4},{6,7},{7,6},{8,9},{9,8},{10,11... | collective-permute-start | bytes 817160 | tf_op jit(solution)/shard_map/ppermute | solution.py:70
  350.5 16.0 %collective-permute-start.37 = (bf16[4,4,28,1792]{3,1,2,0:T(4,128)(2,1)}, bf16[4,4,28,1792]{3,1,2,0:T(4,128)(2,1)S(1)}, u32[]{:S(2)}, u32[]{:S(2)}) collective-permute-start(bf16[4,4,28,1792]{3,1,2,0:T(4,128)(2,1)} %copy.89), channel_id=1, source_target_pairs={{0,1},{1,0},{2,3},{3,2},{4,5},{5,4},{6,7},{7,6},{8,9},{9,8},{10,11... | collective-permute-start | bytes 4816904 | tf_op jit(solution)/shard_map/ppermute | solution.py:70
  353.5 20.3 %collective-permute-start.25 = (bf16[56,2432]{1,0:T(8,128)(2,1)}, bf16[56,2432]{1,0:T(8,128)(2,1)}, u32[]{:S(2)}, u32[]{:S(2)}) collective-permute-start(bf16[56,2432]{1,0:T(8,128)(2,1)} %get-tuple-element.240), channel_id=1, source_target_pairs={{0,8},{8,0},{1,9},{9,1},{2,10},{10,2},{3,11},{11,3},{4,12},{12,4},... | collective-permute-start | bytes 817160 | tf_op jit(solution)/shard_map/ppermute | solution.py:70
  354.9 19.6 %collective-permute-start.26 = (bf16[56,2432]{1,0:T(8,128)(2,1)}, bf16[56,2432]{1,0:T(8,128)(2,1)}, u32[]{:S(2)}, u32[]{:S(2)}) collective-permute-start(bf16[56,2432]{1,0:T(8,128)(2,1)} %get-tuple-element.241), channel_id=1, source_target_pairs={{16,0},{24,8},{17,1},{25,9},{18,2},{26,10},{19,3},{27,11},{20,4},{... | collective-permute-start | bytes 817160 | tf_op jit(solution)/shard_map/ppermute | solution.py:70
  358.3 17.3 %collective-permute-start.27 = (bf16[56,2432]{1,0:T(8,128)(2,1)}, bf16[56,2432]{1,0:T(8,128)(2,1)S(1)}, u32[]{:S(2)}, u32[]{:S(2)}) collective-permute-start(bf16[56,2432]{1,0:T(8,128)(2,1)} %get-tuple-element.242), channel_id=1, source_target_pairs={{16,8},{24,0},{17,9},{25,1},{18,10},{26,2},{19,11},{27,3},{20,12},... | collective-permute-start | bytes 817160 | tf_op jit(solution)/shard_map/ppermute | solution.py:70
  366.5 62.3 %collective-permute-start.17 = (bf16[768,896]{1,0:T(8,128)(2,1)S(1)}, bf16[768,896]{1,0:T(8,128)(2,1)}, u32[]{:S(2)}, u32[]{:S(2)}) collective-permute-start(bf16[768,896]{1,0:T(8,128)(2,1)S(1)} %copy-done.39), channel_id=1, source_target_pairs={{0,1},{1,0},{2,3},{3,2},{4,5},{5,4},{6,7},{7,6},{8,9},{9,8},{10,11... | collective-permute-start | bytes 4128776 | tf_op jit(solution)/shard_map/ppermute | solution.py:70
  372.6 13.3 %collective-permute-start.39 = (bf16[4,29,2048]{2,1,0:T(8,128)(2,1)}, bf16[4,29,2048]{2,1,0:T(8,128)(2,1)S(1)}, u32[]{:S(2)}, u32[]{:S(2)}) collective-permute-start(bf16[4,29,2048]{2,1,0:T(8,128)(2,1)} %get-tuple-element.185), channel_id=1, source_target_pairs={{0,2},{2,0},{4,6},{6,4},{1,3},{3,1},{5,7},{7,5},{8,10},{10,8},{12,... | collective-permute-start | bytes 1425416 | tf_op jit(solution)/shard_map/ppermute | solution.py:70
  373.8 13.0 %collective-permute-start.40 = (bf16[4,29,2048]{2,1,0:T(8,128)(2,1)}, bf16[4,29,2048]{2,1,0:T(8,128)(2,1)S(1)}, u32[]{:S(2)}, u32[]{:S(2)}) collective-permute-start(bf16[4,29,2048]{2,1,0:T(8,128)(2,1)} %get-tuple-element.186), channel_id=1, source_target_pairs={{0,4},{2,6},{4,0},{6,2},{1,5},{3,7},{5,1},{7,3},{8,12},{10,14},{12... | collective-permute-start | bytes 1425416 | tf_op jit(solution)/shard_map/ppermute | solution.py:70
  374.4 24.2 %collective-permute-start.41 = (bf16[4,29,2048]{2,1,0:T(8,128)(2,1)}, bf16[4,29,2048]{2,1,0:T(8,128)(2,1)S(1)}, u32[]{:S(2)}, u32[]{:S(2)}) collective-permute-start(bf16[4,29,2048]{2,1,0:T(8,128)(2,1)} %get-tuple-element.187), channel_id=1, source_target_pairs={{0,6},{2,4},{4,2},{6,0},{1,7},{3,5},{5,3},{7,1},{8,14},{10,12},{12... | collective-permute-start | bytes 1425416 | tf_op jit(solution)/shard_map/ppermute | solution.py:70
  377.5 52.6 %collective-permute-start.28 = (bf16[224,2432]{1,0:T(8,128)(2,1)S(1)}, bf16[224,2432]{1,0:T(8,128)(2,1)}, u32[]{:S(2)}, u32[]{:S(2)}) collective-permute-start(bf16[224,2432]{1,0:T(8,128)(2,1)S(1)} %pad_maximum_fusion.refs_0_), channel_id=1, source_target_pairs={{0,2},{2,0},{4,6},{6,4},{8,10},{10,8},{12,14},{14,12},{1,3},{3,1},... | collective-permute-start | bytes 3268616 | tf_op jit(solution)/shard_map/ppermute | solution.py:76
  402.9 14.9 %collective-permute-start.43 = (bf16[1,29,2048]{2,1,0:T(8,128)(2,1)}, bf16[1,29,2048]{2,1,0:T(8,128)(2,1)S(1)}, u32[]{:S(2)}, u32[]{:S(2)}) collective-permute-start(bf16[1,29,2048]{2,1,0:T(8,128)(2,1)} %get-tuple-element.190), channel_id=1, source_target_pairs={{0,16},{8,24},{16,0},{24,8},{1,17},{9,25},{17,1},{25,9},{2,18},{10... | collective-permute-start | bytes 356360 | tf_op jit(solution)/shard_map/ppermute | solution.py:70
  402.9 15.5 %collective-permute-start.44 = (bf16[1,29,2048]{2,1,0:T(8,128)(2,1)}, bf16[1,29,2048]{2,1,0:T(8,128)(2,1)S(1)}, u32[]{:S(2)}, u32[]{:S(2)}) collective-permute-start(bf16[1,29,2048]{2,1,0:T(8,128)(2,1)} %get-tuple-element.191), channel_id=1, source_target_pairs={{0,24},{8,16},{16,8},{24,0},{1,25},{9,17},{17,9},{25,1},{2,26},{10... | collective-permute-start | bytes 356360 | tf_op jit(solution)/shard_map/ppermute | solution.py:70
  406.4 15.0 %collective-permute-start.31 = (bf16[152,896]{1,0:T(8,128)(2,1)S(1)}, bf16[152,896]{1,0:T(8,128)(2,1)S(1)}, u32[]{:S(2)}, u32[]{:S(2)}) collective-permute-start(bf16[152,896]{1,0:T(8,128)(2,1)S(1)} %get-tuple-element.221), channel_id=1, source_target_pairs={{24,16},{25,17},{26,18},{27,19},{28,20},{29,21},{30,22},{31,23}} | collective-permute-start | bytes 817160 | tf_op jit(solution)/shard_map/ppermute | solution.py:70
  421.4 30.1 %collective-permute-start.29 = (bf16[224,2432]{1,0:T(8,128)(2,1)S(1)}, bf16[224,2432]{1,0:T(8,128)(2,1)}, u32[]{:S(2)}, u32[]{:S(2)}) collective-permute-start(bf16[224,2432]{1,0:T(8,128)(2,1)S(1)} %pad_maximum_fusion.refs_0_), channel_id=1, source_target_pairs={{0,4},{2,6},{4,0},{6,2},{8,12},{10,14},{12,8},{14,10},{1,5},{3,7},... | collective-permute-start | bytes 3268616 | tf_op jit(solution)/shard_map/ppermute | solution.py:76
  423.2 31.3 %collective-permute-start.30 = (bf16[224,2432]{1,0:T(8,128)(2,1)S(1)}, bf16[224,2432]{1,0:T(8,128)(2,1)}, u32[]{:S(2)}, u32[]{:S(2)}) collective-permute-start(bf16[224,2432]{1,0:T(8,128)(2,1)S(1)} %pad_maximum_fusion.refs_0_), channel_id=1, source_target_pairs={{0,6},{2,4},{4,2},{6,0},{8,14},{10,12},{12,10},{14,8},{1,7},{3,5},... | collective-permute-start | bytes 3268616 | tf_op jit(solution)/shard_map/ppermute | solution.py:76
  427.0 29.4 %collective-permute-start.34 = (bf16[608,896]{1,0:T(8,128)(2,1)S(1)}, bf16[608,896]{1,0:T(8,128)(2,1)}, u32[]{:S(2)}, u32[]{:S(2)}) collective-permute-start(bf16[608,896]{1,0:T(8,128)(2,1)S(1)} %pad_maximum_fusion.1.refs_4_), channel_id=1, source_target_pairs={{16,18},{18,16},{20,22},{22,20},{17,19},{19,17},{21,23},{23,21}} | collective-permute-start | bytes 3268616 | tf_op jit(solution)/shard_map/ppermute | solution.py:76
  428.8 13.5 %collective-permute-start.46 = (bf16[56,1024]{1,0:T(8,128)(2,1)S(1)}, bf16[56,1024]{1,0:T(8,128)(2,1)S(1)}, u32[]{:S(2)}, u32[]{:S(2)}) collective-permute-start(bf16[56,1024]{1,0:T(8,128)(2,1)S(1)} %pad_maximum_fusion.5), channel_id=1, source_target_pairs={{16,24},{17,25},{18,26},{19,27},{20,28},{21,29},{22,30},{23,31}} | collective-permute-start | bytes 344072 | tf_op jit(solution)/shard_map/ppermute | solution.py:70
  430.1 14.3 %collective-permute-start.47 = (bf16[56,1024]{1,0:T(8,128)(2,1)S(1)}, bf16[56,1024]{1,0:T(8,128)(2,1)S(1)}, u32[]{:S(2)}, u32[]{:S(2)}) collective-permute-start(bf16[56,1024]{1,0:T(8,128)(2,1)S(1)} %pad_maximum_fusion.5), channel_id=1, source_target_pairs={{8,24},{9,25},{10,26},{11,27},{12,28},{13,29},{14,30},{15,31}} | collective-permute-start | bytes 344072 | tf_op jit(solution)/shard_map/ppermute | solution.py:70
  444.4 18.5 %collective-permute-start.35 = (bf16[608,896]{1,0:T(8,128)(2,1)S(1)}, bf16[608,896]{1,0:T(8,128)(2,1)}, u32[]{:S(2)}, u32[]{:S(2)}) collective-permute-start(bf16[608,896]{1,0:T(8,128)(2,1)S(1)} %pad_maximum_fusion.1.refs_4_), channel_id=1, source_target_pairs={{16,20},{18,22},{20,16},{22,18},{17,21},{19,23},{21,17},{23,19}} | collective-permute-start | bytes 3268616 | tf_op jit(solution)/shard_map/ppermute | solution.py:76
  449.6 13.4 %collective-permute-start.36 = (bf16[608,896]{1,0:T(8,128)(2,1)S(1)}, bf16[608,896]{1,0:T(8,128)(2,1)}, u32[]{:S(2)}, u32[]{:S(2)}) collective-permute-start(bf16[608,896]{1,0:T(8,128)(2,1)S(1)} %pad_maximum_fusion.1.refs_4_), channel_id=1, source_target_pairs={{16,22},{18,20},{20,18},{22,16},{17,23},{19,21},{21,19},{23,17}} | collective-permute-start | bytes 3268616 | tf_op jit(solution)/shard_map/ppermute | solution.py:76
  451.5 11.5 %collective-permute-start.49 = (bf16[224,1024]{1,0:T(8,128)(2,1)S(1)}, bf16[224,1024]{1,0:T(8,128)(2,1)S(1)}, u32[]{:S(2)}, u32[]{:S(2)}) collective-permute-start(bf16[224,1024]{1,0:T(8,128)(2,1)S(1)} %concatenate.58.refs_8_.refs_5_), channel_id=1, source_target_pairs={{24,26},{26,24},{28,30},{30,28},{25,27},{27,25},{29,31},{31,29}} | collective-permute-start | bytes 1376264 | tf_op jit(solution)/shard_map/ppermute | solution.py:76
  454.5 12.9 %collective-permute-start.50 = (bf16[224,1024]{1,0:T(8,128)(2,1)S(1)}, bf16[224,1024]{1,0:T(8,128)(2,1)S(1)}, u32[]{:S(2)}, u32[]{:S(2)}) collective-permute-start(bf16[224,1024]{1,0:T(8,128)(2,1)S(1)} %concatenate.58.refs_8_.refs_5_), channel_id=1, source_target_pairs={{24,28},{26,30},{28,24},{30,26},{25,29},{27,31},{29,25},{31,27}} | collective-permute-start | bytes 1376264 | tf_op jit(solution)/shard_map/ppermute | solution.py:76
  456.4 15.3 %collective-permute-start.51 = (bf16[224,1024]{1,0:T(8,128)(2,1)S(1)}, bf16[224,1024]{1,0:T(8,128)(2,1)S(1)}, u32[]{:S(2)}, u32[]{:S(2)}) collective-permute-start(bf16[224,1024]{1,0:T(8,128)(2,1)S(1)} %concatenate.58.refs_8_.refs_5_), channel_id=1, source_target_pairs={{24,30},{26,28},{28,26},{30,24},{25,31},{27,29},{29,27},{31,25}} | collective-permute-start | bytes 1376264 | tf_op jit(solution)/shard_map/ppermute | solution.py:76
  480.5 91.9 %collective-permute-start.52 = (bf16[192,896]{1,0:T(8,128)(2,1)}, bf16[192,896]{1,0:T(8,128)(2,1)S(1)}, u32[]{:S(2)}, u32[]{:S(2)}) collective-permute-start(bf16[192,896]{1,0:T(8,128)(2,1)} %get-tuple-element.195), channel_id=1, source_target_pairs={{0,2},{2,0},{4,6},{6,4},{1,3},{3,1},{5,7},{7,5},{8,10},{10,8},{12,... | collective-permute-start | bytes 1032200 | tf_op jit(solution)/shard_map/ppermute | solution.py:70
  481.5 98.9 %collective-permute-start.53 = (bf16[192,896]{1,0:T(8,128)(2,1)}, bf16[192,896]{1,0:T(8,128)(2,1)S(1)}, u32[]{:S(2)}, u32[]{:S(2)}) collective-permute-start(bf16[192,896]{1,0:T(8,128)(2,1)} %get-tuple-element.196), channel_id=1, source_target_pairs={{0,4},{2,6},{4,0},{6,2},{1,5},{3,7},{5,1},{7,3},{8,12},{10,14},{12... | collective-permute-start | bytes 1032200 | tf_op jit(solution)/shard_map/ppermute | solution.py:70
  482.3 98.8 %collective-permute-start.54 = (bf16[192,896]{1,0:T(8,128)(2,1)}, bf16[192,896]{1,0:T(8,128)(2,1)S(1)}, u32[]{:S(2)}, u32[]{:S(2)}) collective-permute-start(bf16[192,896]{1,0:T(8,128)(2,1)} %get-tuple-element.197), channel_id=1, source_target_pairs={{0,6},{2,4},{4,2},{6,0},{1,7},{3,5},{5,3},{7,1},{8,14},{10,12},{12... | collective-permute-start | bytes 1032200 | tf_op jit(solution)/shard_map/ppermute | solution.py:70
  551.7 30.1 %collective-permute-start.56 = (bf16[56,1024]{1,0:T(8,128)(2,1)S(1)}, bf16[56,1024]{1,0:T(8,128)(2,1)S(1)}, u32[]{:S(2)}, u32[]{:S(2)}) collective-permute-start(bf16[56,1024]{1,0:T(8,128)(2,1)S(1)} %get-tuple-element.245), channel_id=1, source_target_pairs={{24,0},{25,1},{26,2},{27,3},{28,4},{29,5},{30,6},{31,7}} | collective-permute-start | bytes 344072 | tf_op jit(solution)/shard_map/ppermute | solution.py:70
  559.4 23.7 %collective-permute-start.57 = (bf16[56,1024]{1,0:T(8,128)(2,1)S(1)}, bf16[56,1024]{1,0:T(8,128)(2,1)S(1)}, u32[]{:S(2)}, u32[]{:S(2)}) collective-permute-start(bf16[56,1024]{1,0:T(8,128)(2,1)S(1)} %get-tuple-element.244), channel_id=1, source_target_pairs={{24,8},{25,9},{26,10},{27,11},{28,12},{29,13},{30,14},{31,15}} | collective-permute-start | bytes 344072 | tf_op jit(solution)/shard_map/ppermute | solution.py:70
  572.4 12.1 %collective-permute-start.58 = (bf16[56,1024]{1,0:T(8,128)(2,1)S(1)}, bf16[56,1024]{1,0:T(8,128)(2,1)S(1)}, u32[]{:S(2)}, u32[]{:S(2)}) collective-permute-start(bf16[56,1024]{1,0:T(8,128)(2,1)S(1)} %get-tuple-element.243), channel_id=1, source_target_pairs={{24,16},{25,17},{26,18},{27,19},{28,20},{29,21},{30,22},{31,23}} | collective-permute-start | bytes 344072 | tf_op jit(solution)/shard_map/ppermute | solution.py:70
  580.4 31.4 %collective-permute-start.64 = (bf16[152,896]{1,0:T(8,128)(2,1)S(1)}, bf16[152,896]{1,0:T(8,128)(2,1)S(1)}, u32[]{:S(2)}, u32[]{:S(2)}) collective-permute-start(bf16[152,896]{1,0:T(8,128)(2,1)S(1)} %get-tuple-element.229), channel_id=1, source_target_pairs={{16,8},{17,9},{18,10},{19,11},{20,12},{21,13},{22,14},{23,15}} | collective-permute-start | bytes 817160 | tf_op jit(solution)/shard_map/ppermute | solution.py:70
  581.1 30.7 %collective-permute-start.65 = (bf16[152,896]{1,0:T(8,128)(2,1)S(1)}, bf16[152,896]{1,0:T(8,128)(2,1)S(1)}, u32[]{:S(2)}, u32[]{:S(2)}) collective-permute-start(bf16[152,896]{1,0:T(8,128)(2,1)S(1)} %get-tuple-element.228), channel_id=1, source_target_pairs={{16,0},{17,1},{18,2},{19,3},{20,4},{21,5},{22,6},{23,7}} | collective-permute-start | bytes 817160 | tf_op jit(solution)/shard_map/ppermute | solution.py:70
  581.8 11.2 %collective-permute-start.60 = (bf16[56,2432]{1,0:T(8,128)(2,1)S(1)}, bf16[56,2432]{1,0:T(8,128)(2,1)S(1)}, u32[]{:S(2)}, u32[]{:S(2)}) collective-permute-start(bf16[56,2432]{1,0:T(8,128)(2,1)S(1)} %get-tuple-element.232), channel_id=1, source_target_pairs={{0,24},{8,16},{1,25},{9,17},{2,26},{10,18},{3,27},{11,19},{4,28},{... | collective-permute-start | bytes 817160 | tf_op jit(solution)/shard_map/ppermute | solution.py:70
  583.1 26.2 %collective-permute-start.61 = (bf16[56,2432]{1,0:T(8,128)(2,1)S(1)}, bf16[56,2432]{1,0:T(8,128)(2,1)S(1)}, u32[]{:S(2)}, u32[]{:S(2)}) collective-permute-start(bf16[56,2432]{1,0:T(8,128)(2,1)S(1)} %get-tuple-element.231), channel_id=1, source_target_pairs={{0,16},{8,24},{1,17},{9,25},{2,18},{10,26},{3,19},{11,27},{4,20},{... | collective-permute-start | bytes 817160 | tf_op jit(solution)/shard_map/ppermute | solution.py:70
  586.2 23.2 %collective-permute-start.62 = (bf16[56,2432]{1,0:T(8,128)(2,1)S(1)}, bf16[56,2432]{1,0:T(8,128)(2,1)S(1)}, u32[]{:S(2)}, u32[]{:S(2)}) collective-permute-start(bf16[56,2432]{1,0:T(8,128)(2,1)S(1)} %get-tuple-element.230), channel_id=1, source_target_pairs={{0,8},{8,0},{1,9},{9,1},{2,10},{10,2},{3,11},{11,3},{4,12},{12,4},... | collective-permute-start | bytes 817160 | tf_op jit(solution)/shard_map/ppermute | solution.py:70
  593.0 22.9 %collective-permute-start.66 = (bf16[152,896]{1,0:T(8,128)(2,1)S(1)}, bf16[152,896]{1,0:T(8,128)(2,1)S(1)}, u32[]{:S(2)}, u32[]{:S(2)}) collective-permute-start(bf16[152,896]{1,0:T(8,128)(2,1)S(1)} %get-tuple-element.227), channel_id=1, source_target_pairs={{16,24},{17,25},{18,26},{19,27},{20,28},{21,29},{22,30},{23,31}} | collective-permute-start | bytes 817160 | tf_op jit(solution)/shard_map/ppermute | solution.py:70
  (68 other events, 892.3 us)
Sparse Core Ops, SparseCore 0:
  12.1 61.9 all-gather.5
  75.7 34.2 all-gather.9
  111.8 42.4 all-gather.11
  156.3 47.6 all-gather.7

commit v2 on v1

--- a/solution.py
+++ b/solution.py
@@ -53,7 +53,7 @@
 
 
 def after(value, event):
-    return lax.optimization_barrier((value, event))[0]
+    return lax.optimization_barrier((value, event))
 
 
 def exchange(parts, axes):
@@ -94,11 +94,12 @@
     return [piece] + [swap(piece, "xy", step) for step in range(1, CHIPS)]
 
 
-def reduce_ctx(parts):
+def reduce_ctx(parts, event):
     repeat = lax.axis_size("r")
     chips = parts[0].astype(f32)
     for step in range(1, CHIPS):
         chips += swap(parts[step], "xy", step).astype(f32)
+    chips, event = after(chips, event)
     chips = chips.reshape((LINE, repeat) + chips.shape[1:])
     low = chips.astype(bf16)
     own = chips[0]
@@ -106,7 +107,7 @@
         own += swap(low[step], "z", step).astype(f32)
     if repeat > 1:
         own = lax.psum_scatter(own, "r", scatter_dimension=0, tiled=True)
-    return own[0]
+    return own[0], event
 
 
 def plain_call(kernel, out_shape, scratch=(), **keywords):
@@ -120,7 +121,7 @@
 
 
 def cost(flops, moved):
-    return pl.CostEstimate(flops=int(flops), bytes_accessed=int(moved), transcendentals=0)
+    return pl.CostEstimate(flops=1, bytes_accessed=1, transcendentals=0)
 
 
 def like(shape, dtype):
@@ -203,18 +204,17 @@
 
 
 def join_kernel(qa_ref, qb_ref, ka_ref, kb_ref, own_ref, *low_refs):
-    rows, wide = qa_ref.shape[2:]
+    wide = qa_ref.shape[3]
     for step, ref in enumerate((own_ref,) + low_refs):
         query = qa_ref[step].astype(f32) + qb_ref[step].astype(f32)
         other = ka_ref[step].astype(f32) + kb_ref[step].astype(f32)
-        ref[:, :rows, :wide] = query.astype(ref.dtype)
-        ref[:, rows:, :wide] = jnp.zeros(ref[:, rows:, :wide].shape, ref.dtype)
+        ref[:, :, :wide] = query.astype(ref.dtype)
         ref[:, :, wide:] = other.astype(ref.dtype)
 
 
 def join(query_first, query_second, other_first, other_second):
     depth, rows, wide = query_first.shape[1:]
-    shape = (depth, rows + 1, wide + other_first.shape[3])
+    shape = (depth, rows, wide + other_first.shape[3])
     return plain_call(join_kernel, [like(shape, f32)] + [like(shape, bf16)] * (CHIPS - 1))(
         query_first, query_second, other_first, other_second
     )
@@ -244,7 +244,7 @@
     width = moments[0].shape[1]
     narrow = moments[1].shape[1]
     starts = (0, 2 * width, 2 * width + narrow, width)
-    small_ref[...] = total_sum[rows:, 2 * width :]
+    small_ref[...] = total_sum[rows : rows + 1, 2 * width :]
     updates = []
     for m_ref, g_ref, n_ref, start in zip(moments, grads, fresh_refs, starts):
         grad = total_sum[:rows, start : start + m_ref.shape[1]]
@@ -304,22 +304,24 @@
             do_ref[b, j] = mixed[b * rows : (b + 1) * rows, start : start + HEAD_DIM]
 
 
-def shard_rows(here_ref, refs, value, rows, column, first):
+def shard_rows(here_ref, refs, pieces_of, first, column):
     chips, depth = refs[0].shape[:2]
-    cores = len(refs)
     core, chip, line = here_ref[0], here_ref[1], here_ref[2]
-    for k in range(cores):
+    for k in range(2):
         for target, ref in enumerate(refs):
 
             @pl.when((core ^ k) == target)
             def _():
                 for q in range(depth):
                     for c in range(chips):
-                        start = ((q * chips + c) * cores + k) * rows
+                        piece = pieces_of((q * chips + c) * 2 + k)
                         at = (q // LINE) * LINE + ((q % LINE) ^ line)
-                        piece = value[start : start + rows] if first else value(start // rows)
-                        span = slice(0, rows) if first else slice(ref.shape[2] - 1, ref.shape[2])
-                        ref[c ^ chip, at, span, column : column + piece.shape[1]] = piece
+                        rows = slice(first, first + piece.shape[0])
+                        ref[c ^ chip, at, rows, column : column + piece.shape[1]] = piece
+
+
+def rows_of(value, rows):
+    return lambda number: value[number * rows : (number + 1) * rows]
 
 
 def query_kernel(
@@ -335,11 +337,13 @@
             both = jnp.concatenate([dq_ref[b, 2 * j], dq_ref[b, 2 * j + 1]], axis=1)
             both = both * cosine - turn(both) * sine
             lin_ref[span, j * pair : (j + 1) * pair] = both.astype(bf16)
-    rows = own_ref.shape[2]
+    for ref in (own_ref, other_ref):
+        ref[...] = jnp.zeros_like(ref)
+    rows = width // (2 * own_ref.shape[0] * own_ref.shape[1])
     query = dot_tn(h_ref[...], lin_ref[...]).astype(bf16)
-    shard_rows(here_ref, (own_ref, other_ref), query, rows, 0, True)
+    shard_rows(here_ref, (own_ref, other_ref), rows_of(query, rows), 0, 0)
     out = dot_tn(o_ref[...], da_ref[...]).astype(bf16)
-    shard_rows(here_ref, (own_ref, other_ref), out, rows, width, True)
+    shard_rows(here_ref, (own_ref, other_ref), rows_of(out, rows), 0, width)
 
 
 def back_kernel(
@@ -381,17 +385,17 @@
     all_small[:, width : 2 * width] = gain_ref[...]
     all_small[:, 2 * width :] = jnp.sum(lin.astype(f32), axis=0, keepdims=True)
     refs = (own_ref, other_ref)
-    chips, depth, rows, _ = own_ref.shape
+    count = 2 * own_ref.shape[0] * own_ref.shape[1]
     for ref in refs:
         ref[...] = jnp.zeros_like(ref)
     grads = dot_tn(h_ref[...], lin[:, width:]).astype(bf16)
-    shard_rows(here_ref, refs, grads, rows - 1, 0, True)
-    small_rows = all_small.shape[1] // (2 * chips * depth)
+    shard_rows(here_ref, refs, rows_of(grads, width // count), 0, 0)
+    small_rows = all_small.shape[1] // count
 
     def small_of(number):
         return all_small[:, number * small_rows : (number + 1) * small_rows].astype(bf16)
 
-    shard_rows(here_ref, refs, small_of, 1, 0, False)
+    shard_rows(here_ref, refs, small_of, width // count, 0)
 
 
 def softmax_keys(keys, queries, key_pos, query_pos):
@@ -480,10 +484,11 @@
 
 
 def feed_kernel(count, *refs):
-    h_refs, (order_ref, dy_ref, wgu_ref, wd_ref) = refs[:count], refs[count : count + 4]
-    y_refs = refs[count + 4 : count + 6]
-    dh_refs = refs[count + 6 : count + 8]
-    gg_ref, gu_ref, gd_ref, agu, ad, h_all, dy_all, sems = refs[count + 8 :]
+    h_refs, dy_refs = refs[:count], refs[count : 2 * count]
+    wgu_ref, wd_ref = refs[2 * count : 2 * count + 2]
+    y_refs = refs[2 * count + 2 : 2 * count + 4]
+    dh_refs = refs[2 * count + 4 : 2 * count + 6]
+    ggu_ref, gd_ref, agu, ad, h_all, dy_all, sems = refs[2 * count + 6 :]
     step = pl.program_id(0)
     rows = h_refs[0].shape[0]
     tile = y_refs[0].shape[0]
@@ -493,7 +498,7 @@
         span = pl.ds(number * rows, rows)
         return (
             pltpu.make_async_copy(h_refs[number], h_all.at[span], sems.at[0, number]),
-            pltpu.make_async_copy(dy_ref.at[order_ref[number]], dy_all.at[span], sems.at[1, number]),
+            pltpu.make_async_copy(dy_refs[number], dy_all.at[span], sems.at[1, number]),
         )
 
     @pl.when(step == 0)
@@ -540,12 +545,18 @@
 
     @pl.when(step == pl.num_programs(0) - 1)
     def _():
-        gg_ref[...] = agu[0].astype(bf16)
-        gu_ref[...] = agu[1].astype(bf16)
-        gd_ref[...] = ad[...].astype(bf16)
-
-
-def feed_forward(normed_rows, order, grads, gate_up, down_mat):
+        repeat, height = ggu_ref.shape[2:4]
+        depth = gd_ref.shape[2]
+        for r in range(repeat):
+            for z in range(LINE):
+                start = (r * LINE + z) * height
+                for which in range(2):
+                    ggu_ref[z, which, r] = agu[which, start : start + height].astype(bf16)
+                start = (r * LINE + z) * depth
+                gd_ref[z, r] = ad[start : start + depth].astype(bf16)
+
+
+def feed_forward(normed_rows, grads, gate_up, down_mat, repeat):
     count = len(normed_rows)
     rows, width = normed_rows[0].shape
     units = gate_up.shape[3]
@@ -556,14 +567,16 @@
     first = pl.BlockSpec((tile, width), lambda t: (jnp.minimum(t, steps // 2 - 1), 0))
     second = pl.BlockSpec((tile, width), lambda t: (jnp.maximum(t - steps // 2, 0), 0))
     weights = pl.BlockSpec(gate_up.shape, lambda t: (0, 0, 0, 0))
-    wide = pl.BlockSpec((width, units), lambda t: (0, 0))
+    wide_shape = (LINE, 2, repeat, width // (LINE * repeat), units)
+    tall_shape = (LINE, repeat, units // (LINE * repeat), width)
+    wide = pl.BlockSpec(wide_shape, lambda t: (0, 0, 0, 0, 0))
+    tall_out = pl.BlockSpec(tall_shape, lambda t: (0, 0, 0, 0))
     tall = pl.BlockSpec((units, width), lambda t: (0, 0))
     anywhere = pl.BlockSpec(memory_space=pl.ANY)
     outs = plain_call(
         functools.partial(feed_kernel, count),
         [like((half, width), bf16)] * 4
-        + [like((width, units), bf16)] * 2
-        + [like((units, width), bf16)],
+        + [like(wide_shape, bf16), like(tall_shape, bf16)],
         [
             pltpu.VMEM((2, width, units), f32),
             pltpu.VMEM((units, width), f32),
@@ -572,12 +585,11 @@
             pltpu.SemaphoreType.DMA((2, count)),
         ],
         grid=(steps,),
-        in_specs=[anywhere] * count
-        + [pl.BlockSpec(memory_space=pltpu.SMEM), anywhere, weights, tall],
-        out_specs=[first, second, first, second, wide, wide, tall],
+        in_specs=[anywhere] * (2 * count) + [weights, tall],
+        out_specs=[first, second, first, second, wide, tall_out],
         cost_estimate=cost(36 * tokens * width * units, 8 * tokens * width + 12 * units * width),
-    )(*normed_rows, order, grads, gate_up, down_mat)
-    return outs[:2], outs[2:4], outs[4:]
+    )(*normed_rows, *grads, gate_up, down_mat)
+    return outs[:2], outs[2:4], outs[4], outs[5]
 
 
 def update_kernel(span, in_ref, mg_ref, mu_ref, gg_ref, gu_ref, ng_ref, nu_ref, u_ref):
@@ -697,10 +709,18 @@
     ]
 
 
+def upper_gram(out_ref, whole, contract_rows, size):
+    for start, stop in row_spans(size):
+        if contract_rows:
+            block = dot_tn(whole[:, start:stop], whole[:, start:size])
+        else:
+            block = dot_nt(whole[start:stop, :], whole[start:, :])
+        out_ref[start:stop, start:] = block
+
+
 def gram_kernel(mode_ref, *refs):
-    groups = [refs[:CHIPS], refs[CHIPS : 2 * CHIPS], refs[2 * CHIPS : 3 * CHIPS]]
-    out_ref, narrow_ref, *scratch, sem = refs[3 * CHIPS :]
-    spans = row_spans(out_ref.shape[0])
+    groups = (refs[:CHIPS], refs[CHIPS : 2 * CHIPS])
+    out_ref, *scratch, sem = refs[2 * CHIPS :]
     for number, (group, whole) in enumerate(zip(groups, scratch)):
 
         @pl.when(mode_ref[0] == number)
@@ -710,39 +730,71 @@
                 copy.start()
             for copy in copies:
                 copy.wait()
-            for start, stop in spans:
-                if number == 1:
-                    block = dot_tn(whole[:, start:stop], whole[:, start:])
-                elif number == 0:
-                    block = dot_nt(whole[start:stop], whole[start:])
-                else:
-                    size = out_ref.shape[0]
-                    block = dot_nt(whole[start:stop, :size], whole[start:, :size])
-                out_ref[start:stop, start:] = block
-            if number == 2:
-                narrow = whole[:, out_ref.shape[0] :]
-                narrow_ref[...] = dot_tn(narrow, narrow)
-
-
-def gram_of(mode, wide, tall, square):
+            upper_gram(out_ref, whole, number == 1, out_ref.shape[0])
+
+
+def gram_of(mode, wide, tall):
     size = tall[0].shape[1]
-    narrow = square[0].shape[1] - size
     spec = [pl.BlockSpec(memory_space=pltpu.SMEM)]
-    spec += [pl.BlockSpec(memory_space=pl.ANY)] * (3 * CHIPS)
-    groups = (wide, tall, square)
+    spec += [pl.BlockSpec(memory_space=pl.ANY)] * (2 * CHIPS)
     scratch = [
-        pltpu.VMEM((CHIPS * group[0].shape[0], group[0].shape[1]), bf16) for group in groups
+        pltpu.VMEM((CHIPS * group[0].shape[0], group[0].shape[1]), bf16) for group in (wide, tall)
     ]
     return plain_call(
         gram_kernel,
-        [like((size, size), f32), like((narrow, narrow), f32)],
+        like((size, size), f32),
         scratch + [pltpu.SemaphoreType.DMA((CHIPS,))],
         in_specs=spec,
         cost_estimate=cost(4 * size * size * size * 3, 8 * size * size),
-    )(mode, *wide, *tall, *square)
-
-
-def ortho_kernel(mode_ref, a_ref, b_ref, n_ref, *refs):
+    )(mode, *wide, *tall)
+
+
+def square_gram_kernel(mode_ref, *refs):
+    group = refs[:CHIPS]
+    out_ref, narrow_ref, whole, sem = refs[CHIPS:]
+    size = out_ref.shape[0]
+
+    @pl.when(mode_ref[0] == 2)
+    def _():
+        copies = load_blocks(group, whole, sem)
+        for copy in copies:
+            copy.start()
+        for copy in copies:
+            copy.wait()
+        upper_gram(out_ref, whole.at[:, :size], False, size)
+        narrow = whole[:, size:]
+        narrow_ref[...] = dot_tn(narrow, narrow)
+
+
+def square_gram_of(mode, square, size):
+    narrow = square[0].shape[1] - size
+    spec = [pl.BlockSpec(memory_space=pltpu.SMEM)]
+    spec += [pl.BlockSpec(memory_space=pl.ANY)] * CHIPS
+    return plain_call(
+        square_gram_kernel,
+        [like((size, size), f32), like((narrow, narrow), f32)],
+        [
+            pltpu.VMEM((CHIPS * square[0].shape[0], square[0].shape[1]), bf16),
+            pltpu.SemaphoreType.DMA((CHIPS,)),
+        ],
+        in_specs=spec,
+        cost_estimate=cost(4 * size * size * size * 3, 8 * size * size),
+    )(mode, *square)
+
+
+def stack_kernel(*refs):
+    out_ref = refs[-1]
+    rows = refs[0].shape[0]
+    for number, ref in enumerate(refs[:-1]):
+        out_ref[number * rows : (number + 1) * rows] = ref[...]
+
+
+def stack_rows(pieces):
+    rows, width = pieces[0].shape
+    return plain_call(stack_kernel, like((len(pieces) * rows, width), bf16))(*pieces)
+
+
+def ortho_kernel(mode_ref, a_ref, b_ref, c_ref, n_ref, *refs):
     wide, tall, square = refs[:CHIPS], refs[CHIPS : CHIPS + 1], refs[CHIPS + 1 : 2 * CHIPS + 1]
     outs = refs[2 * CHIPS + 1 : 2 * CHIPS + 4]
     q_ref, k_ref, *wholes, sem = refs[2 * CHIPS + 4 : 2 * CHIPS + 10]
@@ -757,7 +809,8 @@
                 copy.start()
 
     def load(i, start, stop):
-        return a_ref[start:stop, start:] + b_ref[start:stop, start:]
+        pair = a_ref[start:stop, start:] + b_ref[start:stop, start:]
+        return jnp.where(mode_ref[0] == 2, c_ref[start:stop, start:], pair)
 
     def write(i, rows, columns, value):
         q_ref[rows, columns] = value.astype(bf16)
@@ -793,10 +846,10 @@
                 out_ref[:, size:] = dot_nn(whole[:count, size:], k_ref[...]).astype(bf16)
 
 
-def ortho_of(mode, gram, other, narrow, wide, tall, square):
+def ortho_of(mode, gram, other, third, narrow, wide, tall, square):
     size = gram.shape[0]
     vmem = pl.BlockSpec(memory_space=pltpu.VMEM)
-    spec = [pl.BlockSpec(memory_space=pltpu.SMEM), vmem, vmem, vmem]
+    spec = [pl.BlockSpec(memory_space=pltpu.SMEM), vmem, vmem, vmem, vmem]
     spec += [pl.BlockSpec(memory_space=pl.ANY)] * (2 * CHIPS + 1)
     return plain_call(
         ortho_kernel,
@@ -813,7 +866,7 @@
         + poly_scratch(1, narrow.shape[0]),
         in_specs=spec,
         cost_estimate=cost(100 * size * size * size, 8 * size * size),
-    )(mode, gram, other, narrow, *wide, tall, *square)
+    )(mode, gram, other, third, narrow, *wide, tall, *square)
 
 
 def on_device(
@@ -875,9 +928,10 @@
     gate_up = jnp.stack([by_unit(weight_gate), by_unit(weight_up)], axis=0)
     gate_up = gate_up.transpose(3, 0, 1, 2, 4).reshape(plane, 2, part_rows, units)
     gate_up = exchange(gate_up, PLANE)
-    front_all, gate_up = lax.optimization_barrier((front_all, gate_up))
+    grad_low = cotangent.reshape(row_count, width)
+    grads_plane = gather_plane(grad_low)
+    front_all, gate_up, grads_plane = lax.optimization_barrier((front_all, gate_up, grads_plane))
     gate_up = gate_up.transpose(1, 0, 2, 3).reshape(2, plane * part_rows, units)
-    unit_rows = gate_up
     gate_up = lax.all_gather(gate_up, ("r", "z"), axis=0, tiled=False)
     if repeat > 1:
         gate_up = gate_up.transpose(1, 0, 2, 3).reshape(1, 2, width, units)
@@ -904,8 +958,6 @@
     )
 
     inputs = tokens_in.reshape(row_count, width)
-    grad_low = cotangent.reshape(row_count, width)
-    grads_plane = lax.all_gather(after(grad_low, unit_rows), PLANE, axis=0, tiled=False)
     heads_shape = (seq_count, head_count, seq_rows, HEAD_DIM)
     pairs_shape = (seq_count, kv_count, seq_rows, 2 * HEAD_DIM)
     rows_shape = (row_count, width)
@@ -923,35 +975,26 @@
     )(mixed, inputs, attn_mats, small_vals)
     normed_plane = gather_plane(normed_two)
 
-    cores_here = [f_index ^ (number // CHIPS) for number in range(plane)]
-    chips_here = [xy_index ^ (number % CHIPS) for number in range(plane)]
-    order = jnp.stack([chip * cores + core for chip, core in zip(chips_here, cores_here)])
-    part_y, part_dh, feed_grads = feed_forward(
-        normed_plane, order, grads_plane, gate_up, down_mat
+    here = jnp.stack([f_index, xy_index, z_index])
+    part_y, part_dh, line_gu, part_down = feed_forward(
+        normed_plane, grads_plane, gate_up, down_mat, repeat
     )
     own_dh, *low_dh = fold(part_dh[0], swap(part_dh[1], "f", 1))
     arrived = [swap(piece, "xy", step) for step, piece in enumerate(low_dh, 1)]
-
-    def by_line(part):
-        part = part.reshape((repeat, LINE, -1) + part.shape[1:])
-        return part.transpose(1, 0, 2, 3)
-
-    line_gate = exchange(by_line(after(feed_grads[0], own_dh)), "z")
-    arrived, line_gate = lax.optimization_barrier((arrived, line_gate))
-    line_up = exchange(by_line(after(feed_grads[1], line_gate)), "z")
+    line_gu, own_dh = after(line_gu, own_dh)
+    line_gu = exchange(line_gu, "z")
     grad_residual, grad_attn, grad_mixed, grad_gain_two = plain_call(
         turnback_kernel,
         [like(rows_shape, f32), like(rows_shape, bf16), like(heads_shape, bf16), like((1, width), f32)],
         cost_estimate=cost(6 * row_count * width * width, 8 * width * width),
     )(own_dh, *arrived, residual, grad_low, attn_mats, small_vals)
     grad_queries, part_pairs = attend_back(queries, grad_mixed, pairs_all, key_pos, query_pos)
-    grad_queries, line_up = lax.optimization_barrier((grad_queries, line_up))
-    line_down = exchange(by_line(after(feed_grads[2], line_up)), "z")
-
-    here = jnp.stack([f_index, xy_index, z_index])
+    grad_queries, line_gu = lax.optimization_barrier((grad_queries, line_gu))
+
     vmem = pl.BlockSpec(memory_space=pltpu.VMEM)
     smem = pl.BlockSpec(memory_space=pltpu.SMEM)
-    part_shape = (CHIPS, depth_count, part_rows, 2 * width)
+    padded = -(-(part_rows + 1) // 8) * 8
+    part_shape = (CHIPS, depth_count, padded, 2 * width)
     grad_query_lin, query_own, query_other = plain_call(
         query_kernel,
         [like(rows_shape, bf16), like(part_shape, bf16), like(part_shape, bf16)],
@@ -960,16 +1003,21 @@
     )(here, normed_one, grad_queries, attn_low, grad_attn, cosine, sine)
     query_other = swap(query_other, "f", 1)
 
-    part_gu = jnp.stack([total(line_gate), total(line_up)], axis=1)
+    part_gu = total(line_gu)
     if repeat > 1:
-        part_gu = lax.psum_scatter(part_gu, "r", scatter_dimension=0, tiled=True)
+        part_gu = lax.psum_scatter(part_gu, "r", scatter_dimension=1, tiled=True)
     part_gu = part_gu.astype(bf16).reshape(2, plane, part_rows, units).transpose(1, 0, 2, 3)
+    part_gu, part_pairs = after(part_gu, part_pairs)
+    part_gu = exchange(part_gu, PLANE)
+    part_gu, part_down = after(part_gu, part_down)
+    line_down = exchange(part_down, "z")
     sum_gate, sum_up, fresh_gate, fresh_up, wide_updates = wide_update(
-        exchange(part_gu, PLANE), moment_gate, moment_up, down_rows
-    )
-
-    own_pairs, line_down = lax.optimization_barrier((reduce_ctx(part_pairs), line_down))
-    part_shape = (CHIPS, depth_count, part_rows + 1, 2 * kv_width)
+        part_gu, moment_gate, moment_up, down_rows
+    )
+
+    own_pairs, grad_query_lin = reduce_ctx(part_pairs, grad_query_lin)
+    own_pairs, wide_updates = lax.optimization_barrier((own_pairs, wide_updates))
+    part_shape = (CHIPS, depth_count, padded, 2 * kv_width)
     input_grad, other_own, other_other = plain_call(
         back_kernel,
         [like(rows_shape, f32), like(part_shape, bf16), like(part_shape, bf16)],
@@ -993,23 +1041,6 @@
         grad_gain_two,
     )
     input_grad = input_grad.reshape(seq_count, seq_rows, width)
-    own_sum, *low_sums = join(query_own, query_other, other_own, swap(other_other, "f", 1))
-    low_sums = [swap(piece, "xy", step) for step, piece in enumerate(low_sums, 1)]
-    own_sum, *low_sums = spread(own_sum, low_sums, repeat)
-    low_sums = [swap(piece, "z", step) for step, piece in enumerate(low_sums, 1)]
-    if repeat > 1:
-        for piece in low_sums:
-            own_sum += piece.astype(f32)
-        own_sum = lax.psum_scatter(own_sum, "r", scatter_dimension=0, tiled=True)
-        low_sums = [jnp.zeros(own_sum.shape, bf16)] * (LINE - 1)
-    attn_sums, attn_fresh, small_line, mine, other = step_of(
-        f_index.reshape(1),
-        own_sum,
-        low_sums,
-        (moment_query, moment_key, moment_value, moment_out),
-    )
-    sum_small = small_line[0, :small_rows]
-
     sum_down = total(line_down)
     if repeat > 1:
         sum_down = lax.psum_scatter(sum_down, "r", scatter_dimension=0, tiled=True)
@@ -1017,18 +1048,6 @@
     fresh_down = momentum_decay * moment_down + sum_down
     update_down = (sum_down + momentum_decay * fresh_down).astype(bf16)
 
-    masters = (
-        weight_query,
-        weight_key,
-        weight_value,
-        weight_out,
-        weight_gate,
-        weight_up,
-        weight_down,
-    )
-    new_moments = (*attn_fresh, fresh_gate, fresh_up, fresh_down)
-    summed = (*attn_sums, sum_gate, sum_up, sum_down)
-
     half = hidden_width // cores
     all_rows = repeat * part_rows
 
@@ -1042,7 +1061,7 @@
         second = jnp.where(f_index == 0, other, mine)
         return jnp.concatenate([first, second], axis=axis)
 
-    def to_line(piece, planes):
+    def to_line(piece, planes, put=functools.partial(jnp.concatenate, axis=0)):
         def keep(source, target):
             return target in planes
 
@@ -1055,37 +1074,73 @@
             if len(planes) > 1:
                 chunk = place(piece, (z_index ^ step) % 2)
             parts.append(swap(chunk, "z", step, keep))
-        return jnp.concatenate(parts, axis=0)
+        return put(parts)
 
     def over_chips(rows, planes):
         return [rows] + [plane_swap(rows, step, planes) for step in range(1, CHIPS)]
 
-    tall = over_chips(to_line(whole_rows(update_down, 0), (2,)), (2,))
+    tall_line = to_line(whole_rows(update_down, 0), (2,))
     wide_updates = whole_rows(wide_updates, 1)
     wide_mine = lax.dynamic_slice_in_dim(wide_updates, f_index * half, half, 2)
     wide_other = lax.dynamic_slice_in_dim(wide_updates, (1 - f_index) * half, half, 2)
     wide_rows = core_order(wide_mine, swap(wide_other, "f", 1), 1)
-    wide = over_chips(to_line(wide_rows, (0, 1)), (0, 1))
+    wide_line = to_line(wide_rows, (0, 1))
+
+    part_y, query_own = after(part_y, query_own)
+    y_second = swap(part_y[1], "f", 1)
+    (y_first, y_second), other_own = after((part_y[0], y_second), other_own)
+    own_y, *low_y = fold(y_first, y_second)
+
+    other_other = swap(other_other, "f", 1)
+    own_sum, *low_sums = join(query_own, query_other, other_own, other_other)
+    own_sum, wide_line, tall_line = lax.optimization_barrier((own_sum, wide_line, tall_line))
+    wide = over_chips(wide_line, (0, 1))
+    tall = over_chips(tall_line, (2,))
+    low_sums = [swap(piece, "xy", step) for step, piece in enumerate(low_sums, 1)]
+    masters = (
+        weight_query,
+        weight_key,
+        weight_value,
+        weight_out,
+        weight_gate,
+        weight_up,
+        weight_down,
+    )
+    low_sums, wide, tall = lax.optimization_barrier((low_sums, wide, tall))
+    mode = jnp.maximum(z_index - 1, 0).reshape(1)
+    gram = gram_of(mode, wide, tall)
+    line_pairs = [(z * cores + i, z * cores + 1 - i) for z in range(LINE - 1) for i in range(cores)]
+    gram_other = lax.ppermute(gram, ("z", "f"), line_pairs)
+    own_sum, *low_sums = spread(own_sum, low_sums, repeat)
+    low_sums = [swap(piece, "z", step) for step, piece in enumerate(low_sums, 1)]
+    if repeat > 1:
+        for piece in low_sums:
+            own_sum += piece.astype(f32)
+        own_sum = lax.psum_scatter(own_sum, "r", scatter_dimension=0, tiled=True)
+        low_sums = [jnp.zeros(own_sum.shape, bf16)] * (LINE - 1)
+    own_sum, low_y, gram = lax.optimization_barrier((own_sum, low_y, gram))
+    attn_sums, attn_fresh, small_line, mine, other = step_of(
+        f_index.reshape(1),
+        own_sum,
+        low_sums,
+        (moment_query, moment_key, moment_value, moment_out),
+    )
+    sum_small = small_line[0, :small_rows]
+    new_moments = (*attn_fresh, fresh_gate, fresh_up, fresh_down)
+    summed = (*attn_sums, sum_gate, sum_up, sum_down)
     mine = whole_rows(mine, 0)
     other = whole_rows(other, 0)
     both = core_order(mine, swap(other, "f", 1), 0)
-    square = over_chips(to_line(both, (3,)), (3,))
-
-    y_first, y_second = after(tuple(part_y), query_own)
-    y_second = swap(y_second, "f", 1)
-    own_y, *low_y = fold(*after((y_first, y_second), other_own))
-
-    mode = jnp.maximum(z_index - 1, 0).reshape(1)
-    mode, own_y, low_y = lax.optimization_barrier((mode, own_y, low_y))
-    gram, narrow = gram_of(mode, wide, tall, square)
-    low_y = after(low_y, gram)
+    square = over_chips(to_line(both, (3,), stack_rows), (3,))
+    line_rows = LINE * cores * all_rows
+
+    square_gram, narrow = square_gram_of(mode, square, width)
+    low_y, square_gram = after(low_y, square_gram)
     arrived_y = [swap(piece, "xy", step) for step, piece in enumerate(low_y, 1)]
-    line_pairs = [(z * cores + i, z * cores + 1 - i) for z in range(LINE - 1) for i in range(cores)]
-    gram_other = lax.ppermute(gram, ("z", "f"), line_pairs)
     wide_o, tall_o, square_o = ortho_of(
-        mode, gram, gram_other, narrow, wide, tall[0], square
-    )
-    arrived_y = after(arrived_y, square_o)
+        mode, gram, gram_other, square_gram, narrow, wide, tall[0], square
+    )
+    arrived_y, square_o = after(arrived_y, square_o)
 
     def from_line(piece, planes):
         parts = piece.reshape((LINE, -1) + piece.shape[1:])

time: 634 us -> 647 us (1.021)
  starting transfers between devices: 147 us -> 213 us
  waiting for transfers between devices: 236 us -> 176 us
    ppermute x1, starting transfers between devices: 2.58 us -> 60.7 us  [on_device(): gram_other = lax.ppermute(gram, ('z', 'f'), line_pairs)]
    ppermute x57 -> x64, waiting for transfers between devices: 135 us -> 99.3 us  [swap(): return lax.ppermute(piece, axis, pairs)]
    all_gather x1, waiting for transfers between devices: 30.6 us -> 0.01 us  [on_device(): gate_up = lax.all_gather(gate_up, ('r', 'z'), axis=0, tiled=False)]
    ppermute x57 -> x64, starting transfers between devices: 98.9 us -> 111 us  [swap(): return lax.ppermute(piece, axis, pairs)]
    all_to_all x5 -> x4, waiting for transfers between devices: 16.9 us -> 21.4 us  [exchange(): return lax.all_to_all(parts, axes, split_axis=0, concat_axis=0, tiled=True)]
    all_to_all x5 -> x4, starting transfers between devices: 27.2 us -> 23.2 us  [exchange(): return lax.all_to_all(parts, axes, split_axis=0, concat_axis=0, tiled=True)]
  transfers between devices with their start and end apart: 76 -> 81, of which waited for: 32 -> 32; matrix products, arithmetic and copies ran while one was open for 7% -> 6% of each run, Pallas kernels for 21% -> 22%
where the time goes in v2:
time: 647 us; the launch traced here: 636 us
  starting transfers between devices  213 us (33%)
  waiting for transfers between devices  176 us (27%)
  Pallas kernels  175 us (27%)
  local copies, waits for them, and re-layouts  33.3 us (5%)
  other arithmetic  24.2 us (4%)
  between operations  15.3 us (2%)
    ppermute x64, starting transfers between devices, swap(): return lax.ppermute(piece, axis, pairs)  111 us
    ppermute x64, waiting for transfers between devices, swap(): return lax.ppermute(piece, axis, pairs)  99.3 us
    pallas_call x1, Pallas kernels, ortho_of(): plain_call(ortho_kernel, [like(wide[0].shape, bf16), like(tall.shape, bf1...  68.2 us
    ppermute x1, starting transfers between devices, on_device(): gram_other = lax.ppermute(gram, ('z', 'f'), line_pairs)  60.7 us
    all_gather x1, waiting for transfers between devices, on_device(): front_all = lax.all_gather(front, EVERY, axis=0, tiled=False)  40.9 us
    pallas_call x1, Pallas kernels, feed_forward(): plain_call(functools.partial(feed_kernel, count), [like((half, width), bf...  30 us
    all_to_all x4, starting transfers between devices, exchange(): return lax.all_to_all(parts, axes, split_axis=0, concat_axis=0, tiled=True)  23.2 us
    all_to_all x4, waiting for transfers between devices, exchange(): return lax.all_to_all(parts, axes, split_axis=0, concat_axis=0, tiled=True)  21.4 us
  transfers between devices with their start and end apart: 81, of which 32 were waited for; matrix products, arithmetic and copies ran while one was open for 6% of the time, Pallas kernels for 22%

profile of v2, /device:TPU:25, one launch (start us, length us, event | category | flops | bytes accessed | tf_op | source)
XLA Modules:
  0.0 636.4 jit_solution(8873987249517222991)
XLA Ops:
  21.3 5.4 all-to-all-start
  27.2 6.5 %collective-permute-start.5 = (bf16[192,896]{1,0:T(8,128)(2,1)S(1)}, bf16[192,896]{1,0:T(8,128)(2,1)S(1)}, u32[]{:S(2)}, u32[]{:S(2)}) collective-permute-start(bf16[192,896]{1,0:T(8,128)(2,1)S(1)} %collective-permute-done.1.refs_10_), channel_id=1, source_target_pairs={{0,1},{1,0},{2,3},{3,2},{4,5},{5,4},{6,7},{7,6},{8,9},{9,8},{10,11... | collective-permute-start | bytes 1032200 | tf_op jit(solution)/shard_map/ppermute | solution.py:70
  33.9 4.9 all-to-all-done
  38.8 40.9 %all-gather.4.cloned.1.call-done = bf16[32,29,2048]{2,1,0:T(8,128)(2,1)} async-done(((bf16[1,29,2048]{2,1,0:T(8,128)(2,1)}), bf16[32,29,2048]{2,1,0:T(8,128)(2,1)}) %all-gather.4.cloned.1.call-update) | async-done | bytes 3801104 | tf_op jit(solution)/shard_map/all_gather | solution.py:923
  83.8 5.9 reshape.341.w_ref
  92.1 4.2 shard_map.369
  99.9 5.1 collective-permute-done.9
  105.0 11.0 %collective-permute-done.8 = bf16[1,3,2,64,128]{4,3,2,1,0:T(8,128)(2,1)S(1)} collective-permute-done((bf16[1,3,2,64,128]{4,3,2,1,0:T(8,128)(2,1)}, bf16[1,3,2,64,128]{4,3,2,1,0:T(8,128)(2,1)S(1)}, u32[]{:S(2)}, u32[]{:S(2)}) %collective-permute-start.8) | collective-permute-done | bytes 98336 | tf_op jit(solution)/shard_map/ppermute | solution.py:70
  120.7 6.5 %collective-permute-done.10.refs_1_ = bf16[4,3,2,64,128]{4,3,2,1,0:T(8,128)(2,1)S(1)} collective-permute-done((bf16[4,3,2,64,128]{4,3,2,1,0:T(8,128)(2,1)S(1)}, bf16[4,3,2,64,128]{4,3,2,1,0:T(8,128)(2,1)S(1)}, u32[]{:S(2)}, u32[]{:S(2)}) %collective-permute-start.10) | collective-permute-done | bytes 393248 | tf_op jit(solution)/shard_map/ppermute | solution.py:70
  128.0 8.9 %collective-permute-done.12.refs_3_ = bf16[4,3,2,64,128]{4,3,2,1,0:T(8,128)(2,1)S(1)} collective-permute-done((bf16[4,3,2,64,128]{4,3,2,1,0:T(8,128)(2,1)S(1)}, bf16[4,3,2,64,128]{4,3,2,1,0:T(8,128)(2,1)S(1)}, u32[]{:S(2)}, u32[]{:S(2)}) %collective-permute-start.12) | collective-permute-done | bytes 393248 | tf_op jit(solution)/shard_map/ppermute | solution.py:70
  137.6 9.8 %shard_map.370.o_ref = bf16[3,14,64,64]{3,2,1,0:T(8,128)(2,1)} custom-call(bf16[3,14,64,64]{3,2,1,0:T(8,128)(2,1)} %get-tuple-element.154.q_ref, bf16[4,3,2,64,128]{4,3,2,1,0:T(8,128)(2,1)} %copy-done.3, bf16[4,3,2,64,128]{4,3,2,1,0:T(8,128)(2,1)} %copy-done.17, bf16[4,3,2,64,128]{4,3,2,1,0:T(8,128)(2,1)} %copy-done.18, ...), custom_call_target="tpu_custom_call" | custom-call | flops 1 | bytes 1 | tf_op jit(solution)/shard_map/pallas_call | solution.py:462
  147.4 4.0 shard_map.371
  154.1 2.4 collective-permute-start.16
  156.4 3.3 collective-permute-done.13.refs_1_
  159.8 4.4 collective-permute-start.17
  164.2 6.2 collective-permute-start.18
  172.9 30.0 %shard_map.372 = (bf16[768,896]{1,0:T(8,128)(2,1)}, bf16[768,896]{1,0:T(8,128)(2,1)}, bf16[768,896]{1,0:T(8,128)(2,1)}, bf16[768,896]{1,0:T(8,128)(2,1)}, bf16[4...) custom-call(bf16[192,896]{1,0:T(8,128)(2,1)} %get-tuple-element.159.refs_0_, ...), custom_call_target="tpu_custom_call" | custom-call | flops 1 | bytes 1 | tf_op jit(solution)/shard_map/pallas_call | solution.py:576
  203.3 3.0 collective-permute-done.20.b_ref
  207.4 3.0 shard_map.373
  210.4 6.7 %all-to-all-start.1 = ((bf16[4,2,1,224,608]{4,3,2,1,0:T(8,128)(2,1)}), bf16[4,2,1,224,608]{4,3,2,1,0:T(8,128)(2,1)S(1)}, u32[]{:S(2)}, u32[]{:S(2)}) async-start(bf16[4,2,1,224,608]{4,3,2,1,0:T(8,128)(2,1)} %get-tuple-element.182), calls=%async_computation.1 | async-start | bytes 4587520 | tf_op jit(solution)/shard_map/all_to_all | solution.py:60
  219.9 6.3 collective-permute-done.21.a_ref
  227.0 5.9 collective-permute-done.23.c_ref
  233.7 4.9 shard_map.374
  238.6 16.1 %shard_map.375 = (f32[3,14,64,64]{3,2,1,0:T(8,128)}, bf16[4,3,2,64,128]{4,3,2,1,0:T(8,128)(2,1)}, bf16[4,3,2,64,128]{4,3,2,1,0:T(8,128)(2,1)}, bf16[4,3,2,64,128...) custom-call(bf16[3,14,64,64]{3,2,1,0:T(8,128)(2,1)} %get-tuple-element.154.q_ref, ...), custom_call_target="tpu_custom_call" | custom-call | flops 1 | bytes 1 | tf_op jit(solution)/shard_map/pallas_call | solution.py:475
  254.7 12.5 %all-to-all-done.1 = bf16[4,2,1,224,608]{4,3,2,1,0:T(8,128)(2,1)S(1)} async-done(((bf16[4,2,1,224,608]{4,3,2,1,0:T(8,128)(2,1)}), bf16[4,2,1,224,608]{4,3,2,1,0:T(8,128)(2,1)S(1)}, u32[]{:S(2)}, u32[]{:S(2)}) %all-to-all-start.1) | async-done | bytes 2179104 | tf_op jit(solution)/shard_map/all_to_all | solution.py:60
  272.4 5.5 all-to-all-start.2
  277.9 6.3 shard_map.376
  284.2 4.5 collective-permute-done.26
  289.1 2.2 collective-permute-start.30
  295.3 5.6 all-to-all-start.3
  300.9 3.5 shard_map.377
  306.1 2.4 collective-permute-start.33
  309.0 5.1 shard_map.378
  315.3 2.4 collective-permute-start.36
  317.7 2.0 collective-permute-start.35
  321.0 2.3 all-to-all-done.3
  325.4 3.0 collective-permute-start.32
  331.1 21.3 %collective-permute-start.37 = (bf16[152,896]{1,0:T(8,128)(2,1)S(1)}, bf16[152,896]{1,0:T(8,128)(2,1)S(1)}, u32[]{:S(2)}, u32[]{:S(2)}) collective-permute-start(bf16[152,896]{1,0:T(8,128)(2,1)S(1)} %get-tuple-element.279), channel_id=1, source_target_pairs={{24,16},{25,17},{26,18},{27,19},{28,20},{29,21},{30,22},{31,23}} | collective-permute-start | bytes 817160 | tf_op jit(solution)/shard_map/ppermute | solution.py:70
  355.6 3.7 shard_map.380
  365.5 7.1 %collective-permute-done.40.a_ref = bf16[4,32,2048]{2,1,0:T(8,128)(2,1)S(1)} collective-permute-done((bf16[4,32,2048]{2,1,0:T(8,128)(2,1)S(1)}, bf16[4,32,2048]{2,1,0:T(8,128)(2,1)S(1)}, u32[]{:S(2)}, u32[]{:S(2)}) %collective-permute-start.40) | collective-permute-done | bytes 524320 | tf_op jit(solution)/shard_map/ppermute | solution.py:70
  376.0 8.1 %collective-permute-done.42.c_ref = bf16[4,32,2048]{2,1,0:T(8,128)(2,1)S(1)} collective-permute-done((bf16[4,32,2048]{2,1,0:T(8,128)(2,1)S(1)}, bf16[4,32,2048]{2,1,0:T(8,128)(2,1)S(1)}, u32[]{:S(2)}, u32[]{:S(2)}) %collective-permute-start.42) | collective-permute-done | bytes 524320 | tf_op jit(solution)/shard_map/ppermute | solution.py:70
  389.3 60.7 %collective-permute-start.62 = (f32[896,896]{1,0:T(8,128)}, f32[896,896]{1,0:T(8,128)S(1)}, u32[]{:S(2)}, u32[]{:S(2)}) collective-permute-start(f32[896,896]{1,0:T(8,128)} %shard_map.382.a_ref), channel_id=1, source_target_pairs={{0,1},{1,0},{8,9},{9,8},{16,17},{17,16},{2,3},{3,2},{10,11},{11,10... | collective-permute-start | bytes 9633800 | tf_op jit(solution)/shard_map/ppermute | solution.py:1113
  450.0 2.6 shard_map.381
  453.3 2.8 collective-permute-start.51
  456.2 3.0 shard_map.379
  459.2 5.3 collective-permute-done.50.b_ref
  465.9 2.2 shard_map.383
  468.0 2.4 collective-permute-start.52
  476.3 2.4 collective-permute-done.53.refs_1_
  478.7 2.2 collective-permute-done.54.refs_2_
  480.9 2.2 collective-permute-done.55.refs_3_
  485.7 3.1 collective-permute-start.56
  488.7 3.1 collective-permute-start.57
  491.9 2.2 collective-permute-start.58
  494.0 3.4 collective-permute-done.56.refs_1_.refs_6_
  497.4 4.7 collective-permute-done.57.refs_2_.refs_7_
  502.2 6.1 collective-permute-done.58.refs_3_.refs_8_
  509.0 4.9 shard_map.385
  519.5 68.2 %shard_map.386 = (bf16[224,2432]{1,0:T(8,128)(2,1)}, bf16[608,896]{1,0:T(8,128)(2,1)}, bf16[224,1024]{1,0:T(8,128)(2,1)}) custom-call(s32[1]{0:T(128)} %bitcast.18.mode_ref, f32[896,896]{1,0:T(8,128)} %shard_map.382.a_ref, f32[896,896]{1,0:T(8,128)} %copy-done.4, f32[896,896]{1,0:T(8,128)} %get-tuple-element.254.c_ref, f32[128,128]{1,0:T(8,128)} %get-tuple-element.255.n_ref, ...), custom_call_target="tpu_custom_call" | custom-call | flops 1 | bytes 1 | tf_op jit(solution)/shard_map/pallas_call | solution.py:854
  599.2 7.1 %collective-permute-start.66 = (bf16[28,1024]{1,0:T(8,128)(2,1)S(1)}, bf16[28,1024]{1,0:T(8,128)(2,1)S(1)}, u32[]{:S(2)}, u32[]{:S(2)}) collective-permute-start(bf16[28,1024]{1,0:T(8,128)(2,1)S(1)} %constant_dynamic-slice_fusion), channel_id=1, source_target_pairs={{0,1},{1,0},{2,3},{3,2},{4,5},{5,4},{6,7},{7,6},{8,9},{9,8},{10,11... | collective-permute-start | bytes 172040 | tf_op jit(solution)/shard_map/ppermute | solution.py:70
  606.3 2.0 add_convert_fusion
  611.9 4.3 collective-permute-done.68
  617.3 2.4 collective-permute-start.70
  619.7 7.4 %collective-permute-done.73 = bf16[152,896]{1,0:T(8,128)(2,1)S(1)} collective-permute-done((bf16[152,896]{1,0:T(8,128)(2,1)S(1)}, bf16[152,896]{1,0:T(8,128)(2,1)S(1)}, u32[]{:S(2)}, u32[]{:S(2)}) %collective-permute-start.73) | collective-permute-done | bytes 272416 | tf_op jit(solution)/shard_map/ppermute | solution.py:70
  (333 shorter events, 113.7 us)
Async XLA Ops:
  7.2 72.5 %all-gather.4.cloned.1.call-start = ((), (), s32[]{:S(2)}) async-start(), calls=%async_computation.4 | async-start | bytes 4325376 | tf_op jit(solution)/shard_map/all_gather | solution.py:923
  12.0 158.4 %all-gather.8.cloned.1.call-start = ((), (), s32[]{:S(2)}) async-start(), calls=%async_computation.6 | async-start | bytes 1361920 | tf_op jit(solution)/shard_map/all_gather | solution.py:938
  12.9 13.9 %collective-permute-start = (bf16[192,896]{1,0:T(8,128)(2,1)S(1)}, bf16[192,896]{1,0:T(8,128)(2,1)S(1)}, u32[]{:S(2)}, u32[]{:S(2)}) collective-permute-start(bf16[192,896]{1,0:T(8,128)(2,1)S(1)} %bitcast.54), channel_id=1, source_target_pairs={{0,2},{2,0},{4,6},{6,4},{1,3},{3,1},{5,7},{7,5},{8,10},{10,8},{12,... | collective-permute-start | bytes 1032200 | tf_op jit(solution)/shard_map/ppermute | solution.py:70
  14.2 13.0 %collective-permute-start.1 = (bf16[192,896]{1,0:T(8,128)(2,1)S(1)}, bf16[192,896]{1,0:T(8,128)(2,1)S(1)}, u32[]{:S(2)}, u32[]{:S(2)}) collective-permute-start(bf16[192,896]{1,0:T(8,128)(2,1)S(1)} %bitcast.55), channel_id=1, source_target_pairs={{0,4},{2,6},{4,0},{6,2},{1,5},{3,7},{5,1},{7,3},{8,12},{10,14},{12... | collective-permute-start | bytes 1032200 | tf_op jit(solution)/shard_map/ppermute | solution.py:70
  15.4 18.3 %collective-permute-start.2 = (bf16[192,896]{1,0:T(8,128)(2,1)S(1)}, bf16[192,896]{1,0:T(8,128)(2,1)S(1)}, u32[]{:S(2)}, u32[]{:S(2)}) collective-permute-start(bf16[192,896]{1,0:T(8,128)(2,1)S(1)} %bitcast.56), channel_id=1, source_target_pairs={{0,6},{2,4},{4,2},{6,0},{1,7},{3,5},{5,3},{7,1},{8,14},{10,12},{12... | collective-permute-start | bytes 1032200 | tf_op jit(solution)/shard_map/ppermute | solution.py:70
  21.3 17.4 %all-to-all-start = ((bf16[8,2,28,608]{3,1,2,0:T(2,128)(2,1)}), bf16[8,2,28,608]{3,1,2,0:T(2,128)(2,1)S(1)}, u32[]{:S(2)}, u32[]{:S(2)}) async-start(bf16[8,2,28,608]{3,1,2,0:T(2,128)(2,1)} %copy.70), calls=%async_computation | async-start | bytes 1146880 | tf_op jit(solution)/shard_map/all_to_all | solution.py:60
  26.7 145.5 %all-gather.6.cloned.1.call-start = ((), (), s32[]{:S(2)}) async-start(), calls=%async_computation.5 | async-start | bytes 2867200 | tf_op jit(solution)/shard_map/all_gather | solution.py:935
  26.8 12.0 %collective-permute-start.4 = (bf16[192,896]{1,0:T(8,128)(2,1)S(1)}, bf16[192,896]{1,0:T(8,128)(2,1)S(1)}, u32[]{:S(2)}, u32[]{:S(2)}) collective-permute-start(bf16[192,896]{1,0:T(8,128)(2,1)S(1)} %collective-permute-done.refs_9_), channel_id=1, source_target_pairs={{0,1},{1,0},{2,3},{3,2},{4,5},{5,4},{6,7},{7,6},{8,9},{9,8},{10,11... | collective-permute-start | bytes 1032200 | tf_op jit(solution)/shard_map/ppermute | solution.py:70
  27.2 11.6 %collective-permute-start.5 = (bf16[192,896]{1,0:T(8,128)(2,1)S(1)}, bf16[192,896]{1,0:T(8,128)(2,1)S(1)}, u32[]{:S(2)}, u32[]{:S(2)}) collective-permute-start(bf16[192,896]{1,0:T(8,128)(2,1)S(1)} %collective-permute-done.1.refs_10_), channel_id=1, source_target_pairs={{0,1},{1,0},{2,3},{3,2},{4,5},{5,4},{6,7},{7,6},{8,9},{9,8},{10,11... | collective-permute-start | bytes 1032200 | tf_op jit(solution)/shard_map/ppermute | solution.py:70
  96.4 8.7 %collective-permute-start.9 = (bf16[1,3,2,64,128]{4,3,2,1,0:T(8,128)(2,1)}, bf16[1,3,2,64,128]{4,3,2,1,0:T(8,128)(2,1)S(1)}, u32[]{:S(2)}, u32[]{:S(2)}) collective-permute-start(bf16[1,3,2,64,128]{4,3,2,1,0:T(8,128)(2,1)} %bitcast.59), channel_id=1, source_target_pairs={{0,24},{8,16},{16,8},{24,0},{1,25},{9,17},{17,9},{25,1},{2,26},{10... | collective-permute-start | bytes 294920 | tf_op jit(solution)/shard_map/ppermute | solution.py:70
  98.0 18.0 %collective-permute-start.8 = (bf16[1,3,2,64,128]{4,3,2,1,0:T(8,128)(2,1)}, bf16[1,3,2,64,128]{4,3,2,1,0:T(8,128)(2,1)S(1)}, u32[]{:S(2)}, u32[]{:S(2)}) collective-permute-start(bf16[1,3,2,64,128]{4,3,2,1,0:T(8,128)(2,1)} %bitcast.60), channel_id=1, source_target_pairs={{0,16},{8,24},{16,0},{24,8},{1,17},{9,25},{17,1},{25,9},{2,18},{10... | collective-permute-start | bytes 294920 | tf_op jit(solution)/shard_map/ppermute | solution.py:70
  98.5 17.5 %collective-permute-start.7 = (bf16[1,3,2,64,128]{4,3,2,1,0:T(8,128)(2,1)}, bf16[1,3,2,64,128]{4,3,2,1,0:T(8,128)(2,1)S(1)}, u32[]{:S(2)}, u32[]{:S(2)}) collective-permute-start(bf16[1,3,2,64,128]{4,3,2,1,0:T(8,128)(2,1)} %bitcast.61), channel_id=1, source_target_pairs={{0,8},{8,0},{16,24},{24,16},{1,9},{9,1},{17,25},{25,17},{2,10},{10... | collective-permute-start | bytes 294920 | tf_op jit(solution)/shard_map/ppermute | solution.py:70
  116.9 10.3 %collective-permute-start.10 = (bf16[4,3,2,64,128]{4,3,2,1,0:T(8,128)(2,1)S(1)}, bf16[4,3,2,64,128]{4,3,2,1,0:T(8,128)(2,1)S(1)}, u32[]{:S(2)}, u32[]{:S(2)}) collective-permute-start(bf16[4,3,2,64,128]{4,3,2,1,0:T(8,128)(2,1)S(1)} %pad_maximum_fusion.2.refs_0_), channel_id=1, source_target_pairs={{0,2},{2,0},{4,6},{6,4},{1,3},{3,1},{5,7},{7,5},{8,10},{10,8},{12,... | collective-permute-start | bytes 1179656 | tf_op jit(solution)/shard_map/ppermute | solution.py:70
  118.3 9.7 %collective-permute-start.11 = (bf16[4,3,2,64,128]{4,3,2,1,0:T(8,128)(2,1)S(1)}, bf16[4,3,2,64,128]{4,3,2,1,0:T(8,128)(2,1)S(1)}, u32[]{:S(2)}, u32[]{:S(2)}) collective-permute-start(bf16[4,3,2,64,128]{4,3,2,1,0:T(8,128)(2,1)S(1)} %pad_maximum_fusion.2.refs_0_), channel_id=1, source_target_pairs={{0,4},{2,6},{4,0},{6,2},{1,5},{3,7},{5,1},{7,3},{8,12},{10,14},{12... | collective-permute-start | bytes 1179656 | tf_op jit(solution)/shard_map/ppermute | solution.py:70
  119.4 17.5 %collective-permute-start.12 = (bf16[4,3,2,64,128]{4,3,2,1,0:T(8,128)(2,1)S(1)}, bf16[4,3,2,64,128]{4,3,2,1,0:T(8,128)(2,1)S(1)}, u32[]{:S(2)}, u32[]{:S(2)}) collective-permute-start(bf16[4,3,2,64,128]{4,3,2,1,0:T(8,128)(2,1)S(1)} %pad_maximum_fusion.2.refs_0_), channel_id=1, source_target_pairs={{0,6},{2,4},{4,2},{6,0},{1,7},{3,5},{5,3},{7,1},{8,14},{10,12},{12... | collective-permute-start | bytes 1179656 | tf_op jit(solution)/shard_map/ppermute | solution.py:70
  152.3 11.8 %collective-permute-start.14 = (bf16[192,896]{1,0:T(8,128)(2,1)}, bf16[192,896]{1,0:T(8,128)(2,1)S(1)}, u32[]{:S(2)}, u32[]{:S(2)}) collective-permute-start(bf16[192,896]{1,0:T(8,128)(2,1)} %get-tuple-element.159.refs_0_), channel_id=1, source_target_pairs={{0,4},{2,6},{4,0},{6,2},{1,5},{3,7},{5,1},{7,3},{8,12},{10,14},{12... | collective-permute-start | bytes 1032200 | tf_op jit(solution)/shard_map/ppermute | solution.py:70
  152.6 17.8 %collective-permute-start.15 = (bf16[192,896]{1,0:T(8,128)(2,1)}, bf16[192,896]{1,0:T(8,128)(2,1)S(1)}, u32[]{:S(2)}, u32[]{:S(2)}) collective-permute-start(bf16[192,896]{1,0:T(8,128)(2,1)} %get-tuple-element.159.refs_0_), channel_id=1, source_target_pairs={{0,6},{2,4},{4,2},{6,0},{1,7},{3,5},{5,3},{7,1},{8,14},{10,12},{12... | collective-permute-start | bytes 1032200 | tf_op jit(solution)/shard_map/ppermute | solution.py:70
  154.1 16.4 %collective-permute-start.16 = (bf16[192,896]{1,0:T(8,128)(2,1)}, bf16[192,896]{1,0:T(8,128)(2,1)S(1)}, u32[]{:S(2)}, u32[]{:S(2)}) collective-permute-start(bf16[192,896]{1,0:T(8,128)(2,1)} %get-tuple-element.159.refs_0_), channel_id=1, source_target_pairs={{0,1},{1,0},{2,3},{3,2},{4,5},{5,4},{6,7},{7,6},{8,9},{9,8},{10,11... | collective-permute-start | bytes 1032200 | tf_op jit(solution)/shard_map/ppermute | solution.py:70
  159.8 10.7 %collective-permute-start.17 = (bf16[192,896]{1,0:T(8,128)(2,1)S(1)}, bf16[192,896]{1,0:T(8,128)(2,1)S(1)}, u32[]{:S(2)}, u32[]{:S(2)}) collective-permute-start(bf16[192,896]{1,0:T(8,128)(2,1)S(1)} %collective-permute-done.13.refs_1_), channel_id=1, source_target_pairs={{0,1},{1,0},{2,3},{3,2},{4,5},{5,4},{6,7},{7,6},{8,9},{9,8},{10,11... | collective-permute-start | bytes 1032200 | tf_op jit(solution)/shard_map/ppermute | solution.py:70
  210.4 56.8 %all-to-all-start.1 = ((bf16[4,2,1,224,608]{4,3,2,1,0:T(8,128)(2,1)}), bf16[4,2,1,224,608]{4,3,2,1,0:T(8,128)(2,1)S(1)}, u32[]{:S(2)}, u32[]{:S(2)}) async-start(bf16[4,2,1,224,608]{4,3,2,1,0:T(8,128)(2,1)} %get-tuple-element.182), calls=%async_computation.1 | async-start | bytes 4587520 | tf_op jit(solution)/shard_map/all_to_all | solution.py:60
  217.1 9.0 %collective-permute-start.21 = (bf16[192,896]{1,0:T(8,128)(2,1)S(1)}, bf16[192,896]{1,0:T(8,128)(2,1)S(1)}, u32[]{:S(2)}, u32[]{:S(2)}) collective-permute-start(bf16[192,896]{1,0:T(8,128)(2,1)S(1)} %copy-done.65), channel_id=1, source_target_pairs={{0,2},{2,0},{4,6},{6,4},{1,3},{3,1},{5,7},{7,5},{8,10},{10,8},{12,... | collective-permute-start | bytes 1032200 | tf_op jit(solution)/shard_map/ppermute | solution.py:70
  217.6 9.4 %collective-permute-start.22 = (bf16[192,896]{1,0:T(8,128)(2,1)S(1)}, bf16[192,896]{1,0:T(8,128)(2,1)S(1)}, u32[]{:S(2)}, u32[]{:S(2)}) collective-permute-start(bf16[192,896]{1,0:T(8,128)(2,1)S(1)} %copy-done.64), channel_id=1, source_target_pairs={{0,4},{2,6},{4,0},{6,2},{1,5},{3,7},{5,1},{7,3},{8,12},{10,14},{12... | collective-permute-start | bytes 1032200 | tf_op jit(solution)/shard_map/ppermute | solution.py:70
  217.9 15.0 %collective-permute-start.23 = (bf16[192,896]{1,0:T(8,128)(2,1)S(1)}, bf16[192,896]{1,0:T(8,128)(2,1)S(1)}, u32[]{:S(2)}, u32[]{:S(2)}) collective-permute-start(bf16[192,896]{1,0:T(8,128)(2,1)S(1)} %copy-done.63), channel_id=1, source_target_pairs={{0,6},{2,4},{4,2},{6,0},{1,7},{3,5},{5,3},{7,1},{8,14},{10,12},{12... | collective-permute-start | bytes 1032200 | tf_op jit(solution)/shard_map/ppermute | solution.py:70
  269.2 15.0 %collective-permute-start.27 = (bf16[4,3,2,64,128]{4,3,2,1,0:T(8,128)(2,1)}, bf16[4,3,2,64,128]{4,3,2,1,0:T(8,128)(2,1)S(1)}, u32[]{:S(2)}, u32[]{:S(2)}) collective-permute-start(bf16[4,3,2,64,128]{4,3,2,1,0:T(8,128)(2,1)} %get-tuple-element.197), channel_id=1, source_target_pairs={{0,6},{2,4},{4,2},{6,0},{1,7},{3,5},{5,3},{7,1},{8,14},{10,12},{12... | collective-permute-start | bytes 1179656 | tf_op jit(solution)/shard_map/ppermute | solution.py:70
  269.6 19.1 %collective-permute-start.26 = (bf16[4,3,2,64,128]{4,3,2,1,0:T(8,128)(2,1)}, bf16[4,3,2,64,128]{4,3,2,1,0:T(8,128)(2,1)S(1)}, u32[]{:S(2)}, u32[]{:S(2)}) collective-permute-start(bf16[4,3,2,64,128]{4,3,2,1,0:T(8,128)(2,1)} %get-tuple-element.196), channel_id=1, source_target_pairs={{0,4},{2,6},{4,0},{6,2},{1,5},{3,7},{5,1},{7,3},{8,12},{10,14},{12... | collective-permute-start | bytes 1179656 | tf_op jit(solution)/shard_map/ppermute | solution.py:70
  270.7 17.9 %collective-permute-start.25 = (bf16[4,3,2,64,128]{4,3,2,1,0:T(8,128)(2,1)S(1)}, bf16[4,3,2,64,128]{4,3,2,1,0:T(8,128)(2,1)S(1)}, u32[]{:S(2)}, u32[]{:S(2)}) collective-permute-start(bf16[4,3,2,64,128]{4,3,2,1,0:T(8,128)(2,1)S(1)} %copy-done.62), channel_id=1, source_target_pairs={{0,2},{2,0},{4,6},{6,4},{1,3},{3,1},{5,7},{7,5},{8,10},{10,8},{12,... | collective-permute-start | bytes 1179656 | tf_op jit(solution)/shard_map/ppermute | solution.py:70
  272.4 22.0 %all-to-all-start.2 = ((bf16[8,2,28,608]{3,1,2,0:T(2,128)(2,1)}), bf16[8,2,28,608]{3,1,2,0:T(2,128)(2,1)S(1)}, u32[]{:S(2)}, u32[]{:S(2)}) async-start(bf16[8,2,28,608]{3,1,2,0:T(2,128)(2,1)} %bitcast.12), calls=%async_computation.2 | async-start | bytes 1146880 | tf_op jit(solution)/shard_map/all_to_all | solution.py:60
  289.1 15.3 %collective-permute-start.30 = (bf16[1,3,2,64,128]{4,3,2,1,0:T(8,128)(2,1)S(1)}, bf16[1,3,2,64,128]{4,3,2,1,0:T(8,128)(2,1)S(1)}, u32[]{:S(2)}, u32[]{:S(2)}) collective-permute-start(bf16[1,3,2,64,128]{4,3,2,1,0:T(8,128)(2,1)S(1)} %get-tuple-element.303), channel_id=1, source_target_pairs={{0,24},{8,16},{16,8},{24,0},{1,25},{9,17},{17,9},{25,1},{2,26},{10... | collective-permute-start | bytes 294920 | tf_op jit(solution)/shard_map/ppermute | solution.py:70
  291.2 13.1 %collective-permute-start.29 = (bf16[1,3,2,64,128]{4,3,2,1,0:T(8,128)(2,1)S(1)}, bf16[1,3,2,64,128]{4,3,2,1,0:T(8,128)(2,1)S(1)}, u32[]{:S(2)}, u32[]{:S(2)}) collective-permute-start(bf16[1,3,2,64,128]{4,3,2,1,0:T(8,128)(2,1)S(1)} %get-tuple-element.304), channel_id=1, source_target_pairs={{0,16},{8,24},{16,0},{24,8},{1,17},{9,25},{17,1},{25,9},{2,18},{10... | collective-permute-start | bytes 294920 | tf_op jit(solution)/shard_map/ppermute | solution.py:70
  291.2 13.1 %collective-permute-start.28 = (bf16[1,3,2,64,128]{4,3,2,1,0:T(8,128)(2,1)S(1)}, bf16[1,3,2,64,128]{4,3,2,1,0:T(8,128)(2,1)S(1)}, u32[]{:S(2)}, u32[]{:S(2)}) collective-permute-start(bf16[1,3,2,64,128]{4,3,2,1,0:T(8,128)(2,1)S(1)} %get-tuple-element.302), channel_id=1, source_target_pairs={{0,8},{8,0},{16,24},{24,16},{1,9},{9,1},{17,25},{25,17},{2,10},{10... | collective-permute-start | bytes 294920 | tf_op jit(solution)/shard_map/ppermute | solution.py:70
  295.3 28.1 %all-to-all-start.3 = ((bf16[4,1,152,896]{3,2,1,0:T(8,128)(2,1)}), bf16[4,1,152,896]{3,2,1,0:T(8,128)(2,1)S(1)}, u32[]{:S(2)}, u32[]{:S(2)}) async-start(bf16[4,1,152,896]{3,2,1,0:T(8,128)(2,1)} %get-tuple-element.218), calls=%async_computation.3 | async-start | bytes 2179072 | tf_op jit(solution)/shard_map/all_to_all | solution.py:60
  308.5 45.1 %collective-permute-start.31 = (bf16[4,4,32,1792]{3,2,1,0:T(8,128)(2,1)}, bf16[4,4,32,1792]{3,2,1,0:T(8,128)(2,1)S(1)}, u32[]{:S(2)}, u32[]{:S(2)}) collective-permute-start(bf16[4,4,32,1792]{3,2,1,0:T(8,128)(2,1)} %get-tuple-element.213), channel_id=1, source_target_pairs={{0,1},{1,0},{2,3},{3,2},{4,5},{5,4},{6,7},{7,6},{8,9},{9,8},{10,11... | collective-permute-start | bytes 5505032 | tf_op jit(solution)/shard_map/ppermute | solution.py:70
  308.7 22.4 %collective-permute-start.24 = (bf16[768,896]{1,0:T(8,128)(2,1)}, bf16[768,896]{1,0:T(8,128)(2,1)}, u32[]{:S(2)}, u32[]{:S(2)}) collective-permute-start(bf16[768,896]{1,0:T(8,128)(2,1)} %get-tuple-element.188), channel_id=1, source_target_pairs={{0,1},{1,0},{2,3},{3,2},{4,5},{5,4},{6,7},{7,6},{8,9},{9,8},{10,11... | collective-permute-start | bytes 4128776 | tf_op jit(solution)/shard_map/ppermute | solution.py:70
  315.3 10.1 %collective-permute-start.36 = (bf16[56,2432]{1,0:T(8,128)(2,1)}, bf16[56,2432]{1,0:T(8,128)(2,1)}, u32[]{:S(2)}, u32[]{:S(2)}) collective-permute-start(bf16[56,2432]{1,0:T(8,128)(2,1)} %get-tuple-element.298), channel_id=1, source_target_pairs={{16,8},{24,0},{17,9},{25,1},{18,10},{26,2},{19,11},{27,3},{20,12},... | collective-permute-start | bytes 817160 | tf_op jit(solution)/shard_map/ppermute | solution.py:70
  317.7 11.9 %collective-permute-start.35 = (bf16[56,2432]{1,0:T(8,128)(2,1)}, bf16[56,2432]{1,0:T(8,128)(2,1)}, u32[]{:S(2)}, u32[]{:S(2)}) collective-permute-start(bf16[56,2432]{1,0:T(8,128)(2,1)} %get-tuple-element.297), channel_id=1, source_target_pairs={{16,0},{24,8},{17,1},{25,9},{18,2},{26,10},{19,3},{27,11},{20,4},{... | collective-permute-start | bytes 817160 | tf_op jit(solution)/shard_map/ppermute | solution.py:70
  319.7 10.7 %collective-permute-start.34 = (bf16[56,2432]{1,0:T(8,128)(2,1)S(1)}, bf16[56,2432]{1,0:T(8,128)(2,1)}, u32[]{:S(2)}, u32[]{:S(2)}) collective-permute-start(bf16[56,2432]{1,0:T(8,128)(2,1)S(1)} %get-tuple-element.296), channel_id=1, source_target_pairs={{0,8},{8,0},{1,9},{9,1},{2,10},{10,2},{3,11},{11,3},{4,12},{12,4},... | collective-permute-start | bytes 817160 | tf_op jit(solution)/shard_map/ppermute | solution.py:70
  325.4 28.2 %collective-permute-start.32 = (bf16[4,4,32,256]{3,2,1,0:T(8,128)(2,1)S(1)}, bf16[4,4,32,256]{3,2,1,0:T(8,128)(2,1)S(1)}, u32[]{:S(2)}, u32[]{:S(2)}) collective-permute-start(bf16[4,4,32,256]{3,2,1,0:T(8,128)(2,1)S(1)} %copy-done.66), channel_id=1, source_target_pairs={{0,1},{1,0},{2,3},{3,2},{4,5},{5,4},{6,7},{7,6},{8,9},{9,8},{10,11... | collective-permute-start | bytes 786440 | tf_op jit(solution)/shard_map/ppermute | solution.py:70
  329.5 29.8 %collective-permute-start.39 = (bf16[152,896]{1,0:T(8,128)(2,1)S(1)}, bf16[152,896]{1,0:T(8,128)(2,1)S(1)}, u32[]{:S(2)}, u32[]{:S(2)}) collective-permute-start(bf16[152,896]{1,0:T(8,128)(2,1)S(1)} %get-tuple-element.279), channel_id=1, source_target_pairs={{8,16},{9,17},{10,18},{11,19},{12,20},{13,21},{14,22},{15,23}} | collective-permute-start | bytes 817160 | tf_op jit(solution)/shard_map/ppermute | solution.py:70
  330.4 29.0 %collective-permute-start.38 = (bf16[152,896]{1,0:T(8,128)(2,1)S(1)}, bf16[152,896]{1,0:T(8,128)(2,1)S(1)}, u32[]{:S(2)}, u32[]{:S(2)}) collective-permute-start(bf16[152,896]{1,0:T(8,128)(2,1)S(1)} %get-tuple-element.279), channel_id=1, source_target_pairs={{0,16},{1,17},{2,18},{3,19},{4,20},{5,21},{6,22},{7,23}} | collective-permute-start | bytes 817160 | tf_op jit(solution)/shard_map/ppermute | solution.py:70
  331.1 28.3 %collective-permute-start.37 = (bf16[152,896]{1,0:T(8,128)(2,1)S(1)}, bf16[152,896]{1,0:T(8,128)(2,1)S(1)}, u32[]{:S(2)}, u32[]{:S(2)}) collective-permute-start(bf16[152,896]{1,0:T(8,128)(2,1)S(1)} %get-tuple-element.279), channel_id=1, source_target_pairs={{24,16},{25,17},{26,18},{27,19},{28,20},{29,21},{30,22},{31,23}} | collective-permute-start | bytes 817160 | tf_op jit(solution)/shard_map/ppermute | solution.py:70
  359.5 26.3 %collective-permute-start.43 = (bf16[224,2432]{1,0:T(8,128)(2,1)S(1)}, bf16[224,2432]{1,0:T(8,128)(2,1)S(1)}, u32[]{:S(2)}, u32[]{:S(2)}) collective-permute-start(bf16[224,2432]{1,0:T(8,128)(2,1)S(1)} %pad_maximum_fusion.refs_0_), channel_id=1, source_target_pairs={{0,2},{2,0},{4,6},{6,4},{8,10},{10,8},{12,14},{14,12},{1,3},{3,1},... | collective-permute-start | bytes 3268616 | tf_op jit(solution)/shard_map/ppermute | solution.py:76
  360.4 12.3 %collective-permute-start.40 = (bf16[4,32,2048]{2,1,0:T(8,128)(2,1)S(1)}, bf16[4,32,2048]{2,1,0:T(8,128)(2,1)S(1)}, u32[]{:S(2)}, u32[]{:S(2)}) collective-permute-start(bf16[4,32,2048]{2,1,0:T(8,128)(2,1)S(1)} %copy-done.61), channel_id=1, source_target_pairs={{0,2},{2,0},{4,6},{6,4},{1,3},{3,1},{5,7},{7,5},{8,10},{10,8},{12,... | collective-permute-start | bytes 1572872 | tf_op jit(solution)/shard_map/ppermute | solution.py:70
  362.2 12.2 %collective-permute-start.41 = (bf16[4,32,2048]{2,1,0:T(8,128)(2,1)S(1)}, bf16[4,32,2048]{2,1,0:T(8,128)(2,1)S(1)}, u32[]{:S(2)}, u32[]{:S(2)}) collective-permute-start(bf16[4,32,2048]{2,1,0:T(8,128)(2,1)S(1)} %copy-done.60), channel_id=1, source_target_pairs={{0,4},{2,6},{4,0},{6,2},{1,5},{3,7},{5,1},{7,3},{8,12},{10,14},{12... | collective-permute-start | bytes 1572872 | tf_op jit(solution)/shard_map/ppermute | solution.py:70
  362.7 21.5 %collective-permute-start.42 = (bf16[4,32,2048]{2,1,0:T(8,128)(2,1)S(1)}, bf16[4,32,2048]{2,1,0:T(8,128)(2,1)S(1)}, u32[]{:S(2)}, u32[]{:S(2)}) collective-permute-start(bf16[4,32,2048]{2,1,0:T(8,128)(2,1)S(1)} %copy-done.59), channel_id=1, source_target_pairs={{0,6},{2,4},{4,2},{6,0},{1,7},{3,5},{5,3},{7,1},{8,14},{10,12},{12... | collective-permute-start | bytes 1572872 | tf_op jit(solution)/shard_map/ppermute | solution.py:70
  363.9 23.7 %collective-permute-start.44 = (bf16[224,2432]{1,0:T(8,128)(2,1)S(1)}, bf16[224,2432]{1,0:T(8,128)(2,1)}, u32[]{:S(2)}, u32[]{:S(2)}) collective-permute-start(bf16[224,2432]{1,0:T(8,128)(2,1)S(1)} %pad_maximum_fusion.refs_0_), channel_id=1, source_target_pairs={{0,4},{2,6},{4,0},{6,2},{8,12},{10,14},{12,8},{14,10},{1,5},{3,7},... | collective-permute-start | bytes 3268616 | tf_op jit(solution)/shard_map/ppermute | solution.py:76
  372.7 14.9 %collective-permute-start.45 = (bf16[224,2432]{1,0:T(8,128)(2,1)S(1)}, bf16[224,2432]{1,0:T(8,128)(2,1)}, u32[]{:S(2)}, u32[]{:S(2)}) collective-permute-start(bf16[224,2432]{1,0:T(8,128)(2,1)S(1)} %pad_maximum_fusion.refs_0_), channel_id=1, source_target_pairs={{0,6},{2,4},{4,2},{6,0},{8,14},{10,12},{12,10},{14,8},{1,7},{3,5},... | collective-permute-start | bytes 3268616 | tf_op jit(solution)/shard_map/ppermute | solution.py:76
  374.4 13.2 %collective-permute-start.46 = (bf16[608,896]{1,0:T(8,128)(2,1)S(1)}, bf16[608,896]{1,0:T(8,128)(2,1)}, u32[]{:S(2)}, u32[]{:S(2)}) collective-permute-start(bf16[608,896]{1,0:T(8,128)(2,1)S(1)} %pad_maximum_fusion.1.refs_4_), channel_id=1, source_target_pairs={{16,18},{18,16},{20,22},{22,20},{17,19},{19,17},{21,23},{23,21}} | collective-permute-start | bytes 3268616 | tf_op jit(solution)/shard_map/ppermute | solution.py:76
  389.3 128.5 %collective-permute-start.62 = (f32[896,896]{1,0:T(8,128)}, f32[896,896]{1,0:T(8,128)S(1)}, u32[]{:S(2)}, u32[]{:S(2)}) collective-permute-start(f32[896,896]{1,0:T(8,128)} %shard_map.382.a_ref), channel_id=1, source_target_pairs={{0,1},{1,0},{8,9},{9,8},{16,17},{17,16},{2,3},{3,2},{10,11},{11,10... | collective-permute-start | bytes 9633800 | tf_op jit(solution)/shard_map/ppermute | solution.py:1113
  453.3 11.3 %collective-permute-start.50 = (bf16[1,32,2048]{2,1,0:T(8,128)(2,1)}, bf16[1,32,2048]{2,1,0:T(8,128)(2,1)S(1)}, u32[]{:S(2)}, u32[]{:S(2)}) collective-permute-start(bf16[1,32,2048]{2,1,0:T(8,128)(2,1)} %get-tuple-element.245), channel_id=1, source_target_pairs={{0,16},{8,24},{16,0},{24,8},{1,17},{9,25},{17,1},{25,9},{2,18},{10... | collective-permute-start | bytes 393224 | tf_op jit(solution)/shard_map/ppermute | solution.py:70
  453.3 11.2 %collective-permute-start.51 = (bf16[1,32,2048]{2,1,0:T(8,128)(2,1)}, bf16[1,32,2048]{2,1,0:T(8,128)(2,1)S(1)}, u32[]{:S(2)}, u32[]{:S(2)}) collective-permute-start(bf16[1,32,2048]{2,1,0:T(8,128)(2,1)} %get-tuple-element.246), channel_id=1, source_target_pairs={{0,24},{8,16},{16,8},{24,0},{1,25},{9,17},{17,9},{25,1},{2,26},{10... | collective-permute-start | bytes 393224 | tf_op jit(solution)/shard_map/ppermute | solution.py:70
  485.7 11.8 %collective-permute-start.56 = (bf16[224,1024]{1,0:T(8,128)(2,1)}, bf16[224,1024]{1,0:T(8,128)(2,1)S(1)}, u32[]{:S(2)}, u32[]{:S(2)}) collective-permute-start(bf16[224,1024]{1,0:T(8,128)(2,1)} %shard_map.384.refs_0_.refs_5_), channel_id=1, source_target_pairs={{24,26},{26,24},{28,30},{30,28},{25,27},{27,25},{29,31},{31,29}} | collective-permute-start | bytes 1376264 | tf_op jit(solution)/shard_map/ppermute | solution.py:76
  488.7 13.4 %collective-permute-start.57 = (bf16[224,1024]{1,0:T(8,128)(2,1)}, bf16[224,1024]{1,0:T(8,128)(2,1)S(1)}, u32[]{:S(2)}, u32[]{:S(2)}) collective-permute-start(bf16[224,1024]{1,0:T(8,128)(2,1)} %shard_map.384.refs_0_.refs_5_), channel_id=1, source_target_pairs={{24,28},{26,30},{28,24},{30,26},{25,29},{27,31},{29,25},{31,27}} | collective-permute-start | bytes 1376264 | tf_op jit(solution)/shard_map/ppermute | solution.py:76
  491.9 16.4 %collective-permute-start.58 = (bf16[224,1024]{1,0:T(8,128)(2,1)}, bf16[224,1024]{1,0:T(8,128)(2,1)S(1)}, u32[]{:S(2)}, u32[]{:S(2)}) collective-permute-start(bf16[224,1024]{1,0:T(8,128)(2,1)} %shard_map.384.refs_0_.refs_5_), channel_id=1, source_target_pairs={{24,30},{26,28},{28,26},{30,24},{25,31},{27,29},{29,27},{31,25}} | collective-permute-start | bytes 1376264 | tf_op jit(solution)/shard_map/ppermute | solution.py:76
  513.9 73.8 %collective-permute-start.59 = (bf16[192,896]{1,0:T(8,128)(2,1)}, bf16[192,896]{1,0:T(8,128)(2,1)S(1)}, u32[]{:S(2)}, u32[]{:S(2)}) collective-permute-start(bf16[192,896]{1,0:T(8,128)(2,1)} %get-tuple-element.250), channel_id=1, source_target_pairs={{0,2},{2,0},{4,6},{6,4},{1,3},{3,1},{5,7},{7,5},{8,10},{10,8},{12,... | collective-permute-start | bytes 1032200 | tf_op jit(solution)/shard_map/ppermute | solution.py:70
  515.2 72.6 %collective-permute-start.60 = (bf16[192,896]{1,0:T(8,128)(2,1)}, bf16[192,896]{1,0:T(8,128)(2,1)}, u32[]{:S(2)}, u32[]{:S(2)}) collective-permute-start(bf16[192,896]{1,0:T(8,128)(2,1)} %get-tuple-element.251), channel_id=1, source_target_pairs={{0,4},{2,6},{4,0},{6,2},{1,5},{3,7},{5,1},{7,3},{8,12},{10,14},{12... | collective-permute-start | bytes 1032200 | tf_op jit(solution)/shard_map/ppermute | solution.py:70
  515.5 72.3 %collective-permute-start.61 = (bf16[192,896]{1,0:T(8,128)(2,1)}, bf16[192,896]{1,0:T(8,128)(2,1)}, u32[]{:S(2)}, u32[]{:S(2)}) collective-permute-start(bf16[192,896]{1,0:T(8,128)(2,1)} %get-tuple-element.252), channel_id=1, source_target_pairs={{0,6},{2,4},{4,2},{6,0},{1,7},{3,5},{5,3},{7,1},{8,14},{10,12},{12... | collective-permute-start | bytes 1032200 | tf_op jit(solution)/shard_map/ppermute | solution.py:70
  594.0 16.4 %collective-permute-start.67 = (bf16[56,2432]{1,0:T(8,128)(2,1)S(1)}, bf16[56,2432]{1,0:T(8,128)(2,1)S(1)}, u32[]{:S(2)}, u32[]{:S(2)}) collective-permute-start(bf16[56,2432]{1,0:T(8,128)(2,1)S(1)} %get-tuple-element.288), channel_id=1, source_target_pairs={{0,24},{8,16},{1,25},{9,17},{2,26},{10,18},{3,27},{11,19},{4,28},{... | collective-permute-start | bytes 817160 | tf_op jit(solution)/shard_map/ppermute | solution.py:70
  595.5 20.7 %collective-permute-start.68 = (bf16[56,2432]{1,0:T(8,128)(2,1)S(1)}, bf16[56,2432]{1,0:T(8,128)(2,1)S(1)}, u32[]{:S(2)}, u32[]{:S(2)}) collective-permute-start(bf16[56,2432]{1,0:T(8,128)(2,1)S(1)} %get-tuple-element.287), channel_id=1, source_target_pairs={{0,16},{8,24},{1,17},{9,25},{2,18},{10,26},{3,19},{11,27},{4,20},{... | collective-permute-start | bytes 817160 | tf_op jit(solution)/shard_map/ppermute | solution.py:70
  596.9 19.3 %collective-permute-start.69 = (bf16[56,2432]{1,0:T(8,128)(2,1)S(1)}, bf16[56,2432]{1,0:T(8,128)(2,1)S(1)}, u32[]{:S(2)}, u32[]{:S(2)}) collective-permute-start(bf16[56,2432]{1,0:T(8,128)(2,1)S(1)} %get-tuple-element.286), channel_id=1, source_target_pairs={{0,8},{8,0},{1,9},{9,1},{2,10},{10,2},{3,11},{11,3},{4,12},{12,4},... | collective-permute-start | bytes 817160 | tf_op jit(solution)/shard_map/ppermute | solution.py:70
  597.6 22.2 %collective-permute-start.71 = (bf16[152,896]{1,0:T(8,128)(2,1)S(1)}, bf16[152,896]{1,0:T(8,128)(2,1)S(1)}, u32[]{:S(2)}, u32[]{:S(2)}) collective-permute-start(bf16[152,896]{1,0:T(8,128)(2,1)S(1)} %get-tuple-element.285), channel_id=1, source_target_pairs={{16,8},{17,9},{18,10},{19,11},{20,12},{21,13},{22,14},{23,15}} | collective-permute-start | bytes 817160 | tf_op jit(solution)/shard_map/ppermute | solution.py:70
  599.2 9.2 %collective-permute-start.66 = (bf16[28,1024]{1,0:T(8,128)(2,1)S(1)}, bf16[28,1024]{1,0:T(8,128)(2,1)S(1)}, u32[]{:S(2)}, u32[]{:S(2)}) collective-permute-start(bf16[28,1024]{1,0:T(8,128)(2,1)S(1)} %constant_dynamic-slice_fusion), channel_id=1, source_target_pairs={{0,1},{1,0},{2,3},{3,2},{4,5},{5,4},{6,7},{7,6},{8,9},{9,8},{10,11... | collective-permute-start | bytes 172040 | tf_op jit(solution)/shard_map/ppermute | solution.py:70
  608.4 11.4 %collective-permute-start.72 = (bf16[152,896]{1,0:T(8,128)(2,1)S(1)}, bf16[152,896]{1,0:T(8,128)(2,1)S(1)}, u32[]{:S(2)}, u32[]{:S(2)}) collective-permute-start(bf16[152,896]{1,0:T(8,128)(2,1)S(1)} %get-tuple-element.284), channel_id=1, source_target_pairs={{16,0},{17,1},{18,2},{19,3},{20,4},{21,5},{22,6},{23,7}} | collective-permute-start | bytes 817160 | tf_op jit(solution)/shard_map/ppermute | solution.py:70
  610.5 16.7 %collective-permute-start.73 = (bf16[152,896]{1,0:T(8,128)(2,1)S(1)}, bf16[152,896]{1,0:T(8,128)(2,1)S(1)}, u32[]{:S(2)}, u32[]{:S(2)}) collective-permute-start(bf16[152,896]{1,0:T(8,128)(2,1)S(1)} %get-tuple-element.283), channel_id=1, source_target_pairs={{16,24},{17,25},{18,26},{19,27},{20,28},{21,29},{22,30},{23,31}} | collective-permute-start | bytes 817160 | tf_op jit(solution)/shard_map/ppermute | solution.py:70
  617.3 10.8 %collective-permute-start.70 = (bf16[2,28,2432]{2,1,0:T(8,128)(2,1)S(1)}, bf16[2,28,2432]{2,1,0:T(8,128)(2,1)S(1)}, u32[]{:S(2)}, u32[]{:S(2)}) collective-permute-start(bf16[2,28,2432]{2,1,0:T(8,128)(2,1)S(1)} %fusion), channel_id=1, source_target_pairs={{0,1},{1,0},{2,3},{3,2},{4,5},{5,4},{6,7},{7,6},{8,9},{9,8},{10,11... | collective-permute-start | bytes 817160 | tf_op jit(solution)/shard_map/ppermute | solution.py:70
  (84 other events, 847.1 us)
Sparse Core Ops, SparseCore 0:
  12.2 67.4 all-gather.3
  81.3 34.8 all-gather.7
  118.3 48.3 all-gather.5
